TPU v7x, 32 devices: a whole 2x2x4 slice. The times are simulated.
32 devices in a mesh: rep: 1, seq: 8 (over z, y), head: 2 (over x), sub: 2 (over core).
Axes of the slice: x: 2, y: 2, z: 4, core: 2. Of those that a mesh axis runs over, the one named last changes fastest.
Arguments:
- head_query_rows: bfloat16 [2048, 2048], P(('rep', 'seq', 'sub'), 'head'), may hold values from -6 to 6, as said below
- head_key_rows: bfloat16 [2048, 2048], P(('rep', 'seq', 'sub'), 'head'), may hold values from -6 to 6, as said below
- head_value_rows: bfloat16 [2048, 2048], P(('rep', 'seq', 'sub'), 'head'), may hold values from -6 to 6
- output_gradient: bfloat16 [2048, 4096], P(('rep', 'seq', 'sub'), 'head'), may hold values from -6 to 6
- output_matrix: bfloat16 [2048, 4096], P('head', 'sub'), may hold values from -0.125 to 0.125
- adapter_down_weight: bfloat16 [2048, 16], P('head'), may hold values from -0.125 to 0.125
- adapter_up_weight: bfloat16 [16, 4096], replicated, may hold values from -0.09375 to 0.09375
Outputs:
- query_gradient: bfloat16 [2048, 2048], P(('rep', 'seq', 'sub'), 'head')
- key_gradient: bfloat16 [2048, 2048], P(('rep', 'seq', 'sub'), 'head')
- value_gradient: bfloat16 [2048, 2048], P(('rep', 'seq', 'sub'), 'head')
- adapter_down_gradient: float32 [2048, 16], P(('rep', 'head'))
- adapter_up_gradient: float32 [16, 4096], P('rep', 'head')
Inputs may be any that keep to these rules, and one draw needn't show every extreme that they name: `head_query_rows`: entries of the queries are real values within the range. `head_key_rows`: entries of the keys are real values within the range.
All inputs are finite; a program needn't handle non-finite values.
Results may differ from a plain program's by a relative error of at most 0.029.
Values may be sent and summed in bfloat16 or wider, within the bound.
No kernel may reach another device: no remote copies, remote signals or barrier semaphores. Data moves between devices by JAX's collectives and lax.ppermute only.
A program may use at most 64 MiB of HBM per device.

v0:
```python
import functools
import math

import jax
import jax.numpy as jnp
from jax import lax
from jax.experimental import pallas as pl
from jax.experimental.pallas import tpu as pltpu
from jax.sharding import PartitionSpec as P

HD = 128
GROUP = 2048
TILE = 256
HIDDEN = -1e30
SCALE = HD ** (-0.5)
LOG2_SCALE = SCALE * math.log2(math.e)


def dot_nt(left, right):
    return lax.dot_general(
        left, right, (((1,), (1,)), ((), ())), preferred_element_type=jnp.float32
    )


def dot_nn(left, right):
    return jnp.dot(left, right, preferred_element_type=jnp.float32)


def rows_of(ref, blocks, first, count):
    return ref[0:blocks, first : first + count, :].reshape(blocks * count, HD)


def scores_of(keys, queries, visible):
    scores = dot_nt(keys, queries)
    head = scores.shape[0] - TILE
    tail = jnp.where(visible, scores[head:], HIDDEN)
    return tail if head == 0 else jnp.concatenate((scores[:head], tail), axis=0)


def tile_index(dimension):
    shape = (TILE, 1) if dimension == 0 else (1, TILE)
    return lax.broadcasted_iota(jnp.int32, shape, dimension)


def own_visible():
    return tile_index(0) <= tile_index(1)


def other_visible(sub, tok):
    return tile_index(0) // tok < tile_index(1) // tok + sub


def summed(terms):
    return functools.reduce(jnp.add, terms)


def forward_own_kernel(tok, scalar_ref, own_ref, total_ref, stat_ref):
    blocks = own_ref.shape[0]
    step = TILE // tok
    values_t = rows_of(own_ref, blocks, 2 * tok, tok).T
    for tile in range(blocks // step):
        upto = (tile + 1) * step
        at = tile * TILE
        queries = own_ref[tile * step : upto, 0:tok, :].reshape(TILE, HD)
        scores = scores_of(rows_of(own_ref, upto, tok, tok), queries, own_visible())
        highest = jnp.max(scores, axis=0, keepdims=True)
        powers = jnp.exp2((scores - highest) * LOG2_SCALE)
        total_ref[:, at : at + TILE] = dot_nn(
            values_t[:, : upto * tok], powers.astype(jnp.bfloat16)
        )
        stat_ref[0:1, at : at + TILE] = highest
        stat_ref[1:2, at : at + TILE] = jnp.sum(powers, axis=0, keepdims=True)


def forward_kernel(
    tok,
    scalar_ref,
    own_ref,
    other_ref,
    total_ref,
    own_stat_ref,
    down_t_ref,
    attn_ref,
    mid_ref,
    stat_ref,
):
    blocks = own_ref.shape[0]
    step = TILE // tok
    sub = scalar_ref[0]
    values_t = rows_of(other_ref, blocks, tok, tok).T
    for tile in range(blocks // step):
        upto = (tile + 1) * step
        at = tile * TILE
        here = pl.ds(at, TILE)
        queries = own_ref[tile * step : upto, 0:tok, :].reshape(TILE, HD)
        scores = scores_of(
            rows_of(other_ref, upto, 0, tok), queries, other_visible(sub, tok)
        )
        own_highest = own_stat_ref[0:1, here]
        highest = jnp.maximum(own_highest, jnp.max(scores, axis=0, keepdims=True))
        powers = jnp.exp2((scores - highest) * LOG2_SCALE)
        share = jnp.exp2((own_highest - highest) * LOG2_SCALE)
        inverse = 1.0 / (
            own_stat_ref[1:2, here] * share + jnp.sum(powers, axis=0, keepdims=True)
        )
        attn = dot_nn(values_t[:, : upto * tok], powers.astype(jnp.bfloat16))
        attn = ((attn + total_ref[:, here] * share) * inverse).astype(jnp.bfloat16)
        attn_ref[:, here] = attn
        mid_ref[:, here] = dot_nn(down_t_ref[...], attn)
        stat_ref[0:1, here] = highest
        stat_ref[1:2, here] = inverse


def backward_kernel(
    tok,
    scalar_ref,
    own_ref,
    other_ref,
    dout_ref,
    attn_ref,
    stat_ref,
    dq_ref,
    dk_own_ref,
    dv_own_ref,
    pair_other_ref,
    down_grad_ref,
    dk_own,
    dv_own,
    dk_other,
    dv_other,
):
    blocks = own_ref.shape[0]
    step = TILE // tok
    sub = scalar_ref[0]
    low_rank = down_grad_ref.shape[0]
    keys_own_t = rows_of(own_ref, blocks, tok, tok).T
    keys_other_t = rows_of(other_ref, blocks, 0, tok).T
    tiles = blocks // step
    down_total = jnp.zeros((low_rank, HD), jnp.float32)
    for tile in reversed(range(tiles)):
        upto = (tile + 1) * step
        width = upto * tok
        at = tile * TILE
        queries = own_ref[tile * step : upto, 0:tok, :].reshape(TILE, HD)
        douts_t = jnp.concatenate(
            [dout_ref[block, 0:HD, :] for block in range(tile * step, upto)], axis=1
        )
        highest = stat_ref[0:1, at : at + TILE]
        inverse = stat_ref[1:2, at : at + TILE]
        own = scores_of(rows_of(own_ref, upto, tok, tok), queries, own_visible())
        other = scores_of(
            rows_of(other_ref, upto, 0, tok), queries, other_visible(sub, tok)
        )
        own = jnp.exp2((own - highest) * LOG2_SCALE) * inverse
        other = jnp.exp2((other - highest) * LOG2_SCALE) * inverse
        dprob_own = dot_nn(rows_of(own_ref, upto, 2 * tok, tok), douts_t)
        dprob_other = dot_nn(rows_of(other_ref, upto, tok, tok), douts_t)
        delta = jnp.sum(own * dprob_own, axis=0, keepdims=True) + jnp.sum(
            other * dprob_other, axis=0, keepdims=True
        )
        ds_own = (own * (dprob_own - delta)).astype(jnp.bfloat16)
        ds_other = (other * (dprob_other - delta)).astype(jnp.bfloat16)
        dq = dot_nn(keys_own_t[:, :width], ds_own) + dot_nn(keys_other_t[:, :width], ds_other)
        dq = (dq * SCALE).T.astype(jnp.bfloat16)
        dq_ref[tile * step : upto] = dq.reshape(step, tok, HD)
        terms = (
            (dk_own, dot_nn(ds_own, queries)),
            (dk_other, dot_nn(ds_other, queries)),
            (dv_own, dot_nt(own.astype(jnp.bfloat16), douts_t)),
            (dv_other, dot_nt(other.astype(jnp.bfloat16), douts_t)),
        )
        for total, term in terms:
            if tile == tiles - 1:
                total[...] = term
            else:
                total[0:width] += term
        for i in range(step):
            lora = dout_ref[tile * step + i, HD : HD + low_rank, :]
            attn = attn_ref[:, at + i * tok : at + (i + 1) * tok]
            down_total += dot_nt(lora, attn)
    shape = (blocks, tok, HD)
    dk_own_ref[...] = (dk_own[...] * SCALE).reshape(shape)
    dv_own_ref[...] = dv_own[...].reshape(shape)
    pair_other_ref[:, 0:tok, :] = (dk_other[...] * SCALE).astype(jnp.bfloat16).reshape(shape)
    pair_other_ref[:, tok : 2 * tok, :] = dv_other[...].astype(jnp.bfloat16).reshape(shape)
    down_grad_ref[...] = 2.0 * down_total


def call_kernel(body, outs, scratch, flops, exps, *operands, declared=None, limit=48):
    in_bytes = sum(x.size * x.dtype.itemsize for x in operands)
    out_bytes = sum(x.size * x.dtype.itemsize for x in outs)
    specs = [pl.BlockSpec(memory_space=pltpu.SMEM)]
    specs += [pl.BlockSpec(memory_space=pltpu.VMEM)] * (len(operands) - 1)
    return pl.pallas_call(
        body,
        out_shape=outs,
        in_specs=specs,
        out_specs=[pl.BlockSpec(memory_space=pltpu.VMEM)] * len(outs),
        scratch_shapes=scratch,
        compiler_params=pltpu.CompilerParams(vmem_limit_bytes=limit * 1024 * 1024),
        cost_estimate=pl.CostEstimate(
            flops=flops,
            bytes_accessed=declared or in_bytes + out_bytes,
            transcendentals=exps,
        ),
    )(*operands)


def shape_of(shape, dtype):
    return jax.ShapeDtypeStruct(shape, dtype)


def butterfly_sum(value, axis, bits, count):
    for bit in bits:
        pairs = [(i, i ^ bit) for i in range(count)]
        value = value.astype(jnp.bfloat16)
        taken = lax.ppermute(value, axis, pairs)
        value = value.astype(jnp.float32) + taken.astype(jnp.float32)
    return value


def powers_below(count):
    return [1 << n for n in range(count.bit_length() - 1)]


def message_kernel(copies, *refs):
    count = (len(refs) - 3) // 2
    operands, message_ref = refs[:count], refs[count]
    held, in_sems, out_sems = refs[count + 1 : -2], refs[-2], refs[-1]
    tok = operands[0].shape[0]
    arriving = [
        pltpu.make_async_copy(ref, to, in_sems.at[n])
        for n, (ref, to) in enumerate(zip(operands, held))
    ]
    for copy in arriving:
        copy.start()
    leaving = []
    for n, (copy, ref) in enumerate(zip(arriving, held)):
        copy.wait()
        for rank in range(message_ref.shape[0]):
            cols = pl.ds((rank // copies) * HD, HD)
            to = message_ref.at[rank, pl.ds(n * tok, tok), :]
            leaving.append(pltpu.make_async_copy(ref.at[:, cols], to, out_sems.at[len(leaving)]))
            leaving[-1].start()
    for copy in leaving:
        copy.wait()


def message_of(copies, ranks, *operands):
    tok = operands[0].shape[0]
    count = len(operands)
    shape = (ranks, count * tok, HD)
    return pl.pallas_call(
        functools.partial(message_kernel, copies),
        out_shape=shape_of(shape, operands[0].dtype),
        in_specs=[pl.BlockSpec(memory_space=pltpu.HBM)] * count,
        out_specs=pl.BlockSpec(memory_space=pltpu.HBM),
        scratch_shapes=[pltpu.VMEM(x.shape, x.dtype) for x in operands]
        + [pltpu.SemaphoreType.DMA((count,)), pltpu.SemaphoreType.DMA((ranks * count,))],
        cost_estimate=pl.CostEstimate(
            flops=0, bytes_accessed=4 * math.prod(shape), transcendentals=0
        ),
    )(*operands)


def unpack_kernel(copies, back_ref, *refs):
    out_refs, down_ref = refs[:3], refs[3] if len(refs) > 3 else None
    tok = out_refs[0].shape[0]
    for at_head in range(out_refs[0].shape[1] // HD):
        cols = slice(at_head * HD, (at_head + 1) * HD)
        for n, ref in enumerate(out_refs):
            ref[:, cols] = back_ref[at_head * copies, n * tok : (n + 1) * tok, :]
        if down_ref is not None:
            down_ref[:, cols] = back_ref[at_head * copies, 3 * tok :, :].astype(jnp.float32)


def in_vmem(body, outs, *operands):
    whole = pl.BlockSpec(memory_space=pltpu.VMEM)
    size = sum(x.size * x.dtype.itemsize for x in operands)
    size += sum(x.size * x.dtype.itemsize for x in outs)
    return pl.pallas_call(
        body,
        out_shape=outs,
        in_specs=[whole] * len(operands),
        out_specs=[whole] * len(outs),
        compiler_params=pltpu.CompilerParams(vmem_limit_bytes=16 * 1024 * 1024),
        cost_estimate=pl.CostEstimate(flops=0, bytes_accessed=size, transcendentals=0),
    )(*operands)


def cotangent_kernel(chunks, plan_ref, *refs):
    pieces, (matrix_ref, up_ref, own_ref, sent_ref) = refs[:-4], refs[-4:]
    tok, cols = pieces[0].shape
    feats, low_rank = matrix_ref.shape[0], up_ref.shape[0]
    count = len(pieces)
    if chunks == 1:
        stacks = [(jnp.concatenate([p[...] for p in pieces], axis=0), pl.ds(0, cols))]
    else:
        stacks = [
            (p[...], pl.ds(pl.multiple_of(plan_ref[count + k], HD), cols))
            for k, p in enumerate(pieces)
        ]
    mine = [plan_ref[k] == 1 for k in range(count)]
    for ref, here in ((matrix_ref, pl.ds(0, feats)), (up_ref, pl.ds(feats, low_rank))):
        terms = [dot_nt(ref[:, at], rows) for rows, at in stacks]
        parts = [t[:, i : i + tok] for t in terms for i in range(0, t.shape[1], tok)]
        own_ref[here, :] = summed([jnp.where(m, p, 0.0) for m, p in zip(mine, parts)])
        sent = summed([jnp.where(m, 0.0, p) for m, p in zip(mine, parts)])
        sent_ref[here, :] = sent.astype(jnp.bfloat16)


def dout_kernel(copies, own_ref, taken_ref, mid_ref, message_ref):
    low_rank = mid_ref.shape[1]
    feats = own_ref.shape[0] - low_rank
    lora = own_ref[feats:, :] + taken_ref[feats:, :].astype(jnp.float32)
    for rank in range(message_ref.shape[0]):
        at = pl.ds((rank // copies) * HD, HD)
        part = own_ref[at, :] + taken_ref[at, :].astype(jnp.float32)
        message_ref[rank, 0:HD, :] = part.astype(jnp.bfloat16)
        message_ref[rank, HD : HD + low_rank, :] = lora.astype(jnp.bfloat16)
        message_ref[rank, HD + low_rank : HD + 2 * low_rank, :] = mid_ref[rank]


def on_device(
    sizes,
    head_query_rows,
    head_key_rows,
    head_value_rows,
    output_gradient,
    output_matrix,
    adapter_down_weight,
    adapter_up_weight,
):
    seqs, heads, subs = sizes
    tok, feats = head_query_rows.shape
    cols = output_gradient.shape[1]
    low_rank = adapter_up_weight.shape[0]
    local_heads = feats // HD
    block_rows = tok * subs
    ranks = GROUP // block_rows
    copies = ranks // local_heads
    shift_blocks = GROUP // 2 // block_rows

    seq = lax.axis_index("seq")
    head = lax.axis_index("head")
    sub = lax.axis_index("sub")
    shifted = head >= heads // 2
    rank = (seq + shift_blocks) % ranks
    my_head = rank // copies

    groups = []
    for at_head in range(heads):
        for first in range(0, seqs, ranks):
            members = [first + shift_blocks + i for i in range(ranks)]
            if at_head < heads // 2:
                members = [first + (m - first) % ranks for m in members]
            members = [m % seqs for m in members]
            groups.append([m * heads + at_head for m in members])
    scalars = jnp.full((1,), sub, jnp.int32)

    def in_order(blocks):
        half = ranks // 2
        turned = jnp.concatenate((blocks[half:], blocks[:half]), axis=0)
        return jnp.where(shifted, blocks, turned)


    def exchange(parts):
        return lax.all_to_all(
            parts, ("seq", "head"), 0, 0, axis_index_groups=groups, tiled=True
        )

    def swap(value):
        if subs == 1:
            return value
        return lax.ppermute(value, "sub", [(0, 1), (1, 0)])

    sent = message_of(copies, ranks, head_query_rows, head_key_rows, head_value_rows)
    sent, output_gradient, output_matrix = lax.optimization_barrier(
        (sent, output_gradient, output_matrix)
    )
    own = exchange(sent)

    chunks = heads // subs
    pieces = []
    for k in range(heads):
        pairs = []
        for src_head in range(heads):
            for src_sub in range(subs):
                j = (src_head % chunks) * subs + src_sub
                dst = ((j + k) % heads) * subs + src_head // chunks
                pairs.append((src_head * subs + src_sub, dst))
        pieces.append(lax.ppermute(output_gradient, ("head", "sub"), pairs))

    up_half = lax.dynamic_slice_in_dim(adapter_up_weight, sub * chunks * cols, chunks * cols, 1)
    folded = dot_nn(adapter_down_weight, up_half)
    folded = (output_matrix.astype(jnp.float32) + 2.0 * folded).astype(jnp.bfloat16)
    sources = [(head - k + heads) % heads for k in range(heads)]
    plan = [(j % subs == sub).astype(jnp.int32) for j in sources]
    plan += [(j // subs * cols).astype(jnp.int32) for j in sources]
    packed_own, packed_sent = call_kernel(
        functools.partial(cotangent_kernel, chunks),
        [
            shape_of((feats + low_rank, tok), jnp.float32),
            shape_of((feats + low_rank, tok), jnp.bfloat16),
        ],
        [],
        0,
        0,
        jnp.stack(plan),
        *pieces,
        folded,
        up_half,
        declared=1024,
        limit=16,
    )
    received = swap(packed_sent)
    down_head = lax.dynamic_slice_in_dim(adapter_down_weight, my_head * HD, HD, 0).T
    own, down_head, _ = lax.optimization_barrier((own, down_head, packed_sent))
    own = in_order(own)
    other = swap(own[:, tok:])

    rows = ranks * tok
    pair_count = rows * (rows + TILE)
    own_total, own_stats = call_kernel(
        functools.partial(forward_own_kernel, tok),
        [shape_of((HD, rows), jnp.float32), shape_of((8, rows), jnp.float32)],
        [],
        2 * pair_count * HD,
        pair_count // 2,
        scalars,
        own,
        limit=16,
    )
    attn_t, middle_rows, stats = call_kernel(
        functools.partial(forward_kernel, tok),
        [
            shape_of((HD, rows), jnp.bfloat16),
            shape_of((low_rank, rows), jnp.float32),
            shape_of((8, rows), jnp.float32),
        ],
        [],
        2 * pair_count * HD,
        pair_count // 2,
        scalars,
        own,
        other,
        own_total,
        own_stats,
        down_head,
        limit=16,
    )

    first_copy = rank % copies == 0
    middle_rows = middle_rows.astype(jnp.bfloat16).reshape(low_rank, ranks, tok)
    middle_rows = in_order(middle_rows.transpose(1, 0, 2))
    if copies > 1:
        middle_rows = jnp.where(first_copy, middle_rows, 0.0)
    (message,) = in_vmem(
        functools.partial(dout_kernel, copies),
        [shape_of((ranks, HD + 2 * low_rank, tok), jnp.bfloat16)],
        packed_own,
        received,
        middle_rows,
    )
    arrived = exchange(message)
    middle = jnp.sum(arrived[:, HD + low_rank :].astype(jnp.float32), axis=0)
    bit = 1
    while bit < heads:
        middle += lax.ppermute(middle, "head", [(i, i ^ bit) for i in range(heads)])
        bit *= 2
    up_part = 2.0 * dot_nn(middle.astype(jnp.bfloat16), output_gradient)

    dq, dk_own, dv_own, pair_other, down_part = call_kernel(
        functools.partial(backward_kernel, tok),
        [
            shape_of((ranks, tok, HD), jnp.bfloat16),
            shape_of((ranks, tok, HD), jnp.float32),
            shape_of((ranks, tok, HD), jnp.float32),
            shape_of((ranks, 2 * tok, HD), jnp.bfloat16),
            shape_of((low_rank, HD), jnp.float32),
        ],
        [pltpu.VMEM((rows, HD), jnp.float32)] * 4,
        10 * pair_count * HD,
        pair_count,
        scalars,
        own,
        other,
        in_order(arrived[:, : HD + low_rank]),
        attn_t,
        stats,
        limit=28,
    )
    pair_other, _ = lax.optimization_barrier((pair_other, middle))
    pair_received = swap(pair_other).astype(jnp.float32)
    down_rows = jnp.where(first_copy, down_part + swap(down_part), 0.0)
    dk = (dk_own + pair_received[:, :tok]).astype(jnp.bfloat16)
    dv = (dv_own + pair_received[:, tok:]).astype(jnp.bfloat16)
    down_rows = jnp.broadcast_to(down_rows.astype(jnp.bfloat16), (ranks, low_rank, HD))
    back_message = jnp.concatenate([*map(in_order, (dq, dk, dv)), down_rows], axis=1)
    back = exchange(back_message)
    outs = [shape_of((tok, feats), back.dtype)] * 3
    if seqs == ranks:
        outs.append(shape_of((low_rank, feats), jnp.float32))
    outs = list(in_vmem(functools.partial(unpack_kernel, copies), outs, back))
    if seqs > ranks:
        bits = [bit for bit in powers_below(seqs) if bit >= ranks]
        down_terms = back[::copies, 3 * tok :].astype(jnp.float32)
        down_terms = butterfly_sum(down_terms, "seq", bits, seqs)
        outs.append(down_terms.transpose(1, 0, 2).reshape(low_rank, feats))
    query_gradient, key_gradient, value_gradient, down_gradient = outs

    up_sum = butterfly_sum(up_part, "seq", powers_below(seqs), seqs)
    _, up_sum = lax.optimization_barrier((back, up_sum))
    up_gradient = butterfly_sum(up_sum, "sub", powers_below(subs), subs)
    return (query_gradient, key_gradient, value_gradient, down_gradient.T, up_gradient)


def solution(mesh):
    rows = P(("rep", "seq", "sub"), "head")
    sizes = (mesh.shape["seq"], mesh.shape["head"], mesh.shape["sub"])
    return jax.shard_map(
        functools.partial(on_device, sizes),
        mesh=mesh,
        in_specs=(rows, rows, rows, rows, P("head", "sub"), P("head", None), P()),
        out_specs=(rows, rows, rows, P(("rep", "head"), None), P("rep", "head")),
        check_vma=False,
    )
```

profile of v0, /device:TPU:0, one launch (start us, length us, event | category | flops | bytes accessed | tf_op | source)
XLA Modules:
  0.0 85.9 jit_solution(11938097698867023559)
XLA Ops:
  0.6 2.1 %shard_map.110 = bf16[8,384,128]{2,1,0:T(8,128)(2,1)} custom-call(bf16[128,1024]{1,0:T(8,128)(2,1)} %refs_0_.1, bf16[128,1024]{1,0:T(8,128)(2,1)} %refs_1_.1, bf16[128,1024]{1,0:T(8,128)(2,1)} %refs_2_.1), custom_call_target="tpu_custom_call" | custom-call | bytes 1572864 | tf_op jit(solution)/shard_map/pallas_call | solution.py:253
  2.8 7.9 %all-to-all-start = ((bf16[8,384,128]{2,1,0:T(8,128)(2,1)}), bf16[8,384,128]{2,1,0:T(8,128)(2,1)S(1)}, u32[]{:S(2)}, u32[]{:S(2)}) async-start(bf16[8,384,128]{2,1,0:T(8,128)(2,1)} %shard_map.110), calls=%async_computation | async-start | bytes 1572864 | tf_op jit(solution)/shard_map/all_to_all | solution.py:368
  10.6 1.7 %collective-permute-start = (bf16[128,2048]{1,0:T(8,128)(2,1)}, bf16[128,2048]{1,0:T(8,128)(2,1)S(1)}, u32[]{:S(2)}, u32[]{:S(2)}) collective-permute-start(bf16[128,2048]{1,0:T(8,128)(2,1)} %param.10), channel_id=1, source_target_pairs={{0,0},{1,2},{2,1},{3,3},{4,4},{5,6},{6,5},{7,7},{8,8},{9,10},{10,9... | collective-permute-start | bytes 1572872 | tf_op jit(solution)/shard_map/ppermute | solution.py:392
  12.3 1.7 %collective-permute-start.1 = (bf16[128,2048]{1,0:T(8,128)(2,1)}, bf16[128,2048]{1,0:T(8,128)(2,1)S(1)}, u32[]{:S(2)}, u32[]{:S(2)}) collective-permute-start(bf16[128,2048]{1,0:T(8,128)(2,1)} %param.10), channel_id=1, source_target_pairs={{0,2},{1,0},{2,3},{3,1},{4,6},{5,4},{6,7},{7,5},{8,10},{9,8},{10,1... | collective-permute-start | bytes 1572872 | tf_op jit(solution)/shard_map/ppermute | solution.py:392
  14.0 0.7 dynamic-slice_bitcast_fusion.down_t_ref
  14.8 3.5 %fusion.refs_2_ = bf16[1024,2048]{1,0:T(8,128)(2,1)S(1)} fusion(bf16[1024,2048]{1,0:T(8,128)(2,1)} %param.11, bf16[16,2048]{1,0:T(8,128)(2,1)S(1)} %constant_dynamic-slice_fusion.refs_3_, bf16[1024,16]{0,1:T(8,128)(2,1)} %param.12), kind=kOutput, calls=%fused_computation.1 | convolution fusion | flops 75497472 | bytes 8486912 | tf_op jit(solution)/shard_map/dot_general | solution.py:26
  18.3 7.7 %collective-permute-done.1.refs_1_ = bf16[128,2048]{1,0:T(8,128)(2,1)S(1)} collective-permute-done((bf16[128,2048]{1,0:T(8,128)(2,1)}, bf16[128,2048]{1,0:T(8,128)(2,1)S(1)}, u32[]{:S(2)}, u32[]{:S(2)}) %collective-permute-start.1) | collective-permute-done | bytes 524320 | tf_op jit(solution)/shard_map/ppermute | solution.py:392
  26.1 2.1 %shard_map.111 = (f32[1040,128]{1,0:T(8,128)S(1)}, bf16[1040,128]{1,0:T(8,128)(2,1)S(1)}) custom-call(s32[4]{0:T(128)S(1)} %pad_add_fusion.plan_ref, bf16[128,2048]{1,0:T(8,128)(2,1)S(1)} %collective-permute-done.refs_0_, bf16[128,2048]{1,0:T(8,128)(2,1)S(1)} %collective-permute-done.1.refs_1_, bf16[1024,2048]{1,0:T(8,128)(2,1)S(1)} %fusion.refs_2_, ...), custom_call_target="tpu_custom_call" | custom-call | bytes 1024 | tf_op jit(solution)/shard_map/pallas_call | solution.py:194
  28.4 0.8 collective-permute-start.2
  29.3 1.7 %shard_map.112 = (f32[128,1024]{1,0:T(8,128)S(1)}, f32[8,1024]{1,0:T(8,128)S(1)}) custom-call(s32[1]{0:T(128)} %bitcast.scalar_ref, bf16[8,384,128]{2,1,0:T(8,128)(2,1)S(1)} %maximum_select_fusion.own_ref), custom_call_target="tpu_custom_call" | custom-call | flops 335544320 | bytes 1343492 | tf_op jit(solution)/shard_map/pallas_call | solution.py:194
  31.0 2.5 %shard_map.113 = (bf16[128,1024]{1,0:T(8,128)(2,1)S(1)}, f32[16,1024]{1,0:T(8,128)S(1)}, f32[8,1024]{1,0:T(8,128)S(1)}) custom-call(s32[1]{0:T(128)} %bitcast.scalar_ref, bf16[8,384,128]{2,1,0:T(8,128)(2,1)S(1)} %maximum_select_fusion.own_ref, bf16[8,256,128]{2,1,0:T(8,128)(2,1)S(1)} %collective-permute-done.2.other_ref, ...), custom_call_target="tpu_custom_call" | custom-call | flops 335544320 | bytes 2232324 | tf_op jit(solution)/shard_map/pallas_call | solution.py:194
  33.7 14.4 %all_to_all.15 = bf16[8,160,128]{2,1,0:T(8,128)(2,1)S(1)} all-to-all(bf16[8,160,128]{2,1,0:T(8,128)(2,1)S(1)} %shard_map.114), channel_id=1, replica_groups={{16,20,24,28,0,4,8,12},{18,22,26,30,2,6,10,14},{17,21,25,29,1,5,9,13},{..., dimensions={0} | all-to-all | bytes 655360 | tf_op jit(solution)/shard_map/all_to_all | solution.py:368
  48.0 1.5 %collective-permute-start.4 = (f32[16,128]{1,0:T(8,128)S(1)}, f32[16,128]{1,0:T(8,128)S(1)}, u32[]{:S(2)}, u32[]{:S(2)}) collective-permute-start(f32[16,128]{1,0:T(8,128)S(1)} %convert_reduce_fusion), channel_id=1, source_target_pairs={{0,2},{2,0},{1,3},{3,1},{4,6},{6,4},{5,7},{7,5},{8,10},{10,8},{9,1... | collective-permute-start | bytes 24584 | tf_op jit(solution)/shard_map/ppermute | solution.py:469
  49.6 4.8 %shard_map.115 = (bf16[8,128,128]{2,1,0:T(8,128)(2,1)S(1)}, f32[8,128,128]{2,1,0:T(8,128)S(1)}, f32[8,128,128]{2,1,0:T(8,128)S(1)}, bf16[8,256,128]{2,1,0:T(8,128)(2,1)S(1)}, f32[16,128]{1,0:T(8,128)S(1)}) custom-call(s32[1]{0:T(128)} %bitcast.scalar_ref, bf16[8,384,128]{2,1,0:T(8,128)(2,1)S(1)} %maximum_select_fusion.own_ref, ...), custom_call_target="tpu_custom_call" | custom-call | flops 1677721600 | bytes 3743748 | tf_op jit(solution)/shard_map/pallas_call | solution.py:194
  54.5 0.6 collective-permute-start.6
  55.2 0.9 %collective-permute-start.7 = (bf16[16,2048]{1,0:T(8,128)(2,1)S(1)}, bf16[16,2048]{1,0:T(8,128)(2,1)S(1)}, u32[]{:S(2)}, u32[]{:S(2)}) collective-permute-start(bf16[16,2048]{1,0:T(8,128)(2,1)S(1)} %fusion.1), channel_id=1, source_target_pairs={{0,4},{4,0},{8,12},{12,8},{16,20},{20,16},{24,28},{28,24},{1,5},{5... | collective-permute-start | bytes 196616 | tf_op jit(solution)/shard_map/ppermute | solution.py:217
  56.8 1.0 %pad_maximum_fusion = bf16[8,400,128]{2,1,0:T(8,128)(2,1)} fusion(bf16[8,16,128]{2,1,0:T(8,128)(2,1)S(1)} %broadcast_in_dim.9, bf16[8,128,128]{2,1,0:T(8,128)(2,1)S(1)} %maximum_select_fusion.3, bf16[8,128,128]{2,1,0:T(8,128)(2,1)S(1)} %get-tuple-element.66, bf16[8,128,128]{2,1,0:T(8,128)(2,1)S(1)} %get-tuple-element.65), kind=kLoop, calls=%fused_computation.4 | loop fusion | flops 3276800 | bytes 1638400 | tf_op jit(solution)/shard_map/concatenate | solution.py:499
  57.7 5.1 %all-to-all-start.2 = ((bf16[8,400,128]{2,1,0:T(8,128)(2,1)}), bf16[8,400,128]{2,1,0:T(8,128)(2,1)S(1)}, u32[]{:S(2)}, u32[]{:S(2)}) async-start(bf16[8,400,128]{2,1,0:T(8,128)(2,1)} %pad_maximum_fusion), calls=%async_computation.2 | async-start | bytes 1638400 | tf_op jit(solution)/shard_map/all_to_all | solution.py:368
  62.9 0.6 collective-permute-start.8
  63.5 14.4 %collective-permute-done.8 = bf16[16,2048]{1,0:T(8,128)(2,1)S(1)} collective-permute-done((bf16[16,2048]{1,0:T(8,128)(2,1)S(1)}, bf16[16,2048]{1,0:T(8,128)(2,1)S(1)}, u32[]{:S(2)}, u32[]{:S(2)}) %collective-permute-start.8) | collective-permute-done | bytes 65568 | tf_op jit(solution)/shard_map/ppermute | solution.py:217
  78.0 3.0 %collective-permute-start.9 = (bf16[16,2048]{1,0:T(8,128)(2,1)S(1)}, bf16[16,2048]{1,0:T(8,128)(2,1)S(1)}, u32[]{:S(2)}, u32[]{:S(2)}) collective-permute-start(bf16[16,2048]{1,0:T(8,128)(2,1)S(1)} %add_convert_fusion), channel_id=1, source_target_pairs={{0,16},{4,20},{8,24},{12,28},{16,0},{20,4},{24,8},{28,12},{1,17},{... | collective-permute-start | bytes 196616 | tf_op jit(solution)/shard_map/ppermute | solution.py:217
  80.9 3.0 %collective-permute-done.9 = bf16[16,2048]{1,0:T(8,128)(2,1)S(1)} collective-permute-done((bf16[16,2048]{1,0:T(8,128)(2,1)S(1)}, bf16[16,2048]{1,0:T(8,128)(2,1)S(1)}, u32[]{:S(2)}, u32[]{:S(2)}) %collective-permute-start.9) | collective-permute-done | bytes 65568 | tf_op jit(solution)/shard_map/ppermute | solution.py:217
  84.0 1.1 %shard_map.116 = (bf16[128,1024]{1,0:T(8,128)(2,1)}, bf16[128,1024]{1,0:T(8,128)(2,1)}, bf16[128,1024]{1,0:T(8,128)(2,1)}, f32[16,1024]{1,0:T(8,128)}) custom-call(bf16[8,400,128]{2,1,0:T(8,128)(2,1)S(1)} %all-to-all-done.2.back_ref), custom_call_target="tpu_custom_call" | custom-call | bytes 1671168 | tf_op jit(solution)/shard_map/pallas_call | solution.py:281
  85.3 0.7 convert_add_fusion
  (43 shorter events, 1.7 us)
Async XLA Ops:
  0.6 14.1 %copy-start = (bf16[16,4096]{1,0:T(8,128)(2,1)S(1)}, bf16[16,4096]{1,0:T(8,128)(2,1)}, u32[]{:S(2)}) copy-start(bf16[16,4096]{1,0:T(8,128)(2,1)} %param.13) | copy-start | bytes 393220
  2.8 25.4 %all-to-all-start = ((bf16[8,384,128]{2,1,0:T(8,128)(2,1)}), bf16[8,384,128]{2,1,0:T(8,128)(2,1)S(1)}, u32[]{:S(2)}, u32[]{:S(2)}) async-start(bf16[8,384,128]{2,1,0:T(8,128)(2,1)} %shard_map.110), calls=%async_computation | async-start | bytes 1572864 | tf_op jit(solution)/shard_map/all_to_all | solution.py:368
  10.6 7.7 %collective-permute-start = (bf16[128,2048]{1,0:T(8,128)(2,1)}, bf16[128,2048]{1,0:T(8,128)(2,1)S(1)}, u32[]{:S(2)}, u32[]{:S(2)}) collective-permute-start(bf16[128,2048]{1,0:T(8,128)(2,1)} %param.10), channel_id=1, source_target_pairs={{0,0},{1,2},{2,1},{3,3},{4,4},{5,6},{6,5},{7,7},{8,8},{9,10},{10,9... | collective-permute-start | bytes 1572872 | tf_op jit(solution)/shard_map/ppermute | solution.py:392
  12.3 13.7 %collective-permute-start.1 = (bf16[128,2048]{1,0:T(8,128)(2,1)}, bf16[128,2048]{1,0:T(8,128)(2,1)S(1)}, u32[]{:S(2)}, u32[]{:S(2)}) collective-permute-start(bf16[128,2048]{1,0:T(8,128)(2,1)} %param.10), channel_id=1, source_target_pairs={{0,2},{1,0},{2,3},{3,1},{4,6},{5,4},{6,7},{7,5},{8,10},{9,8},{10,1... | collective-permute-start | bytes 1572872 | tf_op jit(solution)/shard_map/ppermute | solution.py:392
  28.4 2.6 %collective-permute-start.2 = (bf16[8,256,128]{2,1,0:T(8,128)(2,1)S(1)}, bf16[8,256,128]{2,1,0:T(8,128)(2,1)S(1)}, u32[]{:S(2)}, u32[]{:S(2)}) collective-permute-start(bf16[8,256,128]{2,1,0:T(8,128)(2,1)S(1)} %slice.70), channel_id=1, source_target_pairs={{0,1},{1,0},{2,3},{3,2},{4,5},{5,4},{6,7},{7,6},{8,9},{9,8},{10,11... | collective-permute-start | bytes 1572872 | tf_op jit(solution)/shard_map/ppermute | solution.py:375
  29.2 4.4 %collective-permute-start.3 = (bf16[1040,128]{1,0:T(8,128)(2,1)S(1)}, bf16[1040,128]{1,0:T(8,128)(2,1)S(1)}, u32[]{:S(2)}, u32[]{:S(2)}) collective-permute-start(bf16[1040,128]{1,0:T(8,128)(2,1)S(1)} %get-tuple-element.31), channel_id=1, source_target_pairs={{0,1},{1,0},{2,3},{3,2},{4,5},{5,4},{6,7},{7,6},{8,9},{9,8},{10,11... | collective-permute-start | bytes 798728 | tf_op jit(solution)/shard_map/ppermute | solution.py:375
  48.0 7.0 %copy-start.1 = (bf16[128,2048]{1,0:T(8,128)(2,1)S(1)}, bf16[128,2048]{1,0:T(8,128)(2,1)}, u32[]{:S(2)}) copy-start(bf16[128,2048]{1,0:T(8,128)(2,1)} %param.10) | copy-start | bytes 1572868
  48.0 6.3 %collective-permute-start.4 = (f32[16,128]{1,0:T(8,128)S(1)}, f32[16,128]{1,0:T(8,128)S(1)}, u32[]{:S(2)}, u32[]{:S(2)}) collective-permute-start(f32[16,128]{1,0:T(8,128)S(1)} %convert_reduce_fusion), channel_id=1, source_target_pairs={{0,2},{2,0},{1,3},{3,1},{4,6},{6,4},{5,7},{7,5},{8,10},{10,8},{9,1... | collective-permute-start | bytes 24584 | tf_op jit(solution)/shard_map/ppermute | solution.py:469
  54.4 2.0 %collective-permute-start.5 = (bf16[8,256,128]{2,1,0:T(8,128)(2,1)S(1)}, bf16[8,256,128]{2,1,0:T(8,128)(2,1)S(1)}, u32[]{:S(2)}, u32[]{:S(2)}) collective-permute-start(bf16[8,256,128]{2,1,0:T(8,128)(2,1)S(1)} %get-tuple-element.43), channel_id=1, source_target_pairs={{0,1},{1,0},{2,3},{3,2},{4,5},{5,4},{6,7},{7,6},{8,9},{9,8},{10,11... | collective-permute-start | bytes 1572872 | tf_op jit(solution)/shard_map/ppermute | solution.py:375
  54.5 1.9 %collective-permute-start.6 = (f32[16,128]{1,0:T(8,128)S(1)}, f32[16,128]{1,0:T(8,128)S(1)}, u32[]{:S(2)}, u32[]{:S(2)}) collective-permute-start(f32[16,128]{1,0:T(8,128)S(1)} %get-tuple-element.45), channel_id=1, source_target_pairs={{0,1},{1,0},{2,3},{3,2},{4,5},{5,4},{6,7},{7,6},{8,9},{9,8},{10,11... | collective-permute-start | bytes 24584 | tf_op jit(solution)/shard_map/ppermute | solution.py:375
  55.2 7.6 %collective-permute-start.7 = (bf16[16,2048]{1,0:T(8,128)(2,1)S(1)}, bf16[16,2048]{1,0:T(8,128)(2,1)S(1)}, u32[]{:S(2)}, u32[]{:S(2)}) collective-permute-start(bf16[16,2048]{1,0:T(8,128)(2,1)S(1)} %fusion.1), channel_id=1, source_target_pairs={{0,4},{4,0},{8,12},{12,8},{16,20},{20,16},{24,28},{28,24},{1,5},{5... | collective-permute-start | bytes 196616 | tf_op jit(solution)/shard_map/ppermute | solution.py:217
  57.7 26.2 %all-to-all-start.2 = ((bf16[8,400,128]{2,1,0:T(8,128)(2,1)}), bf16[8,400,128]{2,1,0:T(8,128)(2,1)S(1)}, u32[]{:S(2)}, u32[]{:S(2)}) async-start(bf16[8,400,128]{2,1,0:T(8,128)(2,1)} %pad_maximum_fusion), calls=%async_computation.2 | async-start | bytes 1638400 | tf_op jit(solution)/shard_map/all_to_all | solution.py:368
  62.9 15.1 %collective-permute-start.8 = (bf16[16,2048]{1,0:T(8,128)(2,1)S(1)}, bf16[16,2048]{1,0:T(8,128)(2,1)S(1)}, u32[]{:S(2)}, u32[]{:S(2)}) collective-permute-start(bf16[16,2048]{1,0:T(8,128)(2,1)S(1)} %add_convert_fusion.1), channel_id=1, source_target_pairs={{0,8},{4,12},{8,0},{12,4},{16,24},{20,28},{24,16},{28,20},{1,9},{5... | collective-permute-start | bytes 196616 | tf_op jit(solution)/shard_map/ppermute | solution.py:217
  78.0 5.9 %collective-permute-start.9 = (bf16[16,2048]{1,0:T(8,128)(2,1)S(1)}, bf16[16,2048]{1,0:T(8,128)(2,1)S(1)}, u32[]{:S(2)}, u32[]{:S(2)}) collective-permute-start(bf16[16,2048]{1,0:T(8,128)(2,1)S(1)} %add_convert_fusion), channel_id=1, source_target_pairs={{0,16},{4,20},{8,24},{12,28},{16,0},{20,4},{24,8},{28,12},{1,17},{... | collective-permute-start | bytes 196616 | tf_op jit(solution)/shard_map/ppermute | solution.py:217
  83.9 1.3 %collective-permute-start.10 = (bf16[16,2048]{1,0:T(8,128)(2,1)S(1)}, bf16[16,2048]{1,0:T(8,128)(2,1)S(1)}, u32[]{:S(2)}, u32[]{:S(2)}) collective-permute-start(bf16[16,2048]{1,0:T(8,128)(2,1)S(1)} %convert_add_fusion.1), channel_id=1, source_target_pairs={{0,1},{1,0},{2,3},{3,2},{4,5},{5,4},{6,7},{7,6},{8,9},{9,8},{10,11... | collective-permute-start | bytes 196616 | tf_op jit(solution)/shard_map/ppermute | solution.py:217
where the time goes:
time: 86.4 us; the launch traced here: 85.9 us
  waiting for transfers between devices  25.5 us (30%)
  starting transfers between devices  23.9 us (28%)
  Pallas kernels  14.4 us (17%)
  blocking collectives  14.4 us (17%)
  matrix products  3.69 us (4%)
  other arithmetic  2.27 us (3%)
  between operations  0.89 us (1%)
  local copies, waits for them, and re-layouts  0.88 us (1%)
    ppermute x4, waiting for transfers between devices, butterfly_sum(): taken = lax.ppermute(value, axis, pairs)  17.6 us
    all_to_all x1, blocking collectives, exchange(): lax.all_to_all(parts, ('seq', 'head'), 0, 0, axis_index_groups=groups, ti...  14.4 us
    all_to_all x2, starting transfers between devices, exchange(): lax.all_to_all(parts, ('seq', 'head'), 0, 0, axis_index_groups=groups, ti...  13 us
    pallas_call x4, Pallas kernels, call_kernel(): pl.pallas_call(body, out_shape=outs, in_specs=specs, out_specs=[pl.BlockS...  11.1 us
    ppermute x2, waiting for transfers between devices, on_device(): pieces.append(lax.ppermute(output_gradient, ('head', 'sub'), pairs))  7.71 us
    ppermute x4, starting transfers between devices, butterfly_sum(): taken = lax.ppermute(value, axis, pairs)  4.55 us
    dot_general x2, matrix products, dot_nn(): return jnp.dot(left, right, preferred_element_type=jnp.float32)  3.69 us
    ppermute x2, starting transfers between devices, on_device(): pieces.append(lax.ppermute(output_gradient, ('head', 'sub'), pairs))  3.42 us
  transfers between devices with their start and end apart: 13, of which 5 were waited for; matrix products, arithmetic and copies ran while one was open for 7% of the time, Pallas kernels for 14%

commit v1 on v0

--- a/solution.py
+++ b/solution.py
@@ -106,9 +106,29 @@
         attn = dot_nn(values_t[:, : upto * tok], powers.astype(jnp.bfloat16))
         attn = ((attn + total_ref[:, here] * share) * inverse).astype(jnp.bfloat16)
         attn_ref[:, here] = attn
-        mid_ref[:, here] = dot_nn(down_t_ref[...], attn)
         stat_ref[0:1, here] = highest
         stat_ref[1:2, here] = inverse
+    mid_ref[...] = dot_nn(down_t_ref[...], attn_ref[...])
+
+
+def tile_rows(tile):
+    return pl.ds(tile * (tile + 1) // 2 * TILE, (tile + 1) * TILE)
+
+
+def prob_kernel(tok, scalar_ref, own_ref, other_ref, stat_ref, prob_ref, keys_t_ref):
+    blocks = own_ref.shape[0]
+    step = TILE // tok
+    visible = (own_visible(), other_visible(scalar_ref[0], tok))
+    for tile in range(blocks // step):
+        upto = (tile + 1) * step
+        here = pl.ds(tile * TILE, TILE)
+        queries = own_ref[tile * step : upto, 0:tok, :].reshape(TILE, HD)
+        for side, (ref, first) in enumerate(((own_ref, tok), (other_ref, 0))):
+            scores = scores_of(rows_of(ref, upto, first, tok), queries, visible[side])
+            powers = jnp.exp2((scores - stat_ref[0:1, here]) * LOG2_SCALE)
+            prob_ref[side, tile_rows(tile), :] = powers * stat_ref[1:2, here]
+    keys_t_ref[0] = rows_of(own_ref, blocks, tok, tok).T
+    keys_t_ref[1] = rows_of(other_ref, blocks, 0, tok).T
 
 
 def backward_kernel(
@@ -118,7 +138,8 @@
     other_ref,
     dout_ref,
     attn_ref,
-    stat_ref,
+    prob_ref,
+    keys_t_ref,
     dq_ref,
     dk_own_ref,
     dv_own_ref,
@@ -131,28 +152,21 @@
 ):
     blocks = own_ref.shape[0]
     step = TILE // tok
-    sub = scalar_ref[0]
     low_rank = down_grad_ref.shape[0]
-    keys_own_t = rows_of(own_ref, blocks, tok, tok).T
-    keys_other_t = rows_of(other_ref, blocks, 0, tok).T
     tiles = blocks // step
-    down_total = jnp.zeros((low_rank, HD), jnp.float32)
+    lora = jnp.concatenate(
+        [dout_ref[block, HD : HD + low_rank, :] for block in range(blocks)], axis=1
+    )
+    down_grad_ref[...] = 2.0 * dot_nt(lora, attn_ref[...])
     for tile in reversed(range(tiles)):
         upto = (tile + 1) * step
         width = upto * tok
-        at = tile * TILE
         queries = own_ref[tile * step : upto, 0:tok, :].reshape(TILE, HD)
         douts_t = jnp.concatenate(
             [dout_ref[block, 0:HD, :] for block in range(tile * step, upto)], axis=1
         )
-        highest = stat_ref[0:1, at : at + TILE]
-        inverse = stat_ref[1:2, at : at + TILE]
-        own = scores_of(rows_of(own_ref, upto, tok, tok), queries, own_visible())
-        other = scores_of(
-            rows_of(other_ref, upto, 0, tok), queries, other_visible(sub, tok)
-        )
-        own = jnp.exp2((own - highest) * LOG2_SCALE) * inverse
-        other = jnp.exp2((other - highest) * LOG2_SCALE) * inverse
+        own = prob_ref[0, tile_rows(tile), :]
+        other = prob_ref[1, tile_rows(tile), :]
         dprob_own = dot_nn(rows_of(own_ref, upto, 2 * tok, tok), douts_t)
         dprob_other = dot_nn(rows_of(other_ref, upto, tok, tok), douts_t)
         delta = jnp.sum(own * dprob_own, axis=0, keepdims=True) + jnp.sum(
@@ -160,7 +174,8 @@
         )
         ds_own = (own * (dprob_own - delta)).astype(jnp.bfloat16)
         ds_other = (other * (dprob_other - delta)).astype(jnp.bfloat16)
-        dq = dot_nn(keys_own_t[:, :width], ds_own) + dot_nn(keys_other_t[:, :width], ds_other)
+        dq = dot_nn(keys_t_ref[0, :, 0:width], ds_own)
+        dq += dot_nn(keys_t_ref[1, :, 0:width], ds_other)
         dq = (dq * SCALE).T.astype(jnp.bfloat16)
         dq_ref[tile * step : upto] = dq.reshape(step, tok, HD)
         terms = (
@@ -174,16 +189,11 @@
                 total[...] = term
             else:
                 total[0:width] += term
-        for i in range(step):
-            lora = dout_ref[tile * step + i, HD : HD + low_rank, :]
-            attn = attn_ref[:, at + i * tok : at + (i + 1) * tok]
-            down_total += dot_nt(lora, attn)
     shape = (blocks, tok, HD)
     dk_own_ref[...] = (dk_own[...] * SCALE).reshape(shape)
     dv_own_ref[...] = dv_own[...].reshape(shape)
     pair_other_ref[:, 0:tok, :] = (dk_other[...] * SCALE).astype(jnp.bfloat16).reshape(shape)
     pair_other_ref[:, tok : 2 * tok, :] = dv_other[...].astype(jnp.bfloat16).reshape(shape)
-    down_grad_ref[...] = 2.0 * down_total
 
 
 def call_kernel(body, outs, scratch, flops, exps, *operands, declared=None, limit=48):
@@ -264,14 +274,21 @@
 
 
 def unpack_kernel(copies, back_ref, *refs):
-    out_refs, down_ref = refs[:3], refs[3] if len(refs) > 3 else None
+    (*out_refs, sems), down_ref = (refs[:3] + refs[-1:]), refs[3] if len(refs) > 4 else None
     tok = out_refs[0].shape[0]
+    moves = []
     for at_head in range(out_refs[0].shape[1] // HD):
-        cols = slice(at_head * HD, (at_head + 1) * HD)
+        cols = pl.ds(at_head * HD, HD)
         for n, ref in enumerate(out_refs):
-            ref[:, cols] = back_ref[at_head * copies, n * tok : (n + 1) * tok, :]
-        if down_ref is not None:
+            block = back_ref.at[at_head * copies, pl.ds(n * tok, tok), :]
+            moves.append(pltpu.make_async_copy(block, ref.at[:, cols], sems.at[len(moves)]))
+            moves[-1].start()
+    if down_ref is not None:
+        for at_head in range(out_refs[0].shape[1] // HD):
+            cols = slice(at_head * HD, (at_head + 1) * HD)
             down_ref[:, cols] = back_ref[at_head * copies, 3 * tok :, :].astype(jnp.float32)
+    for move in moves:
+        move.wait()
 
 
 def in_vmem(body, outs, *operands):
@@ -463,6 +480,22 @@
         middle_rows,
     )
     arrived = exchange(message)
+    tiles = rows // TILE
+    probs, keys_t = call_kernel(
+        functools.partial(prob_kernel, tok),
+        [
+            shape_of((2, tiles * (tiles + 1) // 2 * TILE, TILE), jnp.float32),
+            shape_of((2, HD, rows), jnp.bfloat16),
+        ],
+        [],
+        2 * pair_count * HD,
+        pair_count,
+        scalars,
+        own,
+        other,
+        stats,
+        limit=16,
+    )
     middle = jnp.sum(arrived[:, HD + low_rank :].astype(jnp.float32), axis=0)
     bit = 1
     while bit < heads:
@@ -480,15 +513,16 @@
             shape_of((low_rank, HD), jnp.float32),
         ],
         [pltpu.VMEM((rows, HD), jnp.float32)] * 4,
-        10 * pair_count * HD,
-        pair_count,
+        8 * pair_count * HD,
+        0,
         scalars,
         own,
         other,
         in_order(arrived[:, : HD + low_rank]),
         attn_t,
-        stats,
-        limit=28,
+        probs,
+        keys_t,
+        limit=24,
     )
     pair_other, _ = lax.optimization_barrier((pair_other, middle))
     pair_received = swap(pair_other).astype(jnp.float32)
@@ -501,7 +535,20 @@
     outs = [shape_of((tok, feats), back.dtype)] * 3
     if seqs == ranks:
         outs.append(shape_of((low_rank, feats), jnp.float32))
-    outs = list(in_vmem(functools.partial(unpack_kernel, copies), outs, back))
+    whole = pl.BlockSpec(memory_space=pltpu.VMEM)
+    outs = list(
+        pl.pallas_call(
+            functools.partial(unpack_kernel, copies),
+            out_shape=outs,
+            in_specs=[whole],
+            out_specs=[pl.BlockSpec(memory_space=pltpu.HBM)] * 3 + [whole] * (len(outs) - 3),
+            scratch_shapes=[pltpu.SemaphoreType.DMA((3 * local_heads,))],
+            compiler_params=pltpu.CompilerParams(vmem_limit_bytes=16 * 1024 * 1024),
+            cost_estimate=pl.CostEstimate(
+                flops=0, bytes_accessed=4 * back.size, transcendentals=0
+            ),
+        )(back)
+    )
     if seqs > ranks:
         bits = [bit for bit in powers_below(seqs) if bit >= ranks]
         down_terms = back[::copies, 3 * tok :].astype(jnp.float32)

time: 86.4 us -> 88.9 us (1.029)
  blocking collectives: 14.4 us -> 0 us
  starting transfers between devices: 23.9 us -> 29.9 us
  local copies, waits for them, and re-layouts: 0.88 us -> 5.74 us
  waiting for transfers between devices: 25.5 us -> 30.2 us
  Pallas kernels: 14.4 us -> 15.6 us
    all_to_all x1 -> x0, blocking collectives: 14.4 us -> none  [exchange(): lax.all_to_all(parts, ('seq', 'head'), 0, 0, axis_index_groups=groups, ti...]
    all_to_all x2 -> x3, waiting for transfers between devices: 0.01 us -> 7.23 us  [exchange(): lax.all_to_all(parts, ('seq', 'head'), 0, 0, axis_index_groups=groups, ti...]
    all_to_all x2 -> x3, starting transfers between devices: 13 us -> 18.4 us  [exchange(): lax.all_to_all(parts, ('seq', 'head'), 0, 0, axis_index_groups=groups, ti...]
    unnamed x4 -> x8, local copies, waits for them, and re-layouts: 0.01 us -> 4.87 us
    ppermute x2, waiting for transfers between devices: 7.71 us -> 5.3 us  [on_device(): pieces.append(lax.ppermute(output_gradient, ('head', 'sub'), pairs))]
    pallas_call x0 -> x1, Pallas kernels: none -> 1.7 us  [on_device(): pl.pallas_call(functools.partial(unpack_kernel, copies), out_shape=outs,...]
    ppermute x4, starting transfers between devices: 4.55 us -> 5.66 us  [butterfly_sum(): taken = lax.ppermute(value, axis, pairs)]
    pallas_call x4 -> x5, Pallas kernels: 11.1 us -> 11 us  [call_kernel(): pl.pallas_call(body, out_shape=outs, in_specs=specs, out_specs=[pl.BlockS...]
  transfers between devices with their start and end apart: 13 -> 14, of which waited for: 5 -> 5; matrix products, arithmetic and copies ran while one was open for 7% -> 7% of each run, Pallas kernels for 14% -> 14%
where the time goes in v1:
time: 88.9 us; the launch traced here: 88.4 us
  waiting for transfers between devices  30.2 us (34%)
  starting transfers between devices  29.9 us (34%)
  Pallas kernels  15.6 us (18%)
  local copies, waits for them, and re-layouts  5.74 us (6%)
  matrix products  3.69 us (4%)
  other arithmetic  2.25 us (3%)
  between operations  0.93 us (1%)
    all_to_all x3, starting transfers between devices, exchange(): lax.all_to_all(parts, ('seq', 'head'), 0, 0, axis_index_groups=groups, ti...  18.4 us
    ppermute x4, waiting for transfers between devices, butterfly_sum(): taken = lax.ppermute(value, axis, pairs)  17.7 us
    pallas_call x5, Pallas kernels, call_kernel(): pl.pallas_call(body, out_shape=outs, in_specs=specs, out_specs=[pl.BlockS...  11 us
    all_to_all x3, waiting for transfers between devices, exchange(): lax.all_to_all(parts, ('seq', 'head'), 0, 0, axis_index_groups=groups, ti...  7.23 us
    ppermute x4, starting transfers between devices, butterfly_sum(): taken = lax.ppermute(value, axis, pairs)  5.66 us
    ppermute x2, waiting for transfers between devices, on_device(): pieces.append(lax.ppermute(output_gradient, ('head', 'sub'), pairs))  5.3 us
    unnamed x8, local copies, waits for them, and re-layouts  4.87 us
    dot_general x2, matrix products, dot_nn(): return jnp.dot(left, right, preferred_element_type=jnp.float32)  3.69 us
  transfers between devices with their start and end apart: 14, of which 5 were waited for; matrix products, arithmetic and copies ran while one was open for 7% of the time, Pallas kernels for 14%

profile of v1, /device:TPU:0, one launch (start us, length us, event | category | flops | bytes accessed | tf_op | source)
XLA Modules:
  0.0 88.4 jit_solution(4009229137358900587)
XLA Ops:
  0.6 2.1 %shard_map.110 = bf16[8,384,128]{2,1,0:T(8,128)(2,1)} custom-call(bf16[128,1024]{1,0:T(8,128)(2,1)} %refs_0_.1, bf16[128,1024]{1,0:T(8,128)(2,1)} %refs_1_.1, bf16[128,1024]{1,0:T(8,128)(2,1)} %refs_2_.1), custom_call_target="tpu_custom_call" | custom-call | bytes 1572864 | tf_op jit(solution)/shard_map/pallas_call | solution.py:263
  2.8 7.9 %all-to-all-start = ((bf16[8,384,128]{2,1,0:T(8,128)(2,1)}), bf16[8,384,128]{2,1,0:T(8,128)(2,1)S(1)}, u32[]{:S(2)}, u32[]{:S(2)}) async-start(bf16[8,384,128]{2,1,0:T(8,128)(2,1)} %shard_map.110), calls=%async_computation | async-start | bytes 1572864 | tf_op jit(solution)/shard_map/all_to_all | solution.py:385
  10.7 1.5 %collective-permute-start.1 = (bf16[128,2048]{1,0:T(8,128)(2,1)}, bf16[128,2048]{1,0:T(8,128)(2,1)S(1)}, u32[]{:S(2)}, u32[]{:S(2)}) collective-permute-start(bf16[128,2048]{1,0:T(8,128)(2,1)} %param.10), channel_id=1, source_target_pairs={{0,2},{1,0},{2,3},{3,1},{4,6},{5,4},{6,7},{7,5},{8,10},{9,8},{10,1... | collective-permute-start | bytes 1572872 | tf_op jit(solution)/shard_map/ppermute | solution.py:409
  12.1 1.7 %collective-permute-start = (bf16[128,2048]{1,0:T(8,128)(2,1)}, bf16[128,2048]{1,0:T(8,128)(2,1)S(1)}, u32[]{:S(2)}, u32[]{:S(2)}) collective-permute-start(bf16[128,2048]{1,0:T(8,128)(2,1)} %param.10), channel_id=1, source_target_pairs={{0,0},{1,2},{2,1},{3,3},{4,4},{5,6},{6,5},{7,7},{8,8},{9,10},{10,9... | collective-permute-start | bytes 1572872 | tf_op jit(solution)/shard_map/ppermute | solution.py:409
  14.6 3.5 %fusion.refs_2_ = bf16[1024,2048]{1,0:T(8,128)(2,1)S(1)} fusion(bf16[1024,2048]{1,0:T(8,128)(2,1)} %param.11, bf16[16,2048]{1,0:T(8,128)(2,1)S(1)} %constant_dynamic-slice_fusion.refs_3_, bf16[1024,16]{0,1:T(8,128)(2,1)} %param.12), kind=kOutput, calls=%fused_computation.1 | convolution fusion | flops 75497472 | bytes 8486912 | tf_op jit(solution)/shard_map/dot_general | solution.py:26
  18.1 5.3 %collective-permute-done.1.refs_1_ = bf16[128,2048]{1,0:T(8,128)(2,1)S(1)} collective-permute-done((bf16[128,2048]{1,0:T(8,128)(2,1)}, bf16[128,2048]{1,0:T(8,128)(2,1)S(1)}, u32[]{:S(2)}, u32[]{:S(2)}) %collective-permute-start.1) | collective-permute-done | bytes 524320 | tf_op jit(solution)/shard_map/ppermute | solution.py:409
  23.4 2.1 %shard_map.111 = (f32[1040,128]{1,0:T(8,128)S(1)}, bf16[1040,128]{1,0:T(8,128)(2,1)S(1)}) custom-call(s32[4]{0:T(128)S(1)} %pad_add_fusion.plan_ref, bf16[128,2048]{1,0:T(8,128)(2,1)S(1)} %collective-permute-done.refs_0_, bf16[128,2048]{1,0:T(8,128)(2,1)S(1)} %collective-permute-done.1.refs_1_, bf16[1024,2048]{1,0:T(8,128)(2,1)S(1)} %fusion.refs_2_, ...), custom_call_target="tpu_custom_call" | custom-call | bytes 1024 | tf_op jit(solution)/shard_map/pallas_call | solution.py:204
  25.5 2.6 %all-to-all-done = bf16[8,384,128]{2,1,0:T(8,128)(2,1)S(1)} async-done(((bf16[8,384,128]{2,1,0:T(8,128)(2,1)}), bf16[8,384,128]{2,1,0:T(8,128)(2,1)S(1)}, u32[]{:S(2)}, u32[]{:S(2)}) %all-to-all-start) | async-done | bytes 786464 | tf_op jit(solution)/shard_map/all_to_all | solution.py:385
  28.9 1.7 %shard_map.112 = (f32[128,1024]{1,0:T(8,128)S(1)}, f32[8,1024]{1,0:T(8,128)S(1)}) custom-call(s32[1]{0:T(128)} %bitcast.scalar_ref, bf16[8,384,128]{2,1,0:T(8,128)(2,1)S(1)} %maximum_select_fusion.own_ref), custom_call_target="tpu_custom_call" | custom-call | flops 335544320 | bytes 1343492 | tf_op jit(solution)/shard_map/pallas_call | solution.py:204
  30.6 2.1 %shard_map.113 = (bf16[128,1024]{1,0:T(8,128)(2,1)S(1)}, f32[16,1024]{1,0:T(8,128)S(1)}, f32[8,1024]{1,0:T(8,128)S(1)}) custom-call(s32[1]{0:T(128)} %bitcast.scalar_ref, bf16[8,384,128]{2,1,0:T(8,128)(2,1)S(1)} %maximum_select_fusion.own_ref, bf16[8,256,128]{2,1,0:T(8,128)(2,1)S(1)} %collective-permute-done.2.other_ref, ...), custom_call_target="tpu_custom_call" | custom-call | flops 335544320 | bytes 2232324 | tf_op jit(solution)/shard_map/pallas_call | solution.py:204
  33.6 5.4 %all-to-all-start.1 = ((bf16[8,160,128]{2,1,0:T(8,128)(2,1)}), bf16[8,160,128]{2,1,0:T(8,128)(2,1)S(1)}, u32[]{:S(2)}, u32[]{:S(2)}) async-start(bf16[8,160,128]{2,1,0:T(8,128)(2,1)} %shard_map.114), calls=%async_computation.1 | async-start | bytes 655360 | tf_op jit(solution)/shard_map/all_to_all | solution.py:385
  39.0 1.0 %shard_map.115 = (f32[2,2560,256]{2,1,0:T(8,128)S(1)}, bf16[2,128,1024]{2,1,0:T(8,128)(2,1)S(1)}) custom-call(s32[1]{0:T(128)} %bitcast.scalar_ref, bf16[8,384,128]{2,1,0:T(8,128)(2,1)S(1)} %maximum_select_fusion.own_ref, bf16[8,256,128]{2,1,0:T(8,128)(2,1)S(1)} %collective-permute-done.2.other_ref, f32[8,1024]{1,0:T(8,128)S(1)} %get-tuple-element.41.stat_ref), custom_call_target="tpu_custom_call" | custom-call | flops 335544320 | bytes 7110660 | tf_op jit(solution)/shard_map/pallas_call | solution.py:204
  40.0 2.3 %copy-done.1 = f32[2,2560,256]{2,1,0:T(8,128)} copy-done((f32[2,2560,256]{2,1,0:T(8,128)}, f32[2,2560,256]{2,1,0:T(8,128)S(1)}, u32[]{:S(2)}) %copy-start.1) | copy-done | bytes 5242904
  42.3 4.6 %all-to-all-done.1 = bf16[8,160,128]{2,1,0:T(8,128)(2,1)S(1)} async-done(((bf16[8,160,128]{2,1,0:T(8,128)(2,1)}), bf16[8,160,128]{2,1,0:T(8,128)(2,1)S(1)}, u32[]{:S(2)}, u32[]{:S(2)}) %all-to-all-start.1) | async-done | bytes 327712 | tf_op jit(solution)/shard_map/all_to_all | solution.py:385
  47.0 1.5 %collective-permute-start.4 = (f32[16,128]{1,0:T(8,128)S(1)}, f32[16,128]{1,0:T(8,128)S(1)}, u32[]{:S(2)}, u32[]{:S(2)}) collective-permute-start(f32[16,128]{1,0:T(8,128)S(1)} %convert_reduce_fusion), channel_id=1, source_target_pairs={{0,2},{2,0},{1,3},{3,1},{4,6},{6,4},{5,7},{7,5},{8,10},{10,8},{9,1... | collective-permute-start | bytes 24584 | tf_op jit(solution)/shard_map/ppermute | solution.py:502
  48.6 2.5 %copy-done.2 = f32[2,2560,256]{2,1,0:T(8,128)S(1)} copy-done((f32[2,2560,256]{2,1,0:T(8,128)S(1)}, f32[2,2560,256]{2,1,0:T(8,128)}, u32[]{:S(2)}) %copy-start.2) | copy-done | bytes 5242904
  51.1 4.1 %shard_map.116 = (bf16[8,128,128]{2,1,0:T(8,128)(2,1)S(1)}, f32[8,128,128]{2,1,0:T(8,128)S(1)}, f32[8,128,128]{2,1,0:T(8,128)S(1)}, bf16[8,256,128]{2,1,0:T(8,128)(2,1)S(1)}, f32[16,128]{1,0:T(8,128)S(1)}) custom-call(s32[1]{0:T(128)} %bitcast.scalar_ref, bf16[8,384,128]{2,1,0:T(8,128)(2,1)S(1)} %maximum_select_fusion.own_ref, ...), custom_call_target="tpu_custom_call" | custom-call | flops 1342177280 | bytes 9478148 | tf_op jit(solution)/shard_map/pallas_call | solution.py:204
  56.0 1.7 %collective-permute-start.7 = (bf16[16,2048]{1,0:T(8,128)(2,1)S(1)}, bf16[16,2048]{1,0:T(8,128)(2,1)S(1)}, u32[]{:S(2)}, u32[]{:S(2)}) collective-permute-start(bf16[16,2048]{1,0:T(8,128)(2,1)S(1)} %fusion.1), channel_id=1, source_target_pairs={{0,4},{4,0},{8,12},{12,8},{16,20},{20,16},{24,28},{28,24},{1,5},{5... | collective-permute-start | bytes 196616 | tf_op jit(solution)/shard_map/ppermute | solution.py:227
  58.2 1.0 %pad_maximum_fusion = bf16[8,400,128]{2,1,0:T(8,128)(2,1)} fusion(bf16[8,16,128]{2,1,0:T(8,128)(2,1)S(1)} %broadcast_in_dim.9, bf16[8,128,128]{2,1,0:T(8,128)(2,1)S(1)} %maximum_select_fusion.3, bf16[8,128,128]{2,1,0:T(8,128)(2,1)S(1)} %get-tuple-element.70, bf16[8,128,128]{2,1,0:T(8,128)(2,1)S(1)} %get-tuple-element.69), kind=kLoop, calls=%fused_computation.4 | loop fusion | flops 3276800 | bytes 1638400 | tf_op jit(solution)/shard_map/concatenate | solution.py:533
  59.1 5.2 %all-to-all-start.2 = ((bf16[8,400,128]{2,1,0:T(8,128)(2,1)}), bf16[8,400,128]{2,1,0:T(8,128)(2,1)S(1)}, u32[]{:S(2)}, u32[]{:S(2)}) async-start(bf16[8,400,128]{2,1,0:T(8,128)(2,1)} %pad_maximum_fusion), calls=%async_computation.2 | async-start | bytes 1638400 | tf_op jit(solution)/shard_map/all_to_all | solution.py:385
  65.0 14.7 %collective-permute-done.8 = bf16[16,2048]{1,0:T(8,128)(2,1)S(1)} collective-permute-done((bf16[16,2048]{1,0:T(8,128)(2,1)S(1)}, bf16[16,2048]{1,0:T(8,128)(2,1)S(1)}, u32[]{:S(2)}, u32[]{:S(2)}) %collective-permute-start.8) | collective-permute-done | bytes 65568 | tf_op jit(solution)/shard_map/ppermute | solution.py:227
  79.7 3.2 %collective-permute-start.9 = (bf16[16,2048]{1,0:T(8,128)(2,1)S(1)}, bf16[16,2048]{1,0:T(8,128)(2,1)S(1)}, u32[]{:S(2)}, u32[]{:S(2)}) collective-permute-start(bf16[16,2048]{1,0:T(8,128)(2,1)S(1)} %add_convert_fusion), channel_id=1, source_target_pairs={{0,16},{4,20},{8,24},{12,28},{16,0},{20,4},{24,8},{28,12},{1,17},{... | collective-permute-start | bytes 196616 | tf_op jit(solution)/shard_map/ppermute | solution.py:227
  82.9 2.9 %collective-permute-done.9 = bf16[16,2048]{1,0:T(8,128)(2,1)S(1)} collective-permute-done((bf16[16,2048]{1,0:T(8,128)(2,1)S(1)}, bf16[16,2048]{1,0:T(8,128)(2,1)S(1)}, u32[]{:S(2)}, u32[]{:S(2)}) %collective-permute-start.9) | collective-permute-done | bytes 65568 | tf_op jit(solution)/shard_map/ppermute | solution.py:227
  86.0 1.7 %shard_map.117 = (bf16[128,1024]{1,0:T(8,128)(2,1)}, bf16[128,1024]{1,0:T(8,128)(2,1)}, bf16[128,1024]{1,0:T(8,128)(2,1)}, f32[16,1024]{1,0:T(8,128)}) custom-call(bf16[8,400,128]{2,1,0:T(8,128)(2,1)S(1)} %all-to-all-done.2.back_ref), custom_call_target="tpu_custom_call" | custom-call | bytes 1638400 | tf_op jit(solution)/shard_map/pallas_call | solution.py:540
  (49 shorter events, 5.0 us)
Async XLA Ops:
  0.6 13.9 %copy-start = (bf16[16,4096]{1,0:T(8,128)(2,1)S(1)}, bf16[16,4096]{1,0:T(8,128)(2,1)}, u32[]{:S(2)}) copy-start(bf16[16,4096]{1,0:T(8,128)(2,1)} %param.13) | copy-start | bytes 393220
  2.8 25.3 %all-to-all-start = ((bf16[8,384,128]{2,1,0:T(8,128)(2,1)}), bf16[8,384,128]{2,1,0:T(8,128)(2,1)S(1)}, u32[]{:S(2)}, u32[]{:S(2)}) async-start(bf16[8,384,128]{2,1,0:T(8,128)(2,1)} %shard_map.110), calls=%async_computation | async-start | bytes 1572864 | tf_op jit(solution)/shard_map/all_to_all | solution.py:385
  10.7 12.8 %collective-permute-start.1 = (bf16[128,2048]{1,0:T(8,128)(2,1)}, bf16[128,2048]{1,0:T(8,128)(2,1)S(1)}, u32[]{:S(2)}, u32[]{:S(2)}) collective-permute-start(bf16[128,2048]{1,0:T(8,128)(2,1)} %param.10), channel_id=1, source_target_pairs={{0,2},{1,0},{2,3},{3,1},{4,6},{5,4},{6,7},{7,5},{8,10},{9,8},{10,1... | collective-permute-start | bytes 1572872 | tf_op jit(solution)/shard_map/ppermute | solution.py:409
  12.1 11.3 %collective-permute-start = (bf16[128,2048]{1,0:T(8,128)(2,1)}, bf16[128,2048]{1,0:T(8,128)(2,1)S(1)}, u32[]{:S(2)}, u32[]{:S(2)}) collective-permute-start(bf16[128,2048]{1,0:T(8,128)(2,1)} %param.10), channel_id=1, source_target_pairs={{0,0},{1,2},{2,1},{3,3},{4,4},{5,6},{6,5},{7,7},{8,8},{9,10},{10,9... | collective-permute-start | bytes 1572872 | tf_op jit(solution)/shard_map/ppermute | solution.py:409
  28.3 2.3 %collective-permute-start.2 = (bf16[8,256,128]{2,1,0:T(8,128)(2,1)S(1)}, bf16[8,256,128]{2,1,0:T(8,128)(2,1)S(1)}, u32[]{:S(2)}, u32[]{:S(2)}) collective-permute-start(bf16[8,256,128]{2,1,0:T(8,128)(2,1)S(1)} %slice.70), channel_id=1, source_target_pairs={{0,1},{1,0},{2,3},{3,2},{4,5},{5,4},{6,7},{7,6},{8,9},{9,8},{10,11... | collective-permute-start | bytes 1572872 | tf_op jit(solution)/shard_map/ppermute | solution.py:392
  28.4 4.4 %collective-permute-start.3 = (bf16[1040,128]{1,0:T(8,128)(2,1)S(1)}, bf16[1040,128]{1,0:T(8,128)(2,1)S(1)}, u32[]{:S(2)}, u32[]{:S(2)}) collective-permute-start(bf16[1040,128]{1,0:T(8,128)(2,1)S(1)} %get-tuple-element.33), channel_id=1, source_target_pairs={{0,1},{1,0},{2,3},{3,2},{4,5},{5,4},{6,7},{7,6},{8,9},{9,8},{10,11... | collective-permute-start | bytes 798728 | tf_op jit(solution)/shard_map/ppermute | solution.py:392
  33.6 13.3 %all-to-all-start.1 = ((bf16[8,160,128]{2,1,0:T(8,128)(2,1)}), bf16[8,160,128]{2,1,0:T(8,128)(2,1)S(1)}, u32[]{:S(2)}, u32[]{:S(2)}) async-start(bf16[8,160,128]{2,1,0:T(8,128)(2,1)} %shard_map.114), calls=%async_computation.1 | async-start | bytes 655360 | tf_op jit(solution)/shard_map/all_to_all | solution.py:385
  40.0 2.3 %copy-start.1 = (f32[2,2560,256]{2,1,0:T(8,128)}, f32[2,2560,256]{2,1,0:T(8,128)S(1)}, u32[]{:S(2)}) copy-start(f32[2,2560,256]{2,1,0:T(8,128)S(1)} %get-tuple-element.42.prob_ref) | copy-start | bytes 15728644
  47.0 8.3 %collective-permute-start.4 = (f32[16,128]{1,0:T(8,128)S(1)}, f32[16,128]{1,0:T(8,128)S(1)}, u32[]{:S(2)}, u32[]{:S(2)}) collective-permute-start(f32[16,128]{1,0:T(8,128)S(1)} %convert_reduce_fusion), channel_id=1, source_target_pairs={{0,2},{2,0},{1,3},{3,1},{4,6},{6,4},{5,7},{7,5},{8,10},{10,8},{9,1... | collective-permute-start | bytes 24584 | tf_op jit(solution)/shard_map/ppermute | solution.py:502
  48.5 7.3 %copy-start.3 = (bf16[128,2048]{1,0:T(8,128)(2,1)S(1)}, bf16[128,2048]{1,0:T(8,128)(2,1)}, u32[]{:S(2)}) copy-start(bf16[128,2048]{1,0:T(8,128)(2,1)} %param.10) | copy-start | bytes 1572868
  48.6 2.5 %copy-start.2 = (f32[2,2560,256]{2,1,0:T(8,128)S(1)}, f32[2,2560,256]{2,1,0:T(8,128)}, u32[]{:S(2)}) copy-start(f32[2,2560,256]{2,1,0:T(8,128)} %copy-done.1) | copy-start | bytes 15728644
  55.2 2.5 %collective-permute-start.6 = (f32[16,128]{1,0:T(8,128)S(1)}, f32[16,128]{1,0:T(8,128)S(1)}, u32[]{:S(2)}, u32[]{:S(2)}) collective-permute-start(f32[16,128]{1,0:T(8,128)S(1)} %get-tuple-element.49), channel_id=1, source_target_pairs={{0,1},{1,0},{2,3},{3,2},{4,5},{5,4},{6,7},{7,6},{8,9},{9,8},{10,11... | collective-permute-start | bytes 24584 | tf_op jit(solution)/shard_map/ppermute | solution.py:392
  55.3 2.5 %collective-permute-start.5 = (bf16[8,256,128]{2,1,0:T(8,128)(2,1)S(1)}, bf16[8,256,128]{2,1,0:T(8,128)(2,1)S(1)}, u32[]{:S(2)}, u32[]{:S(2)}) collective-permute-start(bf16[8,256,128]{2,1,0:T(8,128)(2,1)S(1)} %get-tuple-element.47), channel_id=1, source_target_pairs={{0,1},{1,0},{2,3},{3,2},{4,5},{5,4},{6,7},{7,6},{8,9},{9,8},{10,11... | collective-permute-start | bytes 1572872 | tf_op jit(solution)/shard_map/ppermute | solution.py:392
  56.0 8.3 %collective-permute-start.7 = (bf16[16,2048]{1,0:T(8,128)(2,1)S(1)}, bf16[16,2048]{1,0:T(8,128)(2,1)S(1)}, u32[]{:S(2)}, u32[]{:S(2)}) collective-permute-start(bf16[16,2048]{1,0:T(8,128)(2,1)S(1)} %fusion.1), channel_id=1, source_target_pairs={{0,4},{4,0},{8,12},{12,8},{16,20},{20,16},{24,28},{28,24},{1,5},{5... | collective-permute-start | bytes 196616 | tf_op jit(solution)/shard_map/ppermute | solution.py:227
  59.1 26.8 %all-to-all-start.2 = ((bf16[8,400,128]{2,1,0:T(8,128)(2,1)}), bf16[8,400,128]{2,1,0:T(8,128)(2,1)S(1)}, u32[]{:S(2)}, u32[]{:S(2)}) async-start(bf16[8,400,128]{2,1,0:T(8,128)(2,1)} %pad_maximum_fusion), calls=%async_computation.2 | async-start | bytes 1638400 | tf_op jit(solution)/shard_map/all_to_all | solution.py:385
  64.3 15.4 %collective-permute-start.8 = (bf16[16,2048]{1,0:T(8,128)(2,1)S(1)}, bf16[16,2048]{1,0:T(8,128)(2,1)S(1)}, u32[]{:S(2)}, u32[]{:S(2)}) collective-permute-start(bf16[16,2048]{1,0:T(8,128)(2,1)S(1)} %add_convert_fusion.1), channel_id=1, source_target_pairs={{0,8},{4,12},{8,0},{12,4},{16,24},{20,28},{24,16},{28,20},{1,9},{5... | collective-permute-start | bytes 196616 | tf_op jit(solution)/shard_map/ppermute | solution.py:227
  79.7 6.2 %collective-permute-start.9 = (bf16[16,2048]{1,0:T(8,128)(2,1)S(1)}, bf16[16,2048]{1,0:T(8,128)(2,1)S(1)}, u32[]{:S(2)}, u32[]{:S(2)}) collective-permute-start(bf16[16,2048]{1,0:T(8,128)(2,1)S(1)} %add_convert_fusion), channel_id=1, source_target_pairs={{0,16},{4,20},{8,24},{12,28},{16,0},{20,4},{24,8},{28,12},{1,17},{... | collective-permute-start | bytes 196616 | tf_op jit(solution)/shard_map/ppermute | solution.py:227
  85.9 1.8 %collective-permute-start.10 = (bf16[16,2048]{1,0:T(8,128)(2,1)S(1)}, bf16[16,2048]{1,0:T(8,128)(2,1)S(1)}, u32[]{:S(2)}, u32[]{:S(2)}) collective-permute-start(bf16[16,2048]{1,0:T(8,128)(2,1)S(1)} %convert_add_fusion.1), channel_id=1, source_target_pairs={{0,1},{1,0},{2,3},{3,2},{4,5},{5,4},{6,7},{7,6},{8,9},{9,8},{10,11... | collective-permute-start | bytes 196616 | tf_op jit(solution)/shard_map/ppermute | solution.py:227

commit v2 on v0

--- a/solution.py
+++ b/solution.py
@@ -106,9 +106,9 @@
         attn = dot_nn(values_t[:, : upto * tok], powers.astype(jnp.bfloat16))
         attn = ((attn + total_ref[:, here] * share) * inverse).astype(jnp.bfloat16)
         attn_ref[:, here] = attn
-        mid_ref[:, here] = dot_nn(down_t_ref[...], attn)
         stat_ref[0:1, here] = highest
         stat_ref[1:2, here] = inverse
+    mid_ref[...] = dot_nn(down_t_ref[...], attn_ref[...])
 
 
 def backward_kernel(
@@ -136,7 +136,10 @@
     keys_own_t = rows_of(own_ref, blocks, tok, tok).T
     keys_other_t = rows_of(other_ref, blocks, 0, tok).T
     tiles = blocks // step
-    down_total = jnp.zeros((low_rank, HD), jnp.float32)
+    lora = jnp.concatenate(
+        [dout_ref[block, HD : HD + low_rank, :] for block in range(blocks)], axis=1
+    )
+    down_grad_ref[...] = 2.0 * dot_nt(lora, attn_ref[...])
     for tile in reversed(range(tiles)):
         upto = (tile + 1) * step
         width = upto * tok
@@ -174,16 +177,11 @@
                 total[...] = term
             else:
                 total[0:width] += term
-        for i in range(step):
-            lora = dout_ref[tile * step + i, HD : HD + low_rank, :]
-            attn = attn_ref[:, at + i * tok : at + (i + 1) * tok]
-            down_total += dot_nt(lora, attn)
     shape = (blocks, tok, HD)
     dk_own_ref[...] = (dk_own[...] * SCALE).reshape(shape)
     dv_own_ref[...] = dv_own[...].reshape(shape)
     pair_other_ref[:, 0:tok, :] = (dk_other[...] * SCALE).astype(jnp.bfloat16).reshape(shape)
     pair_other_ref[:, tok : 2 * tok, :] = dv_other[...].astype(jnp.bfloat16).reshape(shape)
-    down_grad_ref[...] = 2.0 * down_total
 
 
 def call_kernel(body, outs, scratch, flops, exps, *operands, declared=None, limit=48):

time: 86.4 us -> 86 us (level)
  no operation moved by 1% of the time
where the time goes in v2:
time: 86 us; the launch traced here: 85.6 us
  waiting for transfers between devices  25.5 us (30%)
  starting transfers between devices  23.9 us (28%)
  blocking collectives  14.3 us (17%)
  Pallas kernels  14 us (16%)
  matrix products  3.68 us (4%)
  other arithmetic  2.27 us (3%)
  between operations  0.89 us (1%)
  local copies, waits for them, and re-layouts  0.88 us (1%)
    ppermute x4, waiting for transfers between devices, butterfly_sum(): taken = lax.ppermute(value, axis, pairs)  17.6 us
    all_to_all x1, blocking collectives, exchange(): lax.all_to_all(parts, ('seq', 'head'), 0, 0, axis_index_groups=groups, ti...  14.3 us
    all_to_all x2, starting transfers between devices, exchange(): lax.all_to_all(parts, ('seq', 'head'), 0, 0, axis_index_groups=groups, ti...  13 us
    pallas_call x4, Pallas kernels, call_kernel(): pl.pallas_call(body, out_shape=outs, in_specs=specs, out_specs=[pl.BlockS...  10.7 us
    ppermute x2, waiting for transfers between devices, on_device(): pieces.append(lax.ppermute(output_gradient, ('head', 'sub'), pairs))  7.72 us
    ppermute x4, starting transfers between devices, butterfly_sum(): taken = lax.ppermute(value, axis, pairs)  4.56 us
    dot_general x2, matrix products, dot_nn(): return jnp.dot(left, right, preferred_element_type=jnp.float32)  3.68 us
    ppermute x2, starting transfers between devices, on_device(): pieces.append(lax.ppermute(output_gradient, ('head', 'sub'), pairs))  3.42 us
  transfers between devices with their start and end apart: 13, of which 5 were waited for; matrix products, arithmetic and copies ran while one was open for 7% of the time, Pallas kernels for 14%

profile of v2, /device:TPU:0, one launch (start us, length us, event | category | flops | bytes accessed | tf_op | source)
XLA Modules:
  0.0 85.6 jit_solution(17985702581728211884)
XLA Ops:
  0.6 2.1 %shard_map.110 = bf16[8,384,128]{2,1,0:T(8,128)(2,1)} custom-call(bf16[128,1024]{1,0:T(8,128)(2,1)} %refs_0_.1, bf16[128,1024]{1,0:T(8,128)(2,1)} %refs_1_.1, bf16[128,1024]{1,0:T(8,128)(2,1)} %refs_2_.1), custom_call_target="tpu_custom_call" | custom-call | bytes 1572864 | tf_op jit(solution)/shard_map/pallas_call | solution.py:251
  2.8 7.9 %all-to-all-start = ((bf16[8,384,128]{2,1,0:T(8,128)(2,1)}), bf16[8,384,128]{2,1,0:T(8,128)(2,1)S(1)}, u32[]{:S(2)}, u32[]{:S(2)}) async-start(bf16[8,384,128]{2,1,0:T(8,128)(2,1)} %shard_map.110), calls=%async_computation | async-start | bytes 1572864 | tf_op jit(solution)/shard_map/all_to_all | solution.py:366
  10.6 1.7 %collective-permute-start = (bf16[128,2048]{1,0:T(8,128)(2,1)}, bf16[128,2048]{1,0:T(8,128)(2,1)S(1)}, u32[]{:S(2)}, u32[]{:S(2)}) collective-permute-start(bf16[128,2048]{1,0:T(8,128)(2,1)} %param.10), channel_id=1, source_target_pairs={{0,0},{1,2},{2,1},{3,3},{4,4},{5,6},{6,5},{7,7},{8,8},{9,10},{10,9... | collective-permute-start | bytes 1572872 | tf_op jit(solution)/shard_map/ppermute | solution.py:390
  12.3 1.7 %collective-permute-start.1 = (bf16[128,2048]{1,0:T(8,128)(2,1)}, bf16[128,2048]{1,0:T(8,128)(2,1)S(1)}, u32[]{:S(2)}, u32[]{:S(2)}) collective-permute-start(bf16[128,2048]{1,0:T(8,128)(2,1)} %param.10), channel_id=1, source_target_pairs={{0,2},{1,0},{2,3},{3,1},{4,6},{5,4},{6,7},{7,5},{8,10},{9,8},{10,1... | collective-permute-start | bytes 1572872 | tf_op jit(solution)/shard_map/ppermute | solution.py:390
  14.0 0.7 dynamic-slice_bitcast_fusion.down_t_ref
  14.8 3.5 %fusion.refs_2_ = bf16[1024,2048]{1,0:T(8,128)(2,1)S(1)} fusion(bf16[1024,2048]{1,0:T(8,128)(2,1)} %param.11, bf16[16,2048]{1,0:T(8,128)(2,1)S(1)} %constant_dynamic-slice_fusion.refs_3_, bf16[1024,16]{0,1:T(8,128)(2,1)} %param.12), kind=kOutput, calls=%fused_computation.1 | convolution fusion | flops 75497472 | bytes 8486912 | tf_op jit(solution)/shard_map/dot_general | solution.py:26
  18.3 7.7 %collective-permute-done.1.refs_1_ = bf16[128,2048]{1,0:T(8,128)(2,1)S(1)} collective-permute-done((bf16[128,2048]{1,0:T(8,128)(2,1)}, bf16[128,2048]{1,0:T(8,128)(2,1)S(1)}, u32[]{:S(2)}, u32[]{:S(2)}) %collective-permute-start.1) | collective-permute-done | bytes 524320 | tf_op jit(solution)/shard_map/ppermute | solution.py:390
  26.1 2.1 %shard_map.111 = (f32[1040,128]{1,0:T(8,128)S(1)}, bf16[1040,128]{1,0:T(8,128)(2,1)S(1)}) custom-call(s32[4]{0:T(128)S(1)} %pad_add_fusion.plan_ref, bf16[128,2048]{1,0:T(8,128)(2,1)S(1)} %collective-permute-done.refs_0_, bf16[128,2048]{1,0:T(8,128)(2,1)S(1)} %collective-permute-done.1.refs_1_, bf16[1024,2048]{1,0:T(8,128)(2,1)S(1)} %fusion.refs_2_, ...), custom_call_target="tpu_custom_call" | custom-call | bytes 1024 | tf_op jit(solution)/shard_map/pallas_call | solution.py:192
  28.4 0.8 collective-permute-start.2
  29.3 1.7 %shard_map.112 = (f32[128,1024]{1,0:T(8,128)S(1)}, f32[8,1024]{1,0:T(8,128)S(1)}) custom-call(s32[1]{0:T(128)} %bitcast.scalar_ref, bf16[8,384,128]{2,1,0:T(8,128)(2,1)S(1)} %maximum_select_fusion.own_ref), custom_call_target="tpu_custom_call" | custom-call | flops 335544320 | bytes 1343492 | tf_op jit(solution)/shard_map/pallas_call | solution.py:192
  31.0 2.1 %shard_map.113 = (bf16[128,1024]{1,0:T(8,128)(2,1)S(1)}, f32[16,1024]{1,0:T(8,128)S(1)}, f32[8,1024]{1,0:T(8,128)S(1)}) custom-call(s32[1]{0:T(128)} %bitcast.scalar_ref, bf16[8,384,128]{2,1,0:T(8,128)(2,1)S(1)} %maximum_select_fusion.own_ref, bf16[8,256,128]{2,1,0:T(8,128)(2,1)S(1)} %collective-permute-done.2.other_ref, ...), custom_call_target="tpu_custom_call" | custom-call | flops 335544320 | bytes 2232324 | tf_op jit(solution)/shard_map/pallas_call | solution.py:192
  33.3 14.3 %all_to_all.15 = bf16[8,160,128]{2,1,0:T(8,128)(2,1)S(1)} all-to-all(bf16[8,160,128]{2,1,0:T(8,128)(2,1)S(1)} %shard_map.114), channel_id=1, replica_groups={{16,20,24,28,0,4,8,12},{18,22,26,30,2,6,10,14},{17,21,25,29,1,5,9,13},{..., dimensions={0} | all-to-all | bytes 655360 | tf_op jit(solution)/shard_map/all_to_all | solution.py:366
  47.7 1.5 %collective-permute-start.4 = (f32[16,128]{1,0:T(8,128)S(1)}, f32[16,128]{1,0:T(8,128)S(1)}, u32[]{:S(2)}, u32[]{:S(2)}) collective-permute-start(f32[16,128]{1,0:T(8,128)S(1)} %convert_reduce_fusion), channel_id=1, source_target_pairs={{0,2},{2,0},{1,3},{3,1},{4,6},{6,4},{5,7},{7,5},{8,10},{10,8},{9,1... | collective-permute-start | bytes 24584 | tf_op jit(solution)/shard_map/ppermute | solution.py:467
  49.2 4.8 %shard_map.115 = (bf16[8,128,128]{2,1,0:T(8,128)(2,1)S(1)}, f32[8,128,128]{2,1,0:T(8,128)S(1)}, f32[8,128,128]{2,1,0:T(8,128)S(1)}, bf16[8,256,128]{2,1,0:T(8,128)(2,1)S(1)}, f32[16,128]{1,0:T(8,128)S(1)}) custom-call(s32[1]{0:T(128)} %bitcast.scalar_ref, bf16[8,384,128]{2,1,0:T(8,128)(2,1)S(1)} %maximum_select_fusion.own_ref, ...), custom_call_target="tpu_custom_call" | custom-call | flops 1677721600 | bytes 3743748 | tf_op jit(solution)/shard_map/pallas_call | solution.py:192
  54.1 0.6 collective-permute-start.6
  54.8 0.9 %collective-permute-start.7 = (bf16[16,2048]{1,0:T(8,128)(2,1)S(1)}, bf16[16,2048]{1,0:T(8,128)(2,1)S(1)}, u32[]{:S(2)}, u32[]{:S(2)}) collective-permute-start(bf16[16,2048]{1,0:T(8,128)(2,1)S(1)} %fusion.1), channel_id=1, source_target_pairs={{0,4},{4,0},{8,12},{12,8},{16,20},{20,16},{24,28},{28,24},{1,5},{5... | collective-permute-start | bytes 196616 | tf_op jit(solution)/shard_map/ppermute | solution.py:215
  56.4 1.0 %pad_maximum_fusion = bf16[8,400,128]{2,1,0:T(8,128)(2,1)} fusion(bf16[8,16,128]{2,1,0:T(8,128)(2,1)S(1)} %broadcast_in_dim.9, bf16[8,128,128]{2,1,0:T(8,128)(2,1)S(1)} %maximum_select_fusion.3, bf16[8,128,128]{2,1,0:T(8,128)(2,1)S(1)} %get-tuple-element.66, bf16[8,128,128]{2,1,0:T(8,128)(2,1)S(1)} %get-tuple-element.65), kind=kLoop, calls=%fused_computation.4 | loop fusion | flops 3276800 | bytes 1638400 | tf_op jit(solution)/shard_map/concatenate | solution.py:497
  57.3 5.1 %all-to-all-start.2 = ((bf16[8,400,128]{2,1,0:T(8,128)(2,1)}), bf16[8,400,128]{2,1,0:T(8,128)(2,1)S(1)}, u32[]{:S(2)}, u32[]{:S(2)}) async-start(bf16[8,400,128]{2,1,0:T(8,128)(2,1)} %pad_maximum_fusion), calls=%async_computation.2 | async-start | bytes 1638400 | tf_op jit(solution)/shard_map/all_to_all | solution.py:366
  62.5 0.6 collective-permute-start.8
  63.1 14.4 %collective-permute-done.8 = bf16[16,2048]{1,0:T(8,128)(2,1)S(1)} collective-permute-done((bf16[16,2048]{1,0:T(8,128)(2,1)S(1)}, bf16[16,2048]{1,0:T(8,128)(2,1)S(1)}, u32[]{:S(2)}, u32[]{:S(2)}) %collective-permute-start.8) | collective-permute-done | bytes 65568 | tf_op jit(solution)/shard_map/ppermute | solution.py:215
  77.6 3.0 %collective-permute-start.9 = (bf16[16,2048]{1,0:T(8,128)(2,1)S(1)}, bf16[16,2048]{1,0:T(8,128)(2,1)S(1)}, u32[]{:S(2)}, u32[]{:S(2)}) collective-permute-start(bf16[16,2048]{1,0:T(8,128)(2,1)S(1)} %add_convert_fusion), channel_id=1, source_target_pairs={{0,16},{4,20},{8,24},{12,28},{16,0},{20,4},{24,8},{28,12},{1,17},{... | collective-permute-start | bytes 196616 | tf_op jit(solution)/shard_map/ppermute | solution.py:215
  80.5 3.0 %collective-permute-done.9 = bf16[16,2048]{1,0:T(8,128)(2,1)S(1)} collective-permute-done((bf16[16,2048]{1,0:T(8,128)(2,1)S(1)}, bf16[16,2048]{1,0:T(8,128)(2,1)S(1)}, u32[]{:S(2)}, u32[]{:S(2)}) %collective-permute-start.9) | collective-permute-done | bytes 65568 | tf_op jit(solution)/shard_map/ppermute | solution.py:215
  83.6 1.1 %shard_map.116 = (bf16[128,1024]{1,0:T(8,128)(2,1)}, bf16[128,1024]{1,0:T(8,128)(2,1)}, bf16[128,1024]{1,0:T(8,128)(2,1)}, f32[16,1024]{1,0:T(8,128)}) custom-call(bf16[8,400,128]{2,1,0:T(8,128)(2,1)S(1)} %all-to-all-done.2.back_ref), custom_call_target="tpu_custom_call" | custom-call | bytes 1671168 | tf_op jit(solution)/shard_map/pallas_call | solution.py:279
  84.9 0.7 convert_add_fusion
  (43 shorter events, 1.7 us)
Async XLA Ops:
  0.6 14.1 %copy-start = (bf16[16,4096]{1,0:T(8,128)(2,1)S(1)}, bf16[16,4096]{1,0:T(8,128)(2,1)}, u32[]{:S(2)}) copy-start(bf16[16,4096]{1,0:T(8,128)(2,1)} %param.13) | copy-start | bytes 393220
  2.8 25.4 %all-to-all-start = ((bf16[8,384,128]{2,1,0:T(8,128)(2,1)}), bf16[8,384,128]{2,1,0:T(8,128)(2,1)S(1)}, u32[]{:S(2)}, u32[]{:S(2)}) async-start(bf16[8,384,128]{2,1,0:T(8,128)(2,1)} %shard_map.110), calls=%async_computation | async-start | bytes 1572864 | tf_op jit(solution)/shard_map/all_to_all | solution.py:366
  10.6 7.7 %collective-permute-start = (bf16[128,2048]{1,0:T(8,128)(2,1)}, bf16[128,2048]{1,0:T(8,128)(2,1)S(1)}, u32[]{:S(2)}, u32[]{:S(2)}) collective-permute-start(bf16[128,2048]{1,0:T(8,128)(2,1)} %param.10), channel_id=1, source_target_pairs={{0,0},{1,2},{2,1},{3,3},{4,4},{5,6},{6,5},{7,7},{8,8},{9,10},{10,9... | collective-permute-start | bytes 1572872 | tf_op jit(solution)/shard_map/ppermute | solution.py:390
  12.3 13.7 %collective-permute-start.1 = (bf16[128,2048]{1,0:T(8,128)(2,1)}, bf16[128,2048]{1,0:T(8,128)(2,1)S(1)}, u32[]{:S(2)}, u32[]{:S(2)}) collective-permute-start(bf16[128,2048]{1,0:T(8,128)(2,1)} %param.10), channel_id=1, source_target_pairs={{0,2},{1,0},{2,3},{3,1},{4,6},{5,4},{6,7},{7,5},{8,10},{9,8},{10,1... | collective-permute-start | bytes 1572872 | tf_op jit(solution)/shard_map/ppermute | solution.py:390
  28.4 2.6 %collective-permute-start.2 = (bf16[8,256,128]{2,1,0:T(8,128)(2,1)S(1)}, bf16[8,256,128]{2,1,0:T(8,128)(2,1)S(1)}, u32[]{:S(2)}, u32[]{:S(2)}) collective-permute-start(bf16[8,256,128]{2,1,0:T(8,128)(2,1)S(1)} %slice.70), channel_id=1, source_target_pairs={{0,1},{1,0},{2,3},{3,2},{4,5},{5,4},{6,7},{7,6},{8,9},{9,8},{10,11... | collective-permute-start | bytes 1572872 | tf_op jit(solution)/shard_map/ppermute | solution.py:373
  29.2 4.0 %collective-permute-start.3 = (bf16[1040,128]{1,0:T(8,128)(2,1)S(1)}, bf16[1040,128]{1,0:T(8,128)(2,1)S(1)}, u32[]{:S(2)}, u32[]{:S(2)}) collective-permute-start(bf16[1040,128]{1,0:T(8,128)(2,1)S(1)} %get-tuple-element.31), channel_id=1, source_target_pairs={{0,1},{1,0},{2,3},{3,2},{4,5},{5,4},{6,7},{7,6},{8,9},{9,8},{10,11... | collective-permute-start | bytes 798728 | tf_op jit(solution)/shard_map/ppermute | solution.py:373
  47.6 7.0 %copy-start.1 = (bf16[128,2048]{1,0:T(8,128)(2,1)S(1)}, bf16[128,2048]{1,0:T(8,128)(2,1)}, u32[]{:S(2)}) copy-start(bf16[128,2048]{1,0:T(8,128)(2,1)} %param.10) | copy-start | bytes 1572868
  47.7 6.3 %collective-permute-start.4 = (f32[16,128]{1,0:T(8,128)S(1)}, f32[16,128]{1,0:T(8,128)S(1)}, u32[]{:S(2)}, u32[]{:S(2)}) collective-permute-start(f32[16,128]{1,0:T(8,128)S(1)} %convert_reduce_fusion), channel_id=1, source_target_pairs={{0,2},{2,0},{1,3},{3,1},{4,6},{6,4},{5,7},{7,5},{8,10},{10,8},{9,1... | collective-permute-start | bytes 24584 | tf_op jit(solution)/shard_map/ppermute | solution.py:467
  54.0 2.0 %collective-permute-start.5 = (bf16[8,256,128]{2,1,0:T(8,128)(2,1)S(1)}, bf16[8,256,128]{2,1,0:T(8,128)(2,1)S(1)}, u32[]{:S(2)}, u32[]{:S(2)}) collective-permute-start(bf16[8,256,128]{2,1,0:T(8,128)(2,1)S(1)} %get-tuple-element.43), channel_id=1, source_target_pairs={{0,1},{1,0},{2,3},{3,2},{4,5},{5,4},{6,7},{7,6},{8,9},{9,8},{10,11... | collective-permute-start | bytes 1572872 | tf_op jit(solution)/shard_map/ppermute | solution.py:373
  54.1 1.9 %collective-permute-start.6 = (f32[16,128]{1,0:T(8,128)S(1)}, f32[16,128]{1,0:T(8,128)S(1)}, u32[]{:S(2)}, u32[]{:S(2)}) collective-permute-start(f32[16,128]{1,0:T(8,128)S(1)} %get-tuple-element.45), channel_id=1, source_target_pairs={{0,1},{1,0},{2,3},{3,2},{4,5},{5,4},{6,7},{7,6},{8,9},{9,8},{10,11... | collective-permute-start | bytes 24584 | tf_op jit(solution)/shard_map/ppermute | solution.py:373
  54.8 7.6 %collective-permute-start.7 = (bf16[16,2048]{1,0:T(8,128)(2,1)S(1)}, bf16[16,2048]{1,0:T(8,128)(2,1)S(1)}, u32[]{:S(2)}, u32[]{:S(2)}) collective-permute-start(bf16[16,2048]{1,0:T(8,128)(2,1)S(1)} %fusion.1), channel_id=1, source_target_pairs={{0,4},{4,0},{8,12},{12,8},{16,20},{20,16},{24,28},{28,24},{1,5},{5... | collective-permute-start | bytes 196616 | tf_op jit(solution)/shard_map/ppermute | solution.py:215
  57.3 26.2 %all-to-all-start.2 = ((bf16[8,400,128]{2,1,0:T(8,128)(2,1)}), bf16[8,400,128]{2,1,0:T(8,128)(2,1)S(1)}, u32[]{:S(2)}, u32[]{:S(2)}) async-start(bf16[8,400,128]{2,1,0:T(8,128)(2,1)} %pad_maximum_fusion), calls=%async_computation.2 | async-start | bytes 1638400 | tf_op jit(solution)/shard_map/all_to_all | solution.py:366
  62.5 15.1 %collective-permute-start.8 = (bf16[16,2048]{1,0:T(8,128)(2,1)S(1)}, bf16[16,2048]{1,0:T(8,128)(2,1)S(1)}, u32[]{:S(2)}, u32[]{:S(2)}) collective-permute-start(bf16[16,2048]{1,0:T(8,128)(2,1)S(1)} %add_convert_fusion.1), channel_id=1, source_target_pairs={{0,8},{4,12},{8,0},{12,4},{16,24},{20,28},{24,16},{28,20},{1,9},{5... | collective-permute-start | bytes 196616 | tf_op jit(solution)/shard_map/ppermute | solution.py:215
  77.6 5.9 %collective-permute-start.9 = (bf16[16,2048]{1,0:T(8,128)(2,1)S(1)}, bf16[16,2048]{1,0:T(8,128)(2,1)S(1)}, u32[]{:S(2)}, u32[]{:S(2)}) collective-permute-start(bf16[16,2048]{1,0:T(8,128)(2,1)S(1)} %add_convert_fusion), channel_id=1, source_target_pairs={{0,16},{4,20},{8,24},{12,28},{16,0},{20,4},{24,8},{28,12},{1,17},{... | collective-permute-start | bytes 196616 | tf_op jit(solution)/shard_map/ppermute | solution.py:215
  83.6 1.3 %collective-permute-start.10 = (bf16[16,2048]{1,0:T(8,128)(2,1)S(1)}, bf16[16,2048]{1,0:T(8,128)(2,1)S(1)}, u32[]{:S(2)}, u32[]{:S(2)}) collective-permute-start(bf16[16,2048]{1,0:T(8,128)(2,1)S(1)} %convert_add_fusion.1), channel_id=1, source_target_pairs={{0,1},{1,0},{2,3},{3,2},{4,5},{5,4},{6,7},{7,6},{8,9},{9,8},{10,11... | collective-permute-start | bytes 196616 | tf_op jit(solution)/shard_map/ppermute | solution.py:215

commit v3 on v2

--- a/solution.py
+++ b/solution.py
@@ -19,6 +19,12 @@
 def dot_nt(left, right):
     return lax.dot_general(
         left, right, (((1,), (1,)), ((), ())), preferred_element_type=jnp.float32
+    )
+
+
+def dot_tn(left, right):
+    return lax.dot_general(
+        left, right, (((0,), (0,)), ((), ())), preferred_element_type=jnp.float32
     )
 
 
@@ -133,8 +139,6 @@
     step = TILE // tok
     sub = scalar_ref[0]
     low_rank = down_grad_ref.shape[0]
-    keys_own_t = rows_of(own_ref, blocks, tok, tok).T
-    keys_other_t = rows_of(other_ref, blocks, 0, tok).T
     tiles = blocks // step
     lora = jnp.concatenate(
         [dout_ref[block, HD : HD + low_rank, :] for block in range(blocks)], axis=1
@@ -150,10 +154,10 @@
         )
         highest = stat_ref[0:1, at : at + TILE]
         inverse = stat_ref[1:2, at : at + TILE]
-        own = scores_of(rows_of(own_ref, upto, tok, tok), queries, own_visible())
-        other = scores_of(
-            rows_of(other_ref, upto, 0, tok), queries, other_visible(sub, tok)
-        )
+        keys_own = rows_of(own_ref, upto, tok, tok)
+        keys_other = rows_of(other_ref, upto, 0, tok)
+        own = scores_of(keys_own, queries, own_visible())
+        other = scores_of(keys_other, queries, other_visible(sub, tok))
         own = jnp.exp2((own - highest) * LOG2_SCALE) * inverse
         other = jnp.exp2((other - highest) * LOG2_SCALE) * inverse
         dprob_own = dot_nn(rows_of(own_ref, upto, 2 * tok, tok), douts_t)
@@ -163,8 +167,8 @@
         )
         ds_own = (own * (dprob_own - delta)).astype(jnp.bfloat16)
         ds_other = (other * (dprob_other - delta)).astype(jnp.bfloat16)
-        dq = dot_nn(keys_own_t[:, :width], ds_own) + dot_nn(keys_other_t[:, :width], ds_other)
-        dq = (dq * SCALE).T.astype(jnp.bfloat16)
+        dq = dot_tn(ds_own, keys_own) + dot_tn(ds_other, keys_other)
+        dq = (dq * SCALE).astype(jnp.bfloat16)
         dq_ref[tile * step : upto] = dq.reshape(step, tok, HD)
         terms = (
             (dk_own, dot_nn(ds_own, queries)),
@@ -226,19 +230,23 @@
     operands, message_ref = refs[:count], refs[count]
     held, in_sems, out_sems = refs[count + 1 : -2], refs[-2], refs[-1]
     tok = operands[0].shape[0]
+    halves = [pl.ds(0, tok // 2), pl.ds(tok // 2, tok // 2)]
     arriving = [
-        pltpu.make_async_copy(ref, to, in_sems.at[n])
+        pltpu.make_async_copy(ref.at[half], to.at[half], in_sems.at[n, i])
         for n, (ref, to) in enumerate(zip(operands, held))
+        for i, half in enumerate(halves)
     ]
     for copy in arriving:
         copy.start()
     leaving = []
-    for n, (copy, ref) in enumerate(zip(arriving, held)):
+    for at, copy in enumerate(arriving):
         copy.wait()
+        n, i = divmod(at, 2)
         for rank in range(message_ref.shape[0]):
             cols = pl.ds((rank // copies) * HD, HD)
-            to = message_ref.at[rank, pl.ds(n * tok, tok), :]
-            leaving.append(pltpu.make_async_copy(ref.at[:, cols], to, out_sems.at[len(leaving)]))
+            to = message_ref.at[rank, pl.ds(n * tok + i * (tok // 2), tok // 2), :]
+            block = held[n].at[halves[i], cols]
+            leaving.append(pltpu.make_async_copy(block, to, out_sems.at[len(leaving)]))
             leaving[-1].start()
     for copy in leaving:
         copy.wait()
@@ -254,7 +262,7 @@
         in_specs=[pl.BlockSpec(memory_space=pltpu.HBM)] * count,
         out_specs=pl.BlockSpec(memory_space=pltpu.HBM),
         scratch_shapes=[pltpu.VMEM(x.shape, x.dtype) for x in operands]
-        + [pltpu.SemaphoreType.DMA((count,)), pltpu.SemaphoreType.DMA((ranks * count,))],
+        + [pltpu.SemaphoreType.DMA((count, 2)), pltpu.SemaphoreType.DMA((2 * ranks * count,))],
         cost_estimate=pl.CostEstimate(
             flops=0, bytes_accessed=4 * math.prod(shape), transcendentals=0
         ),

time: 86 us -> 86.5 us (level)
  no operation moved by 1% of the time
where the time goes in v3:
time: 86.5 us; the launch traced here: 86 us
  waiting for transfers between devices  25.5 us (29%)
  starting transfers between devices  23.9 us (28%)
  Pallas kernels  14.5 us (17%)
  blocking collectives  14.3 us (17%)
  matrix products  3.68 us (4%)
  other arithmetic  2.27 us (3%)
  local copies, waits for them, and re-layouts  0.88 us (1%)
  between operations  0.88 us (1%)
    ppermute x4, waiting for transfers between devices, butterfly_sum(): taken = lax.ppermute(value, axis, pairs)  17.6 us
    all_to_all x1, blocking collectives, exchange(): lax.all_to_all(parts, ('seq', 'head'), 0, 0, axis_index_groups=groups, ti...  14.3 us
    all_to_all x2, starting transfers between devices, exchange(): lax.all_to_all(parts, ('seq', 'head'), 0, 0, axis_index_groups=groups, ti...  13 us
    pallas_call x4, Pallas kernels, call_kernel(): pl.pallas_call(body, out_shape=outs, in_specs=specs, out_specs=[pl.BlockS...  10.9 us
    ppermute x2, waiting for transfers between devices, on_device(): pieces.append(lax.ppermute(output_gradient, ('head', 'sub'), pairs))  7.71 us
    ppermute x4, starting transfers between devices, butterfly_sum(): taken = lax.ppermute(value, axis, pairs)  4.56 us
    dot_general x2, matrix products, dot_nn(): return jnp.dot(left, right, preferred_element_type=jnp.float32)  3.68 us
    ppermute x2, starting transfers between devices, on_device(): pieces.append(lax.ppermute(output_gradient, ('head', 'sub'), pairs))  3.42 us
  transfers between devices with their start and end apart: 13, of which 5 were waited for; matrix products, arithmetic and copies ran while one was open for 7% of the time, Pallas kernels for 14%

profile of v3, /device:TPU:0, one launch (start us, length us, event | category | flops | bytes accessed | tf_op | source)
XLA Modules:
  0.0 86.0 jit_solution(13799621107237058995)
XLA Ops:
  0.6 2.4 %shard_map.110 = bf16[8,384,128]{2,1,0:T(8,128)(2,1)} custom-call(bf16[128,1024]{1,0:T(8,128)(2,1)} %refs_0_.1, bf16[128,1024]{1,0:T(8,128)(2,1)} %refs_1_.1, bf16[128,1024]{1,0:T(8,128)(2,1)} %refs_2_.1), custom_call_target="tpu_custom_call" | custom-call | bytes 1572864 | tf_op jit(solution)/shard_map/pallas_call | solution.py:259
  3.0 7.9 %all-to-all-start = ((bf16[8,384,128]{2,1,0:T(8,128)(2,1)}), bf16[8,384,128]{2,1,0:T(8,128)(2,1)S(1)}, u32[]{:S(2)}, u32[]{:S(2)}) async-start(bf16[8,384,128]{2,1,0:T(8,128)(2,1)} %shard_map.110), calls=%async_computation | async-start | bytes 1572864 | tf_op jit(solution)/shard_map/all_to_all | solution.py:374
  10.9 1.7 %collective-permute-start = (bf16[128,2048]{1,0:T(8,128)(2,1)}, bf16[128,2048]{1,0:T(8,128)(2,1)S(1)}, u32[]{:S(2)}, u32[]{:S(2)}) collective-permute-start(bf16[128,2048]{1,0:T(8,128)(2,1)} %param.10), channel_id=1, source_target_pairs={{0,0},{1,2},{2,1},{3,3},{4,4},{5,6},{6,5},{7,7},{8,8},{9,10},{10,9... | collective-permute-start | bytes 1572872 | tf_op jit(solution)/shard_map/ppermute | solution.py:398
  12.6 1.7 %collective-permute-start.1 = (bf16[128,2048]{1,0:T(8,128)(2,1)}, bf16[128,2048]{1,0:T(8,128)(2,1)S(1)}, u32[]{:S(2)}, u32[]{:S(2)}) collective-permute-start(bf16[128,2048]{1,0:T(8,128)(2,1)} %param.10), channel_id=1, source_target_pairs={{0,2},{1,0},{2,3},{3,1},{4,6},{5,4},{6,7},{7,5},{8,10},{9,8},{10,1... | collective-permute-start | bytes 1572872 | tf_op jit(solution)/shard_map/ppermute | solution.py:398
  14.3 0.7 dynamic-slice_bitcast_fusion.down_t_ref
  15.1 3.5 %fusion.refs_2_ = bf16[1024,2048]{1,0:T(8,128)(2,1)S(1)} fusion(bf16[1024,2048]{1,0:T(8,128)(2,1)} %param.11, bf16[16,2048]{1,0:T(8,128)(2,1)S(1)} %constant_dynamic-slice_fusion.refs_3_, bf16[1024,16]{0,1:T(8,128)(2,1)} %param.12), kind=kOutput, calls=%fused_computation.1 | convolution fusion | flops 75497472 | bytes 8486912 | tf_op jit(solution)/shard_map/dot_general | solution.py:32
  18.6 7.7 %collective-permute-done.1.refs_1_ = bf16[128,2048]{1,0:T(8,128)(2,1)S(1)} collective-permute-done((bf16[128,2048]{1,0:T(8,128)(2,1)}, bf16[128,2048]{1,0:T(8,128)(2,1)S(1)}, u32[]{:S(2)}, u32[]{:S(2)}) %collective-permute-start.1) | collective-permute-done | bytes 524320 | tf_op jit(solution)/shard_map/ppermute | solution.py:398
  26.3 2.1 %shard_map.111 = (f32[1040,128]{1,0:T(8,128)S(1)}, bf16[1040,128]{1,0:T(8,128)(2,1)S(1)}) custom-call(s32[4]{0:T(128)S(1)} %pad_add_fusion.plan_ref, bf16[128,2048]{1,0:T(8,128)(2,1)S(1)} %collective-permute-done.refs_0_, bf16[128,2048]{1,0:T(8,128)(2,1)S(1)} %collective-permute-done.1.refs_1_, bf16[1024,2048]{1,0:T(8,128)(2,1)S(1)} %fusion.refs_2_, ...), custom_call_target="tpu_custom_call" | custom-call | bytes 1024 | tf_op jit(solution)/shard_map/pallas_call | solution.py:196
  28.6 0.8 collective-permute-start.2
  29.6 1.7 %shard_map.112 = (f32[128,1024]{1,0:T(8,128)S(1)}, f32[8,1024]{1,0:T(8,128)S(1)}) custom-call(s32[1]{0:T(128)} %bitcast.scalar_ref, bf16[8,384,128]{2,1,0:T(8,128)(2,1)S(1)} %maximum_select_fusion.own_ref), custom_call_target="tpu_custom_call" | custom-call | flops 335544320 | bytes 1343492 | tf_op jit(solution)/shard_map/pallas_call | solution.py:196
  31.3 2.1 %shard_map.113 = (bf16[128,1024]{1,0:T(8,128)(2,1)S(1)}, f32[16,1024]{1,0:T(8,128)S(1)}, f32[8,1024]{1,0:T(8,128)S(1)}) custom-call(s32[1]{0:T(128)} %bitcast.scalar_ref, bf16[8,384,128]{2,1,0:T(8,128)(2,1)S(1)} %maximum_select_fusion.own_ref, bf16[8,256,128]{2,1,0:T(8,128)(2,1)S(1)} %collective-permute-done.2.other_ref, ...), custom_call_target="tpu_custom_call" | custom-call | flops 335544320 | bytes 2232324 | tf_op jit(solution)/shard_map/pallas_call | solution.py:196
  33.6 14.3 %all_to_all.15 = bf16[8,160,128]{2,1,0:T(8,128)(2,1)S(1)} all-to-all(bf16[8,160,128]{2,1,0:T(8,128)(2,1)S(1)} %shard_map.114), channel_id=1, replica_groups={{16,20,24,28,0,4,8,12},{18,22,26,30,2,6,10,14},{17,21,25,29,1,5,9,13},{..., dimensions={0} | all-to-all | bytes 655360 | tf_op jit(solution)/shard_map/all_to_all | solution.py:374
  47.9 1.5 %collective-permute-start.4 = (f32[16,128]{1,0:T(8,128)S(1)}, f32[16,128]{1,0:T(8,128)S(1)}, u32[]{:S(2)}, u32[]{:S(2)}) collective-permute-start(f32[16,128]{1,0:T(8,128)S(1)} %convert_reduce_fusion), channel_id=1, source_target_pairs={{0,2},{2,0},{1,3},{3,1},{4,6},{6,4},{5,7},{7,5},{8,10},{10,8},{9,1... | collective-permute-start | bytes 24584 | tf_op jit(solution)/shard_map/ppermute | solution.py:475
  49.5 5.0 %shard_map.115 = (bf16[8,128,128]{2,1,0:T(8,128)(2,1)S(1)}, f32[8,128,128]{2,1,0:T(8,128)S(1)}, f32[8,128,128]{2,1,0:T(8,128)S(1)}, bf16[8,256,128]{2,1,0:T(8,128)(2,1)S(1)}, f32[16,128]{1,0:T(8,128)S(1)}) custom-call(s32[1]{0:T(128)} %bitcast.scalar_ref, bf16[8,384,128]{2,1,0:T(8,128)(2,1)S(1)} %maximum_select_fusion.own_ref, ...), custom_call_target="tpu_custom_call" | custom-call | flops 1677721600 | bytes 3743748 | tf_op jit(solution)/shard_map/pallas_call | solution.py:196
  54.6 0.6 collective-permute-start.6
  55.3 0.9 %collective-permute-start.7 = (bf16[16,2048]{1,0:T(8,128)(2,1)S(1)}, bf16[16,2048]{1,0:T(8,128)(2,1)S(1)}, u32[]{:S(2)}, u32[]{:S(2)}) collective-permute-start(bf16[16,2048]{1,0:T(8,128)(2,1)S(1)} %fusion.1), channel_id=1, source_target_pairs={{0,4},{4,0},{8,12},{12,8},{16,20},{20,16},{24,28},{28,24},{1,5},{5... | collective-permute-start | bytes 196616 | tf_op jit(solution)/shard_map/ppermute | solution.py:219
  56.9 1.0 %pad_maximum_fusion = bf16[8,400,128]{2,1,0:T(8,128)(2,1)} fusion(bf16[8,16,128]{2,1,0:T(8,128)(2,1)S(1)} %broadcast_in_dim.9, bf16[8,128,128]{2,1,0:T(8,128)(2,1)S(1)} %maximum_select_fusion.3, bf16[8,128,128]{2,1,0:T(8,128)(2,1)S(1)} %get-tuple-element.66, bf16[8,128,128]{2,1,0:T(8,128)(2,1)S(1)} %get-tuple-element.65), kind=kLoop, calls=%fused_computation.4 | loop fusion | flops 3276800 | bytes 1638400 | tf_op jit(solution)/shard_map/concatenate | solution.py:505
  57.8 5.1 %all-to-all-start.2 = ((bf16[8,400,128]{2,1,0:T(8,128)(2,1)}), bf16[8,400,128]{2,1,0:T(8,128)(2,1)S(1)}, u32[]{:S(2)}, u32[]{:S(2)}) async-start(bf16[8,400,128]{2,1,0:T(8,128)(2,1)} %pad_maximum_fusion), calls=%async_computation.2 | async-start | bytes 1638400 | tf_op jit(solution)/shard_map/all_to_all | solution.py:374
  63.0 0.6 collective-permute-start.8
  63.6 14.4 %collective-permute-done.8 = bf16[16,2048]{1,0:T(8,128)(2,1)S(1)} collective-permute-done((bf16[16,2048]{1,0:T(8,128)(2,1)S(1)}, bf16[16,2048]{1,0:T(8,128)(2,1)S(1)}, u32[]{:S(2)}, u32[]{:S(2)}) %collective-permute-start.8) | collective-permute-done | bytes 65568 | tf_op jit(solution)/shard_map/ppermute | solution.py:219
  78.1 3.0 %collective-permute-start.9 = (bf16[16,2048]{1,0:T(8,128)(2,1)S(1)}, bf16[16,2048]{1,0:T(8,128)(2,1)S(1)}, u32[]{:S(2)}, u32[]{:S(2)}) collective-permute-start(bf16[16,2048]{1,0:T(8,128)(2,1)S(1)} %add_convert_fusion), channel_id=1, source_target_pairs={{0,16},{4,20},{8,24},{12,28},{16,0},{20,4},{24,8},{28,12},{1,17},{... | collective-permute-start | bytes 196616 | tf_op jit(solution)/shard_map/ppermute | solution.py:219
  81.0 3.0 %collective-permute-done.9 = bf16[16,2048]{1,0:T(8,128)(2,1)S(1)} collective-permute-done((bf16[16,2048]{1,0:T(8,128)(2,1)S(1)}, bf16[16,2048]{1,0:T(8,128)(2,1)S(1)}, u32[]{:S(2)}, u32[]{:S(2)}) %collective-permute-start.9) | collective-permute-done | bytes 65568 | tf_op jit(solution)/shard_map/ppermute | solution.py:219
  84.1 1.1 %shard_map.116 = (bf16[128,1024]{1,0:T(8,128)(2,1)}, bf16[128,1024]{1,0:T(8,128)(2,1)}, bf16[128,1024]{1,0:T(8,128)(2,1)}, f32[16,1024]{1,0:T(8,128)}) custom-call(bf16[8,400,128]{2,1,0:T(8,128)(2,1)S(1)} %all-to-all-done.2.back_ref), custom_call_target="tpu_custom_call" | custom-call | bytes 1671168 | tf_op jit(solution)/shard_map/pallas_call | solution.py:287
  85.4 0.7 convert_add_fusion
  (43 shorter events, 1.7 us)
Async XLA Ops:
  0.6 14.4 %copy-start = (bf16[16,4096]{1,0:T(8,128)(2,1)S(1)}, bf16[16,4096]{1,0:T(8,128)(2,1)}, u32[]{:S(2)}) copy-start(bf16[16,4096]{1,0:T(8,128)(2,1)} %param.13) | copy-start | bytes 393220
  3.0 25.4 %all-to-all-start = ((bf16[8,384,128]{2,1,0:T(8,128)(2,1)}), bf16[8,384,128]{2,1,0:T(8,128)(2,1)S(1)}, u32[]{:S(2)}, u32[]{:S(2)}) async-start(bf16[8,384,128]{2,1,0:T(8,128)(2,1)} %shard_map.110), calls=%async_computation | async-start | bytes 1572864 | tf_op jit(solution)/shard_map/all_to_all | solution.py:374
  10.9 7.7 %collective-permute-start = (bf16[128,2048]{1,0:T(8,128)(2,1)}, bf16[128,2048]{1,0:T(8,128)(2,1)S(1)}, u32[]{:S(2)}, u32[]{:S(2)}) collective-permute-start(bf16[128,2048]{1,0:T(8,128)(2,1)} %param.10), channel_id=1, source_target_pairs={{0,0},{1,2},{2,1},{3,3},{4,4},{5,6},{6,5},{7,7},{8,8},{9,10},{10,9... | collective-permute-start | bytes 1572872 | tf_op jit(solution)/shard_map/ppermute | solution.py:398
  12.6 13.7 %collective-permute-start.1 = (bf16[128,2048]{1,0:T(8,128)(2,1)}, bf16[128,2048]{1,0:T(8,128)(2,1)S(1)}, u32[]{:S(2)}, u32[]{:S(2)}) collective-permute-start(bf16[128,2048]{1,0:T(8,128)(2,1)} %param.10), channel_id=1, source_target_pairs={{0,2},{1,0},{2,3},{3,1},{4,6},{5,4},{6,7},{7,5},{8,10},{9,8},{10,1... | collective-permute-start | bytes 1572872 | tf_op jit(solution)/shard_map/ppermute | solution.py:398
  28.6 2.6 %collective-permute-start.2 = (bf16[8,256,128]{2,1,0:T(8,128)(2,1)S(1)}, bf16[8,256,128]{2,1,0:T(8,128)(2,1)S(1)}, u32[]{:S(2)}, u32[]{:S(2)}) collective-permute-start(bf16[8,256,128]{2,1,0:T(8,128)(2,1)S(1)} %slice.70), channel_id=1, source_target_pairs={{0,1},{1,0},{2,3},{3,2},{4,5},{5,4},{6,7},{7,6},{8,9},{9,8},{10,11... | collective-permute-start | bytes 1572872 | tf_op jit(solution)/shard_map/ppermute | solution.py:381
  29.5 4.0 %collective-permute-start.3 = (bf16[1040,128]{1,0:T(8,128)(2,1)S(1)}, bf16[1040,128]{1,0:T(8,128)(2,1)S(1)}, u32[]{:S(2)}, u32[]{:S(2)}) collective-permute-start(bf16[1040,128]{1,0:T(8,128)(2,1)S(1)} %get-tuple-element.31), channel_id=1, source_target_pairs={{0,1},{1,0},{2,3},{3,2},{4,5},{5,4},{6,7},{7,6},{8,9},{9,8},{10,11... | collective-permute-start | bytes 798728 | tf_op jit(solution)/shard_map/ppermute | solution.py:381
  47.9 7.2 %copy-start.1 = (bf16[128,2048]{1,0:T(8,128)(2,1)S(1)}, bf16[128,2048]{1,0:T(8,128)(2,1)}, u32[]{:S(2)}) copy-start(bf16[128,2048]{1,0:T(8,128)(2,1)} %param.10) | copy-start | bytes 1572868
  47.9 6.5 %collective-permute-start.4 = (f32[16,128]{1,0:T(8,128)S(1)}, f32[16,128]{1,0:T(8,128)S(1)}, u32[]{:S(2)}, u32[]{:S(2)}) collective-permute-start(f32[16,128]{1,0:T(8,128)S(1)} %convert_reduce_fusion), channel_id=1, source_target_pairs={{0,2},{2,0},{1,3},{3,1},{4,6},{6,4},{5,7},{7,5},{8,10},{10,8},{9,1... | collective-permute-start | bytes 24584 | tf_op jit(solution)/shard_map/ppermute | solution.py:475
  54.5 2.0 %collective-permute-start.5 = (bf16[8,256,128]{2,1,0:T(8,128)(2,1)S(1)}, bf16[8,256,128]{2,1,0:T(8,128)(2,1)S(1)}, u32[]{:S(2)}, u32[]{:S(2)}) collective-permute-start(bf16[8,256,128]{2,1,0:T(8,128)(2,1)S(1)} %get-tuple-element.43), channel_id=1, source_target_pairs={{0,1},{1,0},{2,3},{3,2},{4,5},{5,4},{6,7},{7,6},{8,9},{9,8},{10,11... | collective-permute-start | bytes 1572872 | tf_op jit(solution)/shard_map/ppermute | solution.py:381
  54.6 1.9 %collective-permute-start.6 = (f32[16,128]{1,0:T(8,128)S(1)}, f32[16,128]{1,0:T(8,128)S(1)}, u32[]{:S(2)}, u32[]{:S(2)}) collective-permute-start(f32[16,128]{1,0:T(8,128)S(1)} %get-tuple-element.45), channel_id=1, source_target_pairs={{0,1},{1,0},{2,3},{3,2},{4,5},{5,4},{6,7},{7,6},{8,9},{9,8},{10,11... | collective-permute-start | bytes 24584 | tf_op jit(solution)/shard_map/ppermute | solution.py:381
  55.3 7.6 %collective-permute-start.7 = (bf16[16,2048]{1,0:T(8,128)(2,1)S(1)}, bf16[16,2048]{1,0:T(8,128)(2,1)S(1)}, u32[]{:S(2)}, u32[]{:S(2)}) collective-permute-start(bf16[16,2048]{1,0:T(8,128)(2,1)S(1)} %fusion.1), channel_id=1, source_target_pairs={{0,4},{4,0},{8,12},{12,8},{16,20},{20,16},{24,28},{28,24},{1,5},{5... | collective-permute-start | bytes 196616 | tf_op jit(solution)/shard_map/ppermute | solution.py:219
  57.8 26.2 %all-to-all-start.2 = ((bf16[8,400,128]{2,1,0:T(8,128)(2,1)}), bf16[8,400,128]{2,1,0:T(8,128)(2,1)S(1)}, u32[]{:S(2)}, u32[]{:S(2)}) async-start(bf16[8,400,128]{2,1,0:T(8,128)(2,1)} %pad_maximum_fusion), calls=%async_computation.2 | async-start | bytes 1638400 | tf_op jit(solution)/shard_map/all_to_all | solution.py:374
  63.0 15.1 %collective-permute-start.8 = (bf16[16,2048]{1,0:T(8,128)(2,1)S(1)}, bf16[16,2048]{1,0:T(8,128)(2,1)S(1)}, u32[]{:S(2)}, u32[]{:S(2)}) collective-permute-start(bf16[16,2048]{1,0:T(8,128)(2,1)S(1)} %add_convert_fusion.1), channel_id=1, source_target_pairs={{0,8},{4,12},{8,0},{12,4},{16,24},{20,28},{24,16},{28,20},{1,9},{5... | collective-permute-start | bytes 196616 | tf_op jit(solution)/shard_map/ppermute | solution.py:219
  78.1 5.9 %collective-permute-start.9 = (bf16[16,2048]{1,0:T(8,128)(2,1)S(1)}, bf16[16,2048]{1,0:T(8,128)(2,1)S(1)}, u32[]{:S(2)}, u32[]{:S(2)}) collective-permute-start(bf16[16,2048]{1,0:T(8,128)(2,1)S(1)} %add_convert_fusion), channel_id=1, source_target_pairs={{0,16},{4,20},{8,24},{12,28},{16,0},{20,4},{24,8},{28,12},{1,17},{... | collective-permute-start | bytes 196616 | tf_op jit(solution)/shard_map/ppermute | solution.py:219
  84.0 1.3 %collective-permute-start.10 = (bf16[16,2048]{1,0:T(8,128)(2,1)S(1)}, bf16[16,2048]{1,0:T(8,128)(2,1)S(1)}, u32[]{:S(2)}, u32[]{:S(2)}) collective-permute-start(bf16[16,2048]{1,0:T(8,128)(2,1)S(1)} %convert_add_fusion.1), channel_id=1, source_target_pairs={{0,1},{1,0},{2,3},{3,2},{4,5},{5,4},{6,7},{7,6},{8,9},{9,8},{10,11... | collective-permute-start | bytes 196616 | tf_op jit(solution)/shard_map/ppermute | solution.py:219

commit v4 on v2

--- a/solution.py
+++ b/solution.py
@@ -222,9 +222,10 @@
 
 
 def message_kernel(copies, *refs):
-    count = (len(refs) - 3) // 2
+    count = (len(refs) - 3) // 3
     operands, message_ref = refs[:count], refs[count]
-    held, in_sems, out_sems = refs[count + 1 : -2], refs[-2], refs[-1]
+    held, grouped = refs[count + 1 : 2 * count + 1], refs[2 * count + 1 : 3 * count + 1]
+    in_sems, out_sems = refs[-2], refs[-1]
     tok = operands[0].shape[0]
     arriving = [
         pltpu.make_async_copy(ref, to, in_sems.at[n])
@@ -233,13 +234,14 @@
     for copy in arriving:
         copy.start()
     leaving = []
-    for n, (copy, ref) in enumerate(zip(arriving, held)):
+    for n, copy in enumerate(arriving):
         copy.wait()
         for rank in range(message_ref.shape[0]):
-            cols = pl.ds((rank // copies) * HD, HD)
-            to = message_ref.at[rank, pl.ds(n * tok, tok), :]
-            leaving.append(pltpu.make_async_copy(ref.at[:, cols], to, out_sems.at[len(leaving)]))
-            leaving[-1].start()
+            at = (rank // copies) * HD
+            grouped[n][rank] = held[n][:, at : at + HD]
+        to = message_ref.at[:, pl.ds(n * tok, tok), :]
+        leaving.append(pltpu.make_async_copy(grouped[n], to, out_sems.at[n]))
+        leaving[-1].start()
     for copy in leaving:
         copy.wait()
 
@@ -254,22 +256,68 @@
         in_specs=[pl.BlockSpec(memory_space=pltpu.HBM)] * count,
         out_specs=pl.BlockSpec(memory_space=pltpu.HBM),
         scratch_shapes=[pltpu.VMEM(x.shape, x.dtype) for x in operands]
-        + [pltpu.SemaphoreType.DMA((count,)), pltpu.SemaphoreType.DMA((ranks * count,))],
+        + [pltpu.VMEM((ranks, tok, HD), x.dtype) for x in operands]
+        + [pltpu.SemaphoreType.DMA((count,))] * 2,
         cost_estimate=pl.CostEstimate(
             flops=0, bytes_accessed=4 * math.prod(shape), transcendentals=0
         ),
     )(*operands)
 
 
+def return_kernel(turn_ref, dq_ref, dk_ref, dv_ref, pair_ref, down_ref, taken_ref, *refs):
+    message_ref, held, sems = refs
+    blocks, tok, _ = dq_ref.shape
+    down = (down_ref[...] + taken_ref[...]).astype(held.dtype)
+    copies = []
+    for slot in range(blocks):
+        block = (slot + turn_ref[0]) % blocks
+        held[slot, 0:tok, :] = dq_ref[block]
+        dk = dk_ref[block] + pair_ref[block, 0:tok, :].astype(jnp.float32)
+        dv = dv_ref[block] + pair_ref[block, tok : 2 * tok, :].astype(jnp.float32)
+        held[slot, tok : 2 * tok, :] = dk.astype(held.dtype)
+        held[slot, 2 * tok : 3 * tok, :] = dv.astype(held.dtype)
+        held[slot, 3 * tok :, :] = down
+        copies.append(pltpu.make_async_copy(held.at[slot], message_ref.at[slot], sems.at[slot]))
+        copies[-1].start()
+    for copy in copies:
+        copy.wait()
+
+
+def return_message(turn, dq, *operands):
+    blocks, tok, _ = dq.shape
+    shape = (blocks, 3 * tok + operands[-1].shape[0], HD)
+    return pl.pallas_call(
+        return_kernel,
+        out_shape=shape_of(shape, dq.dtype),
+        in_specs=[pl.BlockSpec(memory_space=pltpu.SMEM)]
+        + [pl.BlockSpec(memory_space=pltpu.VMEM)] * (len(operands) + 1),
+        out_specs=pl.BlockSpec(memory_space=pltpu.HBM),
+        scratch_shapes=[pltpu.VMEM(shape, dq.dtype), pltpu.SemaphoreType.DMA((blocks,))],
+        compiler_params=pltpu.CompilerParams(vmem_limit_bytes=16 * 1024 * 1024),
+        cost_estimate=pl.CostEstimate(
+            flops=0, bytes_accessed=4 * math.prod(shape), transcendentals=0
+        ),
+    )(turn, dq, *operands)
+
+
 def unpack_kernel(copies, back_ref, *refs):
-    out_refs, down_ref = refs[:3], refs[3] if len(refs) > 3 else None
+    out_refs, held, sems = refs[:3], refs[-4:-1], refs[-1]
+    down_ref = refs[3] if len(refs) > 7 else None
     tok = out_refs[0].shape[0]
-    for at_head in range(out_refs[0].shape[1] // HD):
-        cols = slice(at_head * HD, (at_head + 1) * HD)
-        for n, ref in enumerate(out_refs):
-            ref[:, cols] = back_ref[at_head * copies, n * tok : (n + 1) * tok, :]
-        if down_ref is not None:
+    heads = out_refs[0].shape[1] // HD
+    leaving = []
+    for n, ref in enumerate(out_refs):
+        for at_head in range(heads):
+            cols = slice(at_head * HD, (at_head + 1) * HD)
+            held[n][:, cols] = back_ref[at_head * copies, n * tok : (n + 1) * tok, :]
+        leaving.append(pltpu.make_async_copy(held[n], ref, sems.at[n]))
+        leaving[-1].start()
+    if down_ref is not None:
+        for at_head in range(heads):
+            cols = slice(at_head * HD, (at_head + 1) * HD)
             down_ref[:, cols] = back_ref[at_head * copies, 3 * tok :, :].astype(jnp.float32)
+    for copy in leaving:
+        copy.wait()
 
 
 def in_vmem(body, outs, *operands):
@@ -489,17 +537,29 @@
         limit=28,
     )
     pair_other, _ = lax.optimization_barrier((pair_other, middle))
-    pair_received = swap(pair_other).astype(jnp.float32)
-    down_rows = jnp.where(first_copy, down_part + swap(down_part), 0.0)
-    dk = (dk_own + pair_received[:, :tok]).astype(jnp.bfloat16)
-    dv = (dv_own + pair_received[:, tok:]).astype(jnp.bfloat16)
-    down_rows = jnp.broadcast_to(down_rows.astype(jnp.bfloat16), (ranks, low_rank, HD))
-    back_message = jnp.concatenate([*map(in_order, (dq, dk, dv)), down_rows], axis=1)
+    turn = jnp.full((1,), jnp.where(shifted, 0, ranks // 2), jnp.int32)
+    back_message = return_message(
+        turn, dq, dk_own, dv_own, swap(pair_other), down_part, swap(down_part)
+    )
     back = exchange(back_message)
     outs = [shape_of((tok, feats), back.dtype)] * 3
     if seqs == ranks:
         outs.append(shape_of((low_rank, feats), jnp.float32))
-    outs = list(in_vmem(functools.partial(unpack_kernel, copies), outs, back))
+    whole = pl.BlockSpec(memory_space=pltpu.VMEM)
+    outs = list(
+        pl.pallas_call(
+            functools.partial(unpack_kernel, copies),
+            out_shape=outs,
+            in_specs=[whole],
+            out_specs=[pl.BlockSpec(memory_space=pltpu.HBM)] * 3 + [whole] * (len(outs) - 3),
+            scratch_shapes=[pltpu.VMEM((tok, feats), back.dtype)] * 3
+            + [pltpu.SemaphoreType.DMA((3,))],
+            compiler_params=pltpu.CompilerParams(vmem_limit_bytes=16 * 1024 * 1024),
+            cost_estimate=pl.CostEstimate(
+                flops=0, bytes_accessed=4 * back.size, transcendentals=0
+            ),
+        )(back)
+    )
     if seqs > ranks:
         bits = [bit for bit in powers_below(seqs) if bit >= ranks]
         down_terms = back[::copies, 3 * tok :].astype(jnp.float32)

time: 86 us -> 86.2 us (level)
  Pallas kernels: 14 us -> 15.4 us
  other arithmetic: 2.27 us -> 0.99 us
    pallas_call x0 -> x2, Pallas kernels: none -> 2.58 us  [the longest x1 1.6 us: on_device(): pl.pallas_call(functools.partial(unpack_kernel, copies), out_shape=outs,...]
    pallas_call x2 -> x1, Pallas kernels: 1.17 us -> 0.06 us  [in_vmem(): pl.pallas_call(body, out_shape=outs, in_specs=[whole] * len(operands), ou...]
    concatenate x1 -> x0, other arithmetic: 0.96 us -> none  [on_device(): jnp.concatenate([*map(in_order, (dq, dk, dv)), down_rows], axis=1)]
  transfers between devices with their start and end apart: 13 -> 13, of which waited for: 5 -> 4; matrix products, arithmetic and copies ran while one was open for 7% -> 5% of each run, Pallas kernels for 14% -> 16%
where the time goes in v4:
time: 86.2 us; the launch traced here: 85.7 us
  waiting for transfers between devices  26.1 us (30%)
  starting transfers between devices  23.3 us (27%)
  Pallas kernels  15.4 us (18%)
  blocking collectives  14.5 us (17%)
  matrix products  3.69 us (4%)
  other arithmetic  0.99 us (1%)
  between operations  0.87 us (1%)
    ppermute x4, waiting for transfers between devices, butterfly_sum(): taken = lax.ppermute(value, axis, pairs)  17.5 us
    all_to_all x1, blocking collectives, exchange(): lax.all_to_all(parts, ('seq', 'head'), 0, 0, axis_index_groups=groups, ti...  14.5 us
    all_to_all x2, starting transfers between devices, exchange(): lax.all_to_all(parts, ('seq', 'head'), 0, 0, axis_index_groups=groups, ti...  12.7 us
    pallas_call x4, Pallas kernels, call_kernel(): pl.pallas_call(body, out_shape=outs, in_specs=specs, out_specs=[pl.BlockS...  10.8 us
    ppermute x2, waiting for transfers between devices, on_device(): pieces.append(lax.ppermute(output_gradient, ('head', 'sub'), pairs))  7.71 us
    ppermute x4, starting transfers between devices, butterfly_sum(): taken = lax.ppermute(value, axis, pairs)  4.52 us
    dot_general x2, matrix products, dot_nn(): return jnp.dot(left, right, preferred_element_type=jnp.float32)  3.69 us
    ppermute x2, starting transfers between devices, on_device(): pieces.append(lax.ppermute(output_gradient, ('head', 'sub'), pairs))  3.42 us
  transfers between devices with their start and end apart: 13, of which 4 were waited for; matrix products, arithmetic and copies ran while one was open for 5% of the time, Pallas kernels for 16%

profile of v4, /device:TPU:0, one launch (start us, length us, event | category | flops | bytes accessed | tf_op | source)
XLA Modules:
  0.0 85.7 jit_solution(165292149546654568)
XLA Ops:
  0.6 2.0 %shard_map.110 = bf16[8,384,128]{2,1,0:T(8,128)(2,1)} custom-call(bf16[128,1024]{1,0:T(8,128)(2,1)} %refs_0_.1, bf16[128,1024]{1,0:T(8,128)(2,1)} %refs_1_.1, bf16[128,1024]{1,0:T(8,128)(2,1)} %refs_2_.1), custom_call_target="tpu_custom_call" | custom-call | bytes 1572864 | tf_op jit(solution)/shard_map/pallas_call | solution.py:253
  2.6 7.9 %all-to-all-start = ((bf16[8,384,128]{2,1,0:T(8,128)(2,1)}), bf16[8,384,128]{2,1,0:T(8,128)(2,1)S(1)}, u32[]{:S(2)}, u32[]{:S(2)}) async-start(bf16[8,384,128]{2,1,0:T(8,128)(2,1)} %shard_map.110), calls=%async_computation | async-start | bytes 1572864 | tf_op jit(solution)/shard_map/all_to_all | solution.py:414
  10.5 1.7 %collective-permute-start = (bf16[128,2048]{1,0:T(8,128)(2,1)}, bf16[128,2048]{1,0:T(8,128)(2,1)S(1)}, u32[]{:S(2)}, u32[]{:S(2)}) collective-permute-start(bf16[128,2048]{1,0:T(8,128)(2,1)} %param.10), channel_id=1, source_target_pairs={{0,0},{1,2},{2,1},{3,3},{4,4},{5,6},{6,5},{7,7},{8,8},{9,10},{10,9... | collective-permute-start | bytes 1572872 | tf_op jit(solution)/shard_map/ppermute | solution.py:438
  12.2 1.7 %collective-permute-start.1 = (bf16[128,2048]{1,0:T(8,128)(2,1)}, bf16[128,2048]{1,0:T(8,128)(2,1)S(1)}, u32[]{:S(2)}, u32[]{:S(2)}) collective-permute-start(bf16[128,2048]{1,0:T(8,128)(2,1)} %param.10), channel_id=1, source_target_pairs={{0,2},{1,0},{2,3},{3,1},{4,6},{5,4},{6,7},{7,5},{8,10},{9,8},{10,1... | collective-permute-start | bytes 1572872 | tf_op jit(solution)/shard_map/ppermute | solution.py:438
  13.9 0.7 dynamic-slice_bitcast_fusion.down_t_ref
  14.7 3.5 %fusion.refs_2_ = bf16[1024,2048]{1,0:T(8,128)(2,1)S(1)} fusion(bf16[1024,2048]{1,0:T(8,128)(2,1)} %param.11, bf16[16,2048]{1,0:T(8,128)(2,1)S(1)} %constant_dynamic-slice_fusion.refs_3_, bf16[1024,16]{0,1:T(8,128)(2,1)} %param.12), kind=kOutput, calls=%fused_computation.1 | convolution fusion | flops 75497472 | bytes 8486912 | tf_op jit(solution)/shard_map/dot_general | solution.py:26
  18.2 7.7 %collective-permute-done.1.refs_1_ = bf16[128,2048]{1,0:T(8,128)(2,1)S(1)} collective-permute-done((bf16[128,2048]{1,0:T(8,128)(2,1)}, bf16[128,2048]{1,0:T(8,128)(2,1)S(1)}, u32[]{:S(2)}, u32[]{:S(2)}) %collective-permute-start.1) | collective-permute-done | bytes 524320 | tf_op jit(solution)/shard_map/ppermute | solution.py:438
  25.9 2.1 %shard_map.111 = (f32[1040,128]{1,0:T(8,128)S(1)}, bf16[1040,128]{1,0:T(8,128)(2,1)S(1)}) custom-call(s32[4]{0:T(128)S(1)} %pad_add_fusion.plan_ref, bf16[128,2048]{1,0:T(8,128)(2,1)S(1)} %collective-permute-done.refs_0_, bf16[128,2048]{1,0:T(8,128)(2,1)S(1)} %collective-permute-done.1.refs_1_, bf16[1024,2048]{1,0:T(8,128)(2,1)S(1)} %fusion.refs_2_, ...), custom_call_target="tpu_custom_call" | custom-call | bytes 1024 | tf_op jit(solution)/shard_map/pallas_call | solution.py:192
  28.2 0.8 collective-permute-start.2
  29.1 1.7 %shard_map.112 = (f32[128,1024]{1,0:T(8,128)S(1)}, f32[8,1024]{1,0:T(8,128)S(1)}) custom-call(s32[1]{0:T(128)} %bitcast.1.scalar_ref, bf16[8,384,128]{2,1,0:T(8,128)(2,1)S(1)} %maximum_select_fusion.own_ref), custom_call_target="tpu_custom_call" | custom-call | flops 335544320 | bytes 1343492 | tf_op jit(solution)/shard_map/pallas_call | solution.py:192
  30.9 2.2 %shard_map.113 = (bf16[128,1024]{1,0:T(8,128)(2,1)S(1)}, f32[16,1024]{1,0:T(8,128)S(1)}, f32[8,1024]{1,0:T(8,128)S(1)}) custom-call(s32[1]{0:T(128)} %bitcast.1.scalar_ref, bf16[8,384,128]{2,1,0:T(8,128)(2,1)S(1)} %maximum_select_fusion.own_ref, bf16[8,256,128]{2,1,0:T(8,128)(2,1)S(1)} %collective-permute-done.2.other_ref, ...), custom_call_target="tpu_custom_call" | custom-call | flops 335544320 | bytes 2232324 | tf_op jit(solution)/shard_map/pallas_call | solution.py:192
  33.2 14.5 %all_to_all.15 = bf16[8,160,128]{2,1,0:T(8,128)(2,1)S(1)} all-to-all(bf16[8,160,128]{2,1,0:T(8,128)(2,1)S(1)} %shard_map.114), channel_id=1, replica_groups={{16,20,24,28,0,4,8,12},{18,22,26,30,2,6,10,14},{17,21,25,29,1,5,9,13},{..., dimensions={0} | all-to-all | bytes 655360 | tf_op jit(solution)/shard_map/all_to_all | solution.py:414
  47.7 1.4 %collective-permute-start.4 = (f32[16,128]{1,0:T(8,128)S(1)}, f32[16,128]{1,0:T(8,128)S(1)}, u32[]{:S(2)}, u32[]{:S(2)}) collective-permute-start(f32[16,128]{1,0:T(8,128)S(1)} %convert_reduce_fusion), channel_id=1, source_target_pairs={{0,2},{2,0},{1,3},{3,1},{4,6},{6,4},{5,7},{7,5},{8,10},{10,8},{9,1... | collective-permute-start | bytes 24584 | tf_op jit(solution)/shard_map/ppermute | solution.py:515
  49.2 4.8 %shard_map.115 = (bf16[8,128,128]{2,1,0:T(8,128)(2,1)S(1)}, f32[8,128,128]{2,1,0:T(8,128)S(1)}, f32[8,128,128]{2,1,0:T(8,128)S(1)}, bf16[8,256,128]{2,1,0:T(8,128)(2,1)S(1)}, f32[16,128]{1,0:T(8,128)S(1)}) custom-call(s32[1]{0:T(128)} %bitcast.1.scalar_ref, bf16[8,384,128]{2,1,0:T(8,128)(2,1)S(1)} %maximum_select_fusion.own_ref, ...), custom_call_target="tpu_custom_call" | custom-call | flops 1677721600 | bytes 3743748 | tf_op jit(solution)/shard_map/pallas_call | solution.py:192
  54.3 0.9 %collective-permute-start.7 = (bf16[16,2048]{1,0:T(8,128)(2,1)S(1)}, bf16[16,2048]{1,0:T(8,128)(2,1)S(1)}, u32[]{:S(2)}, u32[]{:S(2)}) collective-permute-start(bf16[16,2048]{1,0:T(8,128)(2,1)S(1)} %fusion.1), channel_id=1, source_target_pairs={{0,4},{4,0},{8,12},{12,8},{16,20},{20,16},{24,28},{28,24},{1,5},{5... | collective-permute-start | bytes 196616 | tf_op jit(solution)/shard_map/ppermute | solution.py:215
  55.4 1.0 %collective-permute-done.6.taken_ref = f32[16,128]{1,0:T(8,128)S(1)} collective-permute-done((f32[16,128]{1,0:T(8,128)S(1)}, f32[16,128]{1,0:T(8,128)S(1)}, u32[]{:S(2)}, u32[]{:S(2)}) %collective-permute-start.6) | collective-permute-done | bytes 8224 | tf_op jit(solution)/shard_map/ppermute | solution.py:421
  56.4 1.0 %shard_map.116 = bf16[8,400,128]{2,1,0:T(8,128)(2,1)} custom-call(s32[1]{0:T(128)} %bitcast.turn_ref, bf16[8,128,128]{2,1,0:T(8,128)(2,1)S(1)} %get-tuple-element.40.dq_ref, f32[8,128,128]{2,1,0:T(8,128)S(1)} %get-tuple-element.41.dk_ref, f32[8,128,128]{2,1,0:T(8,128)S(1)} %get-tuple-element.42.dv_ref, ...), custom_call_target="tpu_custom_call" | custom-call | bytes 1638400 | tf_op jit(solution)/shard_map/pallas_call | solution.py:289
  57.4 4.8 %all-to-all-start.2 = ((bf16[8,400,128]{2,1,0:T(8,128)(2,1)}), bf16[8,400,128]{2,1,0:T(8,128)(2,1)S(1)}, u32[]{:S(2)}, u32[]{:S(2)}) async-start(bf16[8,400,128]{2,1,0:T(8,128)(2,1)} %shard_map.116), calls=%async_computation.2 | async-start | bytes 1638400 | tf_op jit(solution)/shard_map/all_to_all | solution.py:414
  62.3 0.6 collective-permute-start.8
  62.9 14.5 %collective-permute-done.8 = bf16[16,2048]{1,0:T(8,128)(2,1)S(1)} collective-permute-done((bf16[16,2048]{1,0:T(8,128)(2,1)S(1)}, bf16[16,2048]{1,0:T(8,128)(2,1)S(1)}, u32[]{:S(2)}, u32[]{:S(2)}) %collective-permute-start.8) | collective-permute-done | bytes 65568 | tf_op jit(solution)/shard_map/ppermute | solution.py:215
  77.4 2.9 %collective-permute-start.9 = (bf16[16,2048]{1,0:T(8,128)(2,1)S(1)}, bf16[16,2048]{1,0:T(8,128)(2,1)S(1)}, u32[]{:S(2)}, u32[]{:S(2)}) collective-permute-start(bf16[16,2048]{1,0:T(8,128)(2,1)S(1)} %add_convert_fusion), channel_id=1, source_target_pairs={{0,16},{4,20},{8,24},{12,28},{16,0},{20,4},{24,8},{28,12},{1,17},{... | collective-permute-start | bytes 196616 | tf_op jit(solution)/shard_map/ppermute | solution.py:215
  80.3 3.0 %collective-permute-done.9 = bf16[16,2048]{1,0:T(8,128)(2,1)S(1)} collective-permute-done((bf16[16,2048]{1,0:T(8,128)(2,1)S(1)}, bf16[16,2048]{1,0:T(8,128)(2,1)S(1)}, u32[]{:S(2)}, u32[]{:S(2)}) %collective-permute-start.9) | collective-permute-done | bytes 65568 | tf_op jit(solution)/shard_map/ppermute | solution.py:215
  83.4 1.6 %shard_map.117 = (bf16[128,1024]{1,0:T(8,128)(2,1)}, bf16[128,1024]{1,0:T(8,128)(2,1)}, bf16[128,1024]{1,0:T(8,128)(2,1)}, f32[16,1024]{1,0:T(8,128)}) custom-call(bf16[8,400,128]{2,1,0:T(8,128)(2,1)S(1)} %all-to-all-done.2.back_ref), custom_call_target="tpu_custom_call" | custom-call | bytes 1638400 | tf_op jit(solution)/shard_map/pallas_call | solution.py:550
  85.0 0.7 convert_add_fusion
  (34 shorter events, 1.2 us)
Async XLA Ops:
  0.6 14.0 %copy-start = (bf16[16,4096]{1,0:T(8,128)(2,1)S(1)}, bf16[16,4096]{1,0:T(8,128)(2,1)}, u32[]{:S(2)}) copy-start(bf16[16,4096]{1,0:T(8,128)(2,1)} %param.13) | copy-start | bytes 393220
  2.6 25.4 %all-to-all-start = ((bf16[8,384,128]{2,1,0:T(8,128)(2,1)}), bf16[8,384,128]{2,1,0:T(8,128)(2,1)S(1)}, u32[]{:S(2)}, u32[]{:S(2)}) async-start(bf16[8,384,128]{2,1,0:T(8,128)(2,1)} %shard_map.110), calls=%async_computation | async-start | bytes 1572864 | tf_op jit(solution)/shard_map/all_to_all | solution.py:414
  10.5 7.7 %collective-permute-start = (bf16[128,2048]{1,0:T(8,128)(2,1)}, bf16[128,2048]{1,0:T(8,128)(2,1)S(1)}, u32[]{:S(2)}, u32[]{:S(2)}) collective-permute-start(bf16[128,2048]{1,0:T(8,128)(2,1)} %param.10), channel_id=1, source_target_pairs={{0,0},{1,2},{2,1},{3,3},{4,4},{5,6},{6,5},{7,7},{8,8},{9,10},{10,9... | collective-permute-start | bytes 1572872 | tf_op jit(solution)/shard_map/ppermute | solution.py:438
  12.2 13.7 %collective-permute-start.1 = (bf16[128,2048]{1,0:T(8,128)(2,1)}, bf16[128,2048]{1,0:T(8,128)(2,1)S(1)}, u32[]{:S(2)}, u32[]{:S(2)}) collective-permute-start(bf16[128,2048]{1,0:T(8,128)(2,1)} %param.10), channel_id=1, source_target_pairs={{0,2},{1,0},{2,3},{3,1},{4,6},{5,4},{6,7},{7,5},{8,10},{9,8},{10,1... | collective-permute-start | bytes 1572872 | tf_op jit(solution)/shard_map/ppermute | solution.py:438
  28.2 2.6 %collective-permute-start.2 = (bf16[8,256,128]{2,1,0:T(8,128)(2,1)S(1)}, bf16[8,256,128]{2,1,0:T(8,128)(2,1)S(1)}, u32[]{:S(2)}, u32[]{:S(2)}) collective-permute-start(bf16[8,256,128]{2,1,0:T(8,128)(2,1)S(1)} %slice.38), channel_id=1, source_target_pairs={{0,1},{1,0},{2,3},{3,2},{4,5},{5,4},{6,7},{7,6},{8,9},{9,8},{10,11... | collective-permute-start | bytes 1572872 | tf_op jit(solution)/shard_map/ppermute | solution.py:421
  29.1 4.0 %collective-permute-start.3 = (bf16[1040,128]{1,0:T(8,128)(2,1)S(1)}, bf16[1040,128]{1,0:T(8,128)(2,1)S(1)}, u32[]{:S(2)}, u32[]{:S(2)}) collective-permute-start(bf16[1040,128]{1,0:T(8,128)(2,1)S(1)} %get-tuple-element.31), channel_id=1, source_target_pairs={{0,1},{1,0},{2,3},{3,2},{4,5},{5,4},{6,7},{7,6},{8,9},{9,8},{10,11... | collective-permute-start | bytes 798728 | tf_op jit(solution)/shard_map/ppermute | solution.py:421
  33.2 21.0 %copy-start.1 = (bf16[128,2048]{1,0:T(8,128)(2,1)S(1)}, bf16[128,2048]{1,0:T(8,128)(2,1)}, u32[]{:S(2)}) copy-start(bf16[128,2048]{1,0:T(8,128)(2,1)} %param.10) | copy-start | bytes 1572868
  47.7 6.4 %collective-permute-start.4 = (f32[16,128]{1,0:T(8,128)S(1)}, f32[16,128]{1,0:T(8,128)S(1)}, u32[]{:S(2)}, u32[]{:S(2)}) collective-permute-start(f32[16,128]{1,0:T(8,128)S(1)} %convert_reduce_fusion), channel_id=1, source_target_pairs={{0,2},{2,0},{1,3},{3,1},{4,6},{6,4},{5,7},{7,5},{8,10},{10,8},{9,1... | collective-permute-start | bytes 24584 | tf_op jit(solution)/shard_map/ppermute | solution.py:515
  54.1 2.3 %collective-permute-start.5 = (bf16[8,256,128]{2,1,0:T(8,128)(2,1)S(1)}, bf16[8,256,128]{2,1,0:T(8,128)(2,1)S(1)}, u32[]{:S(2)}, u32[]{:S(2)}) collective-permute-start(bf16[8,256,128]{2,1,0:T(8,128)(2,1)S(1)} %get-tuple-element.44), channel_id=1, source_target_pairs={{0,1},{1,0},{2,3},{3,2},{4,5},{5,4},{6,7},{7,6},{8,9},{9,8},{10,11... | collective-permute-start | bytes 1572872 | tf_op jit(solution)/shard_map/ppermute | solution.py:421
  54.3 7.9 %collective-permute-start.7 = (bf16[16,2048]{1,0:T(8,128)(2,1)S(1)}, bf16[16,2048]{1,0:T(8,128)(2,1)S(1)}, u32[]{:S(2)}, u32[]{:S(2)}) collective-permute-start(bf16[16,2048]{1,0:T(8,128)(2,1)S(1)} %fusion.1), channel_id=1, source_target_pairs={{0,4},{4,0},{8,12},{12,8},{16,20},{20,16},{24,28},{28,24},{1,5},{5... | collective-permute-start | bytes 196616 | tf_op jit(solution)/shard_map/ppermute | solution.py:215
  55.2 1.2 %collective-permute-start.6 = (f32[16,128]{1,0:T(8,128)S(1)}, f32[16,128]{1,0:T(8,128)S(1)}, u32[]{:S(2)}, u32[]{:S(2)}) collective-permute-start(f32[16,128]{1,0:T(8,128)S(1)} %get-tuple-element.45.down_ref), channel_id=1, source_target_pairs={{0,1},{1,0},{2,3},{3,2},{4,5},{5,4},{6,7},{7,6},{8,9},{9,8},{10,11... | collective-permute-start | bytes 24584 | tf_op jit(solution)/shard_map/ppermute | solution.py:421
  57.4 25.9 %all-to-all-start.2 = ((bf16[8,400,128]{2,1,0:T(8,128)(2,1)}), bf16[8,400,128]{2,1,0:T(8,128)(2,1)S(1)}, u32[]{:S(2)}, u32[]{:S(2)}) async-start(bf16[8,400,128]{2,1,0:T(8,128)(2,1)} %shard_map.116), calls=%async_computation.2 | async-start | bytes 1638400 | tf_op jit(solution)/shard_map/all_to_all | solution.py:414
  62.3 15.1 %collective-permute-start.8 = (bf16[16,2048]{1,0:T(8,128)(2,1)S(1)}, bf16[16,2048]{1,0:T(8,128)(2,1)S(1)}, u32[]{:S(2)}, u32[]{:S(2)}) collective-permute-start(bf16[16,2048]{1,0:T(8,128)(2,1)S(1)} %add_convert_fusion.1), channel_id=1, source_target_pairs={{0,8},{4,12},{8,0},{12,4},{16,24},{20,28},{24,16},{28,20},{1,9},{5... | collective-permute-start | bytes 196616 | tf_op jit(solution)/shard_map/ppermute | solution.py:215
  77.4 5.9 %collective-permute-start.9 = (bf16[16,2048]{1,0:T(8,128)(2,1)S(1)}, bf16[16,2048]{1,0:T(8,128)(2,1)S(1)}, u32[]{:S(2)}, u32[]{:S(2)}) collective-permute-start(bf16[16,2048]{1,0:T(8,128)(2,1)S(1)} %add_convert_fusion), channel_id=1, source_target_pairs={{0,16},{4,20},{8,24},{12,28},{16,0},{20,4},{24,8},{28,12},{1,17},{... | collective-permute-start | bytes 196616 | tf_op jit(solution)/shard_map/ppermute | solution.py:215
  83.3 1.7 %collective-permute-start.10 = (bf16[16,2048]{1,0:T(8,128)(2,1)S(1)}, bf16[16,2048]{1,0:T(8,128)(2,1)S(1)}, u32[]{:S(2)}, u32[]{:S(2)}) collective-permute-start(bf16[16,2048]{1,0:T(8,128)(2,1)S(1)} %convert_add_fusion.1), channel_id=1, source_target_pairs={{0,1},{1,0},{2,3},{3,2},{4,5},{5,4},{6,7},{7,6},{8,9},{9,8},{10,11... | collective-permute-start | bytes 196616 | tf_op jit(solution)/shard_map/ppermute | solution.py:215

commit v5 on v4

--- a/solution.py
+++ b/solution.py
@@ -54,15 +54,27 @@
     return functools.reduce(jnp.add, terms)
 
 
+def ahead(prepare, tiles):
+    tiles = list(tiles)
+    ready = prepare(tiles[0])
+    for tile, following in zip(tiles, tiles[1:] + [None]):
+        present, ready = ready, None if following is None else prepare(following)
+        yield tile, present
+
+
 def forward_own_kernel(tok, scalar_ref, own_ref, total_ref, stat_ref):
     blocks = own_ref.shape[0]
     step = TILE // tok
     values_t = rows_of(own_ref, blocks, 2 * tok, tok).T
-    for tile in range(blocks // step):
+
+    def prepare(tile):
+        upto = (tile + 1) * step
+        queries = own_ref[tile * step : upto, 0:tok, :].reshape(TILE, HD)
+        return scores_of(rows_of(own_ref, upto, tok, tok), queries, own_visible())
+
+    for tile, scores in ahead(prepare, range(blocks // step)):
         upto = (tile + 1) * step
         at = tile * TILE
-        queries = own_ref[tile * step : upto, 0:tok, :].reshape(TILE, HD)
-        scores = scores_of(rows_of(own_ref, upto, tok, tok), queries, own_visible())
         highest = jnp.max(scores, axis=0, keepdims=True)
         powers = jnp.exp2((scores - highest) * LOG2_SCALE)
         total_ref[:, at : at + TILE] = dot_nn(
@@ -88,14 +100,16 @@
     step = TILE // tok
     sub = scalar_ref[0]
     values_t = rows_of(other_ref, blocks, tok, tok).T
-    for tile in range(blocks // step):
+
+    def prepare(tile):
         upto = (tile + 1) * step
-        at = tile * TILE
-        here = pl.ds(at, TILE)
         queries = own_ref[tile * step : upto, 0:tok, :].reshape(TILE, HD)
-        scores = scores_of(
-            rows_of(other_ref, upto, 0, tok), queries, other_visible(sub, tok)
-        )
+        keys = rows_of(other_ref, upto, 0, tok)
+        return scores_of(keys, queries, other_visible(sub, tok))
+
+    for tile, scores in ahead(prepare, range(blocks // step)):
+        upto = (tile + 1) * step
+        here = pl.ds(tile * TILE, TILE)
         own_highest = own_stat_ref[0:1, here]
         highest = jnp.maximum(own_highest, jnp.max(scores, axis=0, keepdims=True))
         powers = jnp.exp2((scores - highest) * LOG2_SCALE)
@@ -140,24 +154,30 @@
         [dout_ref[block, HD : HD + low_rank, :] for block in range(blocks)], axis=1
     )
     down_grad_ref[...] = 2.0 * dot_nt(lora, attn_ref[...])
-    for tile in reversed(range(tiles)):
+
+    def prepare(tile):
+        upto = (tile + 1) * step
+        queries = own_ref[tile * step : upto, 0:tok, :].reshape(TILE, HD)
+        douts_t = jnp.concatenate(
+            [dout_ref[block, 0:HD, :] for block in range(tile * step, upto)], axis=1
+        )
+        own = scores_of(rows_of(own_ref, upto, tok, tok), queries, own_visible())
+        other = scores_of(
+            rows_of(other_ref, upto, 0, tok), queries, other_visible(sub, tok)
+        )
+        dprob_own = dot_nn(rows_of(own_ref, upto, 2 * tok, tok), douts_t)
+        dprob_other = dot_nn(rows_of(other_ref, upto, tok, tok), douts_t)
+        return queries, douts_t, own, other, dprob_own, dprob_other
+
+    for tile, prepared in ahead(prepare, reversed(range(tiles))):
+        queries, douts_t, own, other, dprob_own, dprob_other = prepared
         upto = (tile + 1) * step
         width = upto * tok
         at = tile * TILE
-        queries = own_ref[tile * step : upto, 0:tok, :].reshape(TILE, HD)
-        douts_t = jnp.concatenate(
-            [dout_ref[block, 0:HD, :] for block in range(tile * step, upto)], axis=1
-        )
         highest = stat_ref[0:1, at : at + TILE]
         inverse = stat_ref[1:2, at : at + TILE]
-        own = scores_of(rows_of(own_ref, upto, tok, tok), queries, own_visible())
-        other = scores_of(
-            rows_of(other_ref, upto, 0, tok), queries, other_visible(sub, tok)
-        )
         own = jnp.exp2((own - highest) * LOG2_SCALE) * inverse
         other = jnp.exp2((other - highest) * LOG2_SCALE) * inverse
-        dprob_own = dot_nn(rows_of(own_ref, upto, 2 * tok, tok), douts_t)
-        dprob_other = dot_nn(rows_of(other_ref, upto, tok, tok), douts_t)
         delta = jnp.sum(own * dprob_own, axis=0, keepdims=True) + jnp.sum(
             other * dprob_other, axis=0, keepdims=True
         )
@@ -301,23 +321,14 @@
 
 
 def unpack_kernel(copies, back_ref, *refs):
-    out_refs, held, sems = refs[:3], refs[-4:-1], refs[-1]
-    down_ref = refs[3] if len(refs) > 7 else None
+    out_refs, down_ref = refs[:3], refs[3] if len(refs) > 3 else None
     tok = out_refs[0].shape[0]
-    heads = out_refs[0].shape[1] // HD
-    leaving = []
-    for n, ref in enumerate(out_refs):
-        for at_head in range(heads):
-            cols = slice(at_head * HD, (at_head + 1) * HD)
-            held[n][:, cols] = back_ref[at_head * copies, n * tok : (n + 1) * tok, :]
-        leaving.append(pltpu.make_async_copy(held[n], ref, sems.at[n]))
-        leaving[-1].start()
-    if down_ref is not None:
-        for at_head in range(heads):
-            cols = slice(at_head * HD, (at_head + 1) * HD)
+    for at_head in range(out_refs[0].shape[1] // HD):
+        cols = slice(at_head * HD, (at_head + 1) * HD)
+        for n, ref in enumerate(out_refs):
+            ref[:, cols] = back_ref[at_head * copies, n * tok : (n + 1) * tok, :]
+        if down_ref is not None:
             down_ref[:, cols] = back_ref[at_head * copies, 3 * tok :, :].astype(jnp.float32)
-    for copy in leaving:
-        copy.wait()
 
 
 def in_vmem(body, outs, *operands):
@@ -545,21 +556,7 @@
     outs = [shape_of((tok, feats), back.dtype)] * 3
     if seqs == ranks:
         outs.append(shape_of((low_rank, feats), jnp.float32))
-    whole = pl.BlockSpec(memory_space=pltpu.VMEM)
-    outs = list(
-        pl.pallas_call(
-            functools.partial(unpack_kernel, copies),
-            out_shape=outs,
-            in_specs=[whole],
-            out_specs=[pl.BlockSpec(memory_space=pltpu.HBM)] * 3 + [whole] * (len(outs) - 3),
-            scratch_shapes=[pltpu.VMEM((tok, feats), back.dtype)] * 3
-            + [pltpu.SemaphoreType.DMA((3,))],
-            compiler_params=pltpu.CompilerParams(vmem_limit_bytes=16 * 1024 * 1024),
-            cost_estimate=pl.CostEstimate(
-                flops=0, bytes_accessed=4 * back.size, transcendentals=0
-            ),
-        )(back)
-    )
+    outs = list(in_vmem(functools.partial(unpack_kernel, copies), outs, back))
     if seqs > ranks:
         bits = [bit for bit in powers_below(seqs) if bit >= ranks]
         down_terms = back[::copies, 3 * tok :].astype(jnp.float32)

time: 86.2 us -> 83.9 us (0.973)
  Pallas kernels: 15.4 us -> 12.9 us
    pallas_call x4, Pallas kernels: 10.8 us -> 8.79 us  [call_kernel(): pl.pallas_call(body, out_shape=outs, in_specs=specs, out_specs=[pl.BlockS...]
    pallas_call x1 -> x0, Pallas kernels: 1.6 us -> none  [on_device(): pl.pallas_call(functools.partial(unpack_kernel, copies), out_shape=outs,...]
    pallas_call x1 -> x2, Pallas kernels: 0.06 us -> 1.17 us  [in_vmem(): pl.pallas_call(body, out_shape=outs, in_specs=[whole] * len(operands), ou...]
  transfers between devices with their start and end apart: 13 -> 13, of which waited for: 4 -> 6; matrix products, arithmetic and copies ran while one was open for 5% -> 6% of each run, Pallas kernels for 16% -> 13%
where the time goes in v5:
time: 83.9 us; the launch traced here: 83.4 us
  waiting for transfers between devices  26.4 us (31%)
  starting transfers between devices  23.4 us (28%)
  blocking collectives  14.4 us (17%)
  Pallas kernels  12.9 us (15%)
  matrix products  3.69 us (4%)
  other arithmetic  0.99 us (1%)
  between operations  0.85 us (1%)
    ppermute x4, waiting for transfers between devices, butterfly_sum(): taken = lax.ppermute(value, axis, pairs)  17.6 us
    all_to_all x1, blocking collectives, exchange(): lax.all_to_all(parts, ('seq', 'head'), 0, 0, axis_index_groups=groups, ti...  14.4 us
    all_to_all x2, starting transfers between devices, exchange(): lax.all_to_all(parts, ('seq', 'head'), 0, 0, axis_index_groups=groups, ti...  12.7 us
    pallas_call x4, Pallas kernels, call_kernel(): pl.pallas_call(body, out_shape=outs, in_specs=specs, out_specs=[pl.BlockS...  8.79 us
    ppermute x2, waiting for transfers between devices, on_device(): pieces.append(lax.ppermute(output_gradient, ('head', 'sub'), pairs))  7.71 us
    ppermute x4, starting transfers between devices, butterfly_sum(): taken = lax.ppermute(value, axis, pairs)  4.52 us
    dot_general x2, matrix products, dot_nn(): return jnp.dot(left, right, preferred_element_type=jnp.float32)  3.69 us
    ppermute x2, starting transfers between devices, on_device(): pieces.append(lax.ppermute(output_gradient, ('head', 'sub'), pairs))  3.42 us
  transfers between devices with their start and end apart: 13, of which 6 were waited for; matrix products, arithmetic and copies ran while one was open for 6% of the time, Pallas kernels for 13%

profile of v5, /device:TPU:0, one launch (start us, length us, event | category | flops | bytes accessed | tf_op | source)
XLA Modules:
  0.0 83.4 jit_solution(13410931674911616014)
XLA Ops:
  0.6 2.0 %shard_map.110 = bf16[8,384,128]{2,1,0:T(8,128)(2,1)} custom-call(bf16[128,1024]{1,0:T(8,128)(2,1)} %refs_0_.1, bf16[128,1024]{1,0:T(8,128)(2,1)} %refs_1_.1, bf16[128,1024]{1,0:T(8,128)(2,1)} %refs_2_.1), custom_call_target="tpu_custom_call" | custom-call | bytes 1572864 | tf_op jit(solution)/shard_map/pallas_call | solution.py:273
  2.6 7.9 %all-to-all-start = ((bf16[8,384,128]{2,1,0:T(8,128)(2,1)}), bf16[8,384,128]{2,1,0:T(8,128)(2,1)S(1)}, u32[]{:S(2)}, u32[]{:S(2)}) async-start(bf16[8,384,128]{2,1,0:T(8,128)(2,1)} %shard_map.110), calls=%async_computation | async-start | bytes 1572864 | tf_op jit(solution)/shard_map/all_to_all | solution.py:425
  10.5 1.7 %collective-permute-start = (bf16[128,2048]{1,0:T(8,128)(2,1)}, bf16[128,2048]{1,0:T(8,128)(2,1)S(1)}, u32[]{:S(2)}, u32[]{:S(2)}) collective-permute-start(bf16[128,2048]{1,0:T(8,128)(2,1)} %param.10), channel_id=1, source_target_pairs={{0,0},{1,2},{2,1},{3,3},{4,4},{5,6},{6,5},{7,7},{8,8},{9,10},{10,9... | collective-permute-start | bytes 1572872 | tf_op jit(solution)/shard_map/ppermute | solution.py:449
  12.2 1.7 %collective-permute-start.1 = (bf16[128,2048]{1,0:T(8,128)(2,1)}, bf16[128,2048]{1,0:T(8,128)(2,1)S(1)}, u32[]{:S(2)}, u32[]{:S(2)}) collective-permute-start(bf16[128,2048]{1,0:T(8,128)(2,1)} %param.10), channel_id=1, source_target_pairs={{0,2},{1,0},{2,3},{3,1},{4,6},{5,4},{6,7},{7,5},{8,10},{9,8},{10,1... | collective-permute-start | bytes 1572872 | tf_op jit(solution)/shard_map/ppermute | solution.py:449
  13.9 0.7 dynamic-slice_bitcast_fusion.down_t_ref
  14.7 3.5 %fusion.refs_2_ = bf16[1024,2048]{1,0:T(8,128)(2,1)S(1)} fusion(bf16[1024,2048]{1,0:T(8,128)(2,1)} %param.11, bf16[16,2048]{1,0:T(8,128)(2,1)S(1)} %constant_dynamic-slice_fusion.refs_3_, bf16[1024,16]{0,1:T(8,128)(2,1)} %param.12), kind=kOutput, calls=%fused_computation.1 | convolution fusion | flops 75497472 | bytes 8486912 | tf_op jit(solution)/shard_map/dot_general | solution.py:26
  18.2 7.7 %collective-permute-done.1.refs_1_ = bf16[128,2048]{1,0:T(8,128)(2,1)S(1)} collective-permute-done((bf16[128,2048]{1,0:T(8,128)(2,1)}, bf16[128,2048]{1,0:T(8,128)(2,1)S(1)}, u32[]{:S(2)}, u32[]{:S(2)}) %collective-permute-start.1) | collective-permute-done | bytes 524320 | tf_op jit(solution)/shard_map/ppermute | solution.py:449
  25.9 2.1 %shard_map.111 = (f32[1040,128]{1,0:T(8,128)S(1)}, bf16[1040,128]{1,0:T(8,128)(2,1)S(1)}) custom-call(s32[4]{0:T(128)S(1)} %pad_add_fusion.plan_ref, bf16[128,2048]{1,0:T(8,128)(2,1)S(1)} %collective-permute-done.refs_0_, bf16[128,2048]{1,0:T(8,128)(2,1)S(1)} %collective-permute-done.1.refs_1_, bf16[1024,2048]{1,0:T(8,128)(2,1)S(1)} %fusion.refs_2_, ...), custom_call_target="tpu_custom_call" | custom-call | bytes 1024 | tf_op jit(solution)/shard_map/pallas_call | solution.py:212
  28.2 0.8 collective-permute-start.2
  29.1 1.3 %shard_map.112 = (f32[128,1024]{1,0:T(8,128)S(1)}, f32[8,1024]{1,0:T(8,128)S(1)}) custom-call(s32[1]{0:T(128)} %bitcast.1.scalar_ref, bf16[8,384,128]{2,1,0:T(8,128)(2,1)S(1)} %maximum_select_fusion.own_ref), custom_call_target="tpu_custom_call" | custom-call | flops 335544320 | bytes 1343492 | tf_op jit(solution)/shard_map/pallas_call | solution.py:212
  30.6 1.5 %shard_map.113 = (bf16[128,1024]{1,0:T(8,128)(2,1)S(1)}, f32[16,1024]{1,0:T(8,128)S(1)}, f32[8,1024]{1,0:T(8,128)S(1)}) custom-call(s32[1]{0:T(128)} %bitcast.1.scalar_ref, bf16[8,384,128]{2,1,0:T(8,128)(2,1)S(1)} %maximum_select_fusion.own_ref, bf16[8,256,128]{2,1,0:T(8,128)(2,1)S(1)} %collective-permute-done.2.other_ref, ...), custom_call_target="tpu_custom_call" | custom-call | flops 335544320 | bytes 2232324 | tf_op jit(solution)/shard_map/pallas_call | solution.py:212
  32.2 14.4 %all_to_all.15 = bf16[8,160,128]{2,1,0:T(8,128)(2,1)S(1)} all-to-all(bf16[8,160,128]{2,1,0:T(8,128)(2,1)S(1)} %shard_map.114), channel_id=1, replica_groups={{16,20,24,28,0,4,8,12},{18,22,26,30,2,6,10,14},{17,21,25,29,1,5,9,13},{..., dimensions={0} | all-to-all | bytes 655360 | tf_op jit(solution)/shard_map/all_to_all | solution.py:425
  46.6 1.5 %collective-permute-start.4 = (f32[16,128]{1,0:T(8,128)S(1)}, f32[16,128]{1,0:T(8,128)S(1)}, u32[]{:S(2)}, u32[]{:S(2)}) collective-permute-start(f32[16,128]{1,0:T(8,128)S(1)} %convert_reduce_fusion), channel_id=1, source_target_pairs={{0,2},{2,0},{1,3},{3,1},{4,6},{6,4},{5,7},{7,5},{8,10},{10,8},{9,1... | collective-permute-start | bytes 24584 | tf_op jit(solution)/shard_map/ppermute | solution.py:526
  48.2 3.9 %shard_map.115 = (bf16[8,128,128]{2,1,0:T(8,128)(2,1)S(1)}, f32[8,128,128]{2,1,0:T(8,128)S(1)}, f32[8,128,128]{2,1,0:T(8,128)S(1)}, bf16[8,256,128]{2,1,0:T(8,128)(2,1)S(1)}, f32[16,128]{1,0:T(8,128)S(1)}) custom-call(s32[1]{0:T(128)} %bitcast.1.scalar_ref, bf16[8,384,128]{2,1,0:T(8,128)(2,1)S(1)} %maximum_select_fusion.own_ref, ...), custom_call_target="tpu_custom_call" | custom-call | flops 1677721600 | bytes 3743748 | tf_op jit(solution)/shard_map/pallas_call | solution.py:212
  52.5 0.9 %collective-permute-start.7 = (bf16[16,2048]{1,0:T(8,128)(2,1)S(1)}, bf16[16,2048]{1,0:T(8,128)(2,1)S(1)}, u32[]{:S(2)}, u32[]{:S(2)}) collective-permute-start(bf16[16,2048]{1,0:T(8,128)(2,1)S(1)} %fusion.1), channel_id=1, source_target_pairs={{0,4},{4,0},{8,12},{12,8},{16,20},{20,16},{24,28},{28,24},{1,5},{5... | collective-permute-start | bytes 196616 | tf_op jit(solution)/shard_map/ppermute | solution.py:235
  53.5 1.0 %collective-permute-done.6.taken_ref = f32[16,128]{1,0:T(8,128)S(1)} collective-permute-done((f32[16,128]{1,0:T(8,128)S(1)}, f32[16,128]{1,0:T(8,128)S(1)}, u32[]{:S(2)}, u32[]{:S(2)}) %collective-permute-start.6) | collective-permute-done | bytes 8224 | tf_op jit(solution)/shard_map/ppermute | solution.py:432
  54.5 1.0 %shard_map.116 = bf16[8,400,128]{2,1,0:T(8,128)(2,1)} custom-call(s32[1]{0:T(128)} %bitcast.turn_ref, bf16[8,128,128]{2,1,0:T(8,128)(2,1)S(1)} %get-tuple-element.40.dq_ref, f32[8,128,128]{2,1,0:T(8,128)S(1)} %get-tuple-element.41.dk_ref, f32[8,128,128]{2,1,0:T(8,128)S(1)} %get-tuple-element.42.dv_ref, ...), custom_call_target="tpu_custom_call" | custom-call | bytes 1638400 | tf_op jit(solution)/shard_map/pallas_call | solution.py:309
  55.5 4.9 %all-to-all-start.2 = ((bf16[8,400,128]{2,1,0:T(8,128)(2,1)}), bf16[8,400,128]{2,1,0:T(8,128)(2,1)S(1)}, u32[]{:S(2)}, u32[]{:S(2)}) async-start(bf16[8,400,128]{2,1,0:T(8,128)(2,1)} %shard_map.116), calls=%async_computation.2 | async-start | bytes 1638400 | tf_op jit(solution)/shard_map/all_to_all | solution.py:425
  60.4 0.6 collective-permute-start.8
  61.0 14.5 %collective-permute-done.8 = bf16[16,2048]{1,0:T(8,128)(2,1)S(1)} collective-permute-done((bf16[16,2048]{1,0:T(8,128)(2,1)S(1)}, bf16[16,2048]{1,0:T(8,128)(2,1)S(1)}, u32[]{:S(2)}, u32[]{:S(2)}) %collective-permute-start.8) | collective-permute-done | bytes 65568 | tf_op jit(solution)/shard_map/ppermute | solution.py:235
  75.5 2.9 %collective-permute-start.9 = (bf16[16,2048]{1,0:T(8,128)(2,1)S(1)}, bf16[16,2048]{1,0:T(8,128)(2,1)S(1)}, u32[]{:S(2)}, u32[]{:S(2)}) collective-permute-start(bf16[16,2048]{1,0:T(8,128)(2,1)S(1)} %add_convert_fusion), channel_id=1, source_target_pairs={{0,16},{4,20},{8,24},{12,28},{16,0},{20,4},{24,8},{28,12},{1,17},{... | collective-permute-start | bytes 196616 | tf_op jit(solution)/shard_map/ppermute | solution.py:235
  78.4 3.0 %collective-permute-done.9 = bf16[16,2048]{1,0:T(8,128)(2,1)S(1)} collective-permute-done((bf16[16,2048]{1,0:T(8,128)(2,1)S(1)}, bf16[16,2048]{1,0:T(8,128)(2,1)S(1)}, u32[]{:S(2)}, u32[]{:S(2)}) %collective-permute-start.9) | collective-permute-done | bytes 65568 | tf_op jit(solution)/shard_map/ppermute | solution.py:235
  81.5 1.1 %shard_map.117 = (bf16[128,1024]{1,0:T(8,128)(2,1)}, bf16[128,1024]{1,0:T(8,128)(2,1)}, bf16[128,1024]{1,0:T(8,128)(2,1)}, f32[16,1024]{1,0:T(8,128)}) custom-call(bf16[8,400,128]{2,1,0:T(8,128)(2,1)S(1)} %all-to-all-done.2.back_ref), custom_call_target="tpu_custom_call" | custom-call | bytes 1671168 | tf_op jit(solution)/shard_map/pallas_call | solution.py:338
  82.8 0.7 convert_add_fusion
  (34 shorter events, 1.4 us)
Async XLA Ops:
  0.6 14.0 %copy-start = (bf16[16,4096]{1,0:T(8,128)(2,1)S(1)}, bf16[16,4096]{1,0:T(8,128)(2,1)}, u32[]{:S(2)}) copy-start(bf16[16,4096]{1,0:T(8,128)(2,1)} %param.13) | copy-start | bytes 393220
  2.6 25.4 %all-to-all-start = ((bf16[8,384,128]{2,1,0:T(8,128)(2,1)}), bf16[8,384,128]{2,1,0:T(8,128)(2,1)S(1)}, u32[]{:S(2)}, u32[]{:S(2)}) async-start(bf16[8,384,128]{2,1,0:T(8,128)(2,1)} %shard_map.110), calls=%async_computation | async-start | bytes 1572864 | tf_op jit(solution)/shard_map/all_to_all | solution.py:425
  10.5 7.7 %collective-permute-start = (bf16[128,2048]{1,0:T(8,128)(2,1)}, bf16[128,2048]{1,0:T(8,128)(2,1)S(1)}, u32[]{:S(2)}, u32[]{:S(2)}) collective-permute-start(bf16[128,2048]{1,0:T(8,128)(2,1)} %param.10), channel_id=1, source_target_pairs={{0,0},{1,2},{2,1},{3,3},{4,4},{5,6},{6,5},{7,7},{8,8},{9,10},{10,9... | collective-permute-start | bytes 1572872 | tf_op jit(solution)/shard_map/ppermute | solution.py:449
  12.2 13.7 %collective-permute-start.1 = (bf16[128,2048]{1,0:T(8,128)(2,1)}, bf16[128,2048]{1,0:T(8,128)(2,1)S(1)}, u32[]{:S(2)}, u32[]{:S(2)}) collective-permute-start(bf16[128,2048]{1,0:T(8,128)(2,1)} %param.10), channel_id=1, source_target_pairs={{0,2},{1,0},{2,3},{3,1},{4,6},{5,4},{6,7},{7,5},{8,10},{9,8},{10,1... | collective-permute-start | bytes 1572872 | tf_op jit(solution)/shard_map/ppermute | solution.py:449
  28.2 2.4 %collective-permute-start.2 = (bf16[8,256,128]{2,1,0:T(8,128)(2,1)S(1)}, bf16[8,256,128]{2,1,0:T(8,128)(2,1)S(1)}, u32[]{:S(2)}, u32[]{:S(2)}) collective-permute-start(bf16[8,256,128]{2,1,0:T(8,128)(2,1)S(1)} %slice.38), channel_id=1, source_target_pairs={{0,1},{1,0},{2,3},{3,2},{4,5},{5,4},{6,7},{7,6},{8,9},{9,8},{10,11... | collective-permute-start | bytes 1572872 | tf_op jit(solution)/shard_map/ppermute | solution.py:432
  29.1 3.0 %collective-permute-start.3 = (bf16[1040,128]{1,0:T(8,128)(2,1)S(1)}, bf16[1040,128]{1,0:T(8,128)(2,1)S(1)}, u32[]{:S(2)}, u32[]{:S(2)}) collective-permute-start(bf16[1040,128]{1,0:T(8,128)(2,1)S(1)} %get-tuple-element.31), channel_id=1, source_target_pairs={{0,1},{1,0},{2,3},{3,2},{4,5},{5,4},{6,7},{7,6},{8,9},{9,8},{10,11... | collective-permute-start | bytes 798728 | tf_op jit(solution)/shard_map/ppermute | solution.py:432
  32.2 20.1 %copy-start.1 = (bf16[128,2048]{1,0:T(8,128)(2,1)S(1)}, bf16[128,2048]{1,0:T(8,128)(2,1)}, u32[]{:S(2)}) copy-start(bf16[128,2048]{1,0:T(8,128)(2,1)} %param.10) | copy-start | bytes 1572868
  46.6 5.5 %collective-permute-start.4 = (f32[16,128]{1,0:T(8,128)S(1)}, f32[16,128]{1,0:T(8,128)S(1)}, u32[]{:S(2)}, u32[]{:S(2)}) collective-permute-start(f32[16,128]{1,0:T(8,128)S(1)} %convert_reduce_fusion), channel_id=1, source_target_pairs={{0,2},{2,0},{1,3},{3,1},{4,6},{6,4},{5,7},{7,5},{8,10},{10,8},{9,1... | collective-permute-start | bytes 24584 | tf_op jit(solution)/shard_map/ppermute | solution.py:526
  52.2 2.3 %collective-permute-start.5 = (bf16[8,256,128]{2,1,0:T(8,128)(2,1)S(1)}, bf16[8,256,128]{2,1,0:T(8,128)(2,1)S(1)}, u32[]{:S(2)}, u32[]{:S(2)}) collective-permute-start(bf16[8,256,128]{2,1,0:T(8,128)(2,1)S(1)} %get-tuple-element.44), channel_id=1, source_target_pairs={{0,1},{1,0},{2,3},{3,2},{4,5},{5,4},{6,7},{7,6},{8,9},{9,8},{10,11... | collective-permute-start | bytes 1572872 | tf_op jit(solution)/shard_map/ppermute | solution.py:432
  52.5 7.9 %collective-permute-start.7 = (bf16[16,2048]{1,0:T(8,128)(2,1)S(1)}, bf16[16,2048]{1,0:T(8,128)(2,1)S(1)}, u32[]{:S(2)}, u32[]{:S(2)}) collective-permute-start(bf16[16,2048]{1,0:T(8,128)(2,1)S(1)} %fusion.1), channel_id=1, source_target_pairs={{0,4},{4,0},{8,12},{12,8},{16,20},{20,16},{24,28},{28,24},{1,5},{5... | collective-permute-start | bytes 196616 | tf_op jit(solution)/shard_map/ppermute | solution.py:235
  53.3 1.2 %collective-permute-start.6 = (f32[16,128]{1,0:T(8,128)S(1)}, f32[16,128]{1,0:T(8,128)S(1)}, u32[]{:S(2)}, u32[]{:S(2)}) collective-permute-start(f32[16,128]{1,0:T(8,128)S(1)} %get-tuple-element.45.down_ref), channel_id=1, source_target_pairs={{0,1},{1,0},{2,3},{3,2},{4,5},{5,4},{6,7},{7,6},{8,9},{9,8},{10,11... | collective-permute-start | bytes 24584 | tf_op jit(solution)/shard_map/ppermute | solution.py:432
  55.5 25.9 %all-to-all-start.2 = ((bf16[8,400,128]{2,1,0:T(8,128)(2,1)}), bf16[8,400,128]{2,1,0:T(8,128)(2,1)S(1)}, u32[]{:S(2)}, u32[]{:S(2)}) async-start(bf16[8,400,128]{2,1,0:T(8,128)(2,1)} %shard_map.116), calls=%async_computation.2 | async-start | bytes 1638400 | tf_op jit(solution)/shard_map/all_to_all | solution.py:425
  60.4 15.1 %collective-permute-start.8 = (bf16[16,2048]{1,0:T(8,128)(2,1)S(1)}, bf16[16,2048]{1,0:T(8,128)(2,1)S(1)}, u32[]{:S(2)}, u32[]{:S(2)}) collective-permute-start(bf16[16,2048]{1,0:T(8,128)(2,1)S(1)} %add_convert_fusion.1), channel_id=1, source_target_pairs={{0,8},{4,12},{8,0},{12,4},{16,24},{20,28},{24,16},{28,20},{1,9},{5... | collective-permute-start | bytes 196616 | tf_op jit(solution)/shard_map/ppermute | solution.py:235
  75.5 5.9 %collective-permute-start.9 = (bf16[16,2048]{1,0:T(8,128)(2,1)S(1)}, bf16[16,2048]{1,0:T(8,128)(2,1)S(1)}, u32[]{:S(2)}, u32[]{:S(2)}) collective-permute-start(bf16[16,2048]{1,0:T(8,128)(2,1)S(1)} %add_convert_fusion), channel_id=1, source_target_pairs={{0,16},{4,20},{8,24},{12,28},{16,0},{20,4},{24,8},{28,12},{1,17},{... | collective-permute-start | bytes 196616 | tf_op jit(solution)/shard_map/ppermute | solution.py:235
  81.5 1.3 %collective-permute-start.10 = (bf16[16,2048]{1,0:T(8,128)(2,1)S(1)}, bf16[16,2048]{1,0:T(8,128)(2,1)S(1)}, u32[]{:S(2)}, u32[]{:S(2)}) collective-permute-start(bf16[16,2048]{1,0:T(8,128)(2,1)S(1)} %convert_add_fusion.1), channel_id=1, source_target_pairs={{0,1},{1,0},{2,3},{3,2},{4,5},{5,4},{6,7},{7,6},{8,9},{9,8},{10,11... | collective-permute-start | bytes 196616 | tf_op jit(solution)/shard_map/ppermute | solution.py:235

commit v6 on v5

--- a/solution.py
+++ b/solution.py
@@ -54,12 +54,18 @@
     return functools.reduce(jnp.add, terms)
 
 
-def ahead(prepare, tiles):
+def in_stages(prepare, work, finish, tiles):
     tiles = list(tiles)
-    ready = prepare(tiles[0])
-    for tile, following in zip(tiles, tiles[1:] + [None]):
-        present, ready = ready, None if following is None else prepare(following)
-        yield tile, present
+    ready, worked = prepare(tiles[0]), None
+    for n, tile in enumerate(tiles):
+        present = ready
+        if n + 1 < len(tiles):
+            ready = prepare(tiles[n + 1])
+        now = work(tile, present)
+        if worked is not None:
+            finish(tiles[n - 1], worked)
+        worked = now
+    finish(tiles[-1], worked)
 
 
 def forward_own_kernel(tok, scalar_ref, own_ref, total_ref, stat_ref):
@@ -72,16 +78,20 @@
         queries = own_ref[tile * step : upto, 0:tok, :].reshape(TILE, HD)
         return scores_of(rows_of(own_ref, upto, tok, tok), queries, own_visible())
 
-    for tile, scores in ahead(prepare, range(blocks // step)):
-        upto = (tile + 1) * step
-        at = tile * TILE
+    def work(tile, scores):
+        here = pl.ds(tile * TILE, TILE)
         highest = jnp.max(scores, axis=0, keepdims=True)
         powers = jnp.exp2((scores - highest) * LOG2_SCALE)
-        total_ref[:, at : at + TILE] = dot_nn(
-            values_t[:, : upto * tok], powers.astype(jnp.bfloat16)
+        stat_ref[0:1, here] = highest
+        stat_ref[1:2, here] = jnp.sum(powers, axis=0, keepdims=True)
+        return powers.astype(jnp.bfloat16)
+
+    def finish(tile, powers):
+        total_ref[:, pl.ds(tile * TILE, TILE)] = dot_nn(
+            values_t[:, : (tile + 1) * TILE], powers
         )
-        stat_ref[0:1, at : at + TILE] = highest
-        stat_ref[1:2, at : at + TILE] = jnp.sum(powers, axis=0, keepdims=True)
+
+    in_stages(prepare, work, finish, range(blocks // step))
 
 
 def forward_kernel(
@@ -107,8 +117,7 @@
         keys = rows_of(other_ref, upto, 0, tok)
         return scores_of(keys, queries, other_visible(sub, tok))
 
-    for tile, scores in ahead(prepare, range(blocks // step)):
-        upto = (tile + 1) * step
+    def work(tile, scores):
         here = pl.ds(tile * TILE, TILE)
         own_highest = own_stat_ref[0:1, here]
         highest = jnp.maximum(own_highest, jnp.max(scores, axis=0, keepdims=True))
@@ -117,11 +126,18 @@
         inverse = 1.0 / (
             own_stat_ref[1:2, here] * share + jnp.sum(powers, axis=0, keepdims=True)
         )
-        attn = dot_nn(values_t[:, : upto * tok], powers.astype(jnp.bfloat16))
-        attn = ((attn + total_ref[:, here] * share) * inverse).astype(jnp.bfloat16)
-        attn_ref[:, here] = attn
         stat_ref[0:1, here] = highest
         stat_ref[1:2, here] = inverse
+        return powers.astype(jnp.bfloat16), share, inverse
+
+    def finish(tile, worked):
+        powers, share, inverse = worked
+        here = pl.ds(tile * TILE, TILE)
+        attn = dot_nn(values_t[:, : (tile + 1) * TILE], powers)
+        attn = (attn + total_ref[:, here] * share) * inverse
+        attn_ref[:, here] = attn.astype(jnp.bfloat16)
+
+    in_stages(prepare, work, finish, range(blocks // step))
     mid_ref[...] = dot_nn(down_t_ref[...], attn_ref[...])
 
 
@@ -169,13 +185,11 @@
         dprob_other = dot_nn(rows_of(other_ref, upto, tok, tok), douts_t)
         return queries, douts_t, own, other, dprob_own, dprob_other
 
-    for tile, prepared in ahead(prepare, reversed(range(tiles))):
+    def work(tile, prepared):
         queries, douts_t, own, other, dprob_own, dprob_other = prepared
-        upto = (tile + 1) * step
-        width = upto * tok
-        at = tile * TILE
-        highest = stat_ref[0:1, at : at + TILE]
-        inverse = stat_ref[1:2, at : at + TILE]
+        here = pl.ds(tile * TILE, TILE)
+        highest = stat_ref[0:1, here]
+        inverse = stat_ref[1:2, here]
         own = jnp.exp2((own - highest) * LOG2_SCALE) * inverse
         other = jnp.exp2((other - highest) * LOG2_SCALE) * inverse
         delta = jnp.sum(own * dprob_own, axis=0, keepdims=True) + jnp.sum(
@@ -183,20 +197,29 @@
         )
         ds_own = (own * (dprob_own - delta)).astype(jnp.bfloat16)
         ds_other = (other * (dprob_other - delta)).astype(jnp.bfloat16)
+        probs = own.astype(jnp.bfloat16), other.astype(jnp.bfloat16)
+        return queries, douts_t, ds_own, ds_other, *probs
+
+    def finish(tile, worked):
+        queries, douts_t, ds_own, ds_other, own, other = worked
+        upto = (tile + 1) * step
+        width = upto * tok
         dq = dot_nn(keys_own_t[:, :width], ds_own) + dot_nn(keys_other_t[:, :width], ds_other)
         dq = (dq * SCALE).T.astype(jnp.bfloat16)
         dq_ref[tile * step : upto] = dq.reshape(step, tok, HD)
         terms = (
             (dk_own, dot_nn(ds_own, queries)),
             (dk_other, dot_nn(ds_other, queries)),
-            (dv_own, dot_nt(own.astype(jnp.bfloat16), douts_t)),
-            (dv_other, dot_nt(other.astype(jnp.bfloat16), douts_t)),
+            (dv_own, dot_nt(own, douts_t)),
+            (dv_other, dot_nt(other, douts_t)),
         )
         for total, term in terms:
             if tile == tiles - 1:
                 total[...] = term
             else:
                 total[0:width] += term
+
+    in_stages(prepare, work, finish, reversed(range(tiles)))
     shape = (blocks, tok, HD)
     dk_own_ref[...] = (dk_own[...] * SCALE).reshape(shape)
     dv_own_ref[...] = dv_own[...].reshape(shape)

time: 83.9 us -> 83.8 us (level)
  no operation moved by 1% of the time
where the time goes in v6:
time: 83.8 us; the launch traced here: 83.4 us
  waiting for transfers between devices  26.5 us (32%)
  starting transfers between devices  23.3 us (28%)
  blocking collectives  14.4 us (17%)
  Pallas kernels  12.8 us (15%)
  matrix products  3.69 us (4%)
  other arithmetic  0.99 us (1%)
  between operations  0.85 us (1%)
    ppermute x4, waiting for transfers between devices, butterfly_sum(): taken = lax.ppermute(value, axis, pairs)  17.6 us
    all_to_all x1, blocking collectives, exchange(): lax.all_to_all(parts, ('seq', 'head'), 0, 0, axis_index_groups=groups, ti...  14.4 us
    all_to_all x2, starting transfers between devices, exchange(): lax.all_to_all(parts, ('seq', 'head'), 0, 0, axis_index_groups=groups, ti...  12.7 us
    pallas_call x4, Pallas kernels, call_kernel(): pl.pallas_call(body, out_shape=outs, in_specs=specs, out_specs=[pl.BlockS...  8.64 us
    ppermute x2, waiting for transfers between devices, on_device(): pieces.append(lax.ppermute(output_gradient, ('head', 'sub'), pairs))  7.71 us
    ppermute x4, starting transfers between devices, butterfly_sum(): taken = lax.ppermute(value, axis, pairs)  4.52 us
    dot_general x2, matrix products, dot_nn(): return jnp.dot(left, right, preferred_element_type=jnp.float32)  3.69 us
    ppermute x2, starting transfers between devices, on_device(): pieces.append(lax.ppermute(output_gradient, ('head', 'sub'), pairs))  3.42 us
  transfers between devices with their start and end apart: 13, of which 6 were waited for; matrix products, arithmetic and copies ran while one was open for 6% of the time, Pallas kernels for 13%

profile of v6, /device:TPU:0, one launch (start us, length us, event | category | flops | bytes accessed | tf_op | source)
XLA Modules:
  0.0 83.4 jit_solution(6781893023721760075)
XLA Ops:
  0.6 2.0 %shard_map.110 = bf16[8,384,128]{2,1,0:T(8,128)(2,1)} custom-call(bf16[128,1024]{1,0:T(8,128)(2,1)} %refs_0_.1, bf16[128,1024]{1,0:T(8,128)(2,1)} %refs_1_.1, bf16[128,1024]{1,0:T(8,128)(2,1)} %refs_2_.1), custom_call_target="tpu_custom_call" | custom-call | bytes 1572864 | tf_op jit(solution)/shard_map/pallas_call | solution.py:296
  2.6 7.9 %all-to-all-start = ((bf16[8,384,128]{2,1,0:T(8,128)(2,1)}), bf16[8,384,128]{2,1,0:T(8,128)(2,1)S(1)}, u32[]{:S(2)}, u32[]{:S(2)}) async-start(bf16[8,384,128]{2,1,0:T(8,128)(2,1)} %shard_map.110), calls=%async_computation | async-start | bytes 1572864 | tf_op jit(solution)/shard_map/all_to_all | solution.py:448
  10.5 1.7 %collective-permute-start = (bf16[128,2048]{1,0:T(8,128)(2,1)}, bf16[128,2048]{1,0:T(8,128)(2,1)S(1)}, u32[]{:S(2)}, u32[]{:S(2)}) collective-permute-start(bf16[128,2048]{1,0:T(8,128)(2,1)} %param.10), channel_id=1, source_target_pairs={{0,0},{1,2},{2,1},{3,3},{4,4},{5,6},{6,5},{7,7},{8,8},{9,10},{10,9... | collective-permute-start | bytes 1572872 | tf_op jit(solution)/shard_map/ppermute | solution.py:472
  12.2 1.7 %collective-permute-start.1 = (bf16[128,2048]{1,0:T(8,128)(2,1)}, bf16[128,2048]{1,0:T(8,128)(2,1)S(1)}, u32[]{:S(2)}, u32[]{:S(2)}) collective-permute-start(bf16[128,2048]{1,0:T(8,128)(2,1)} %param.10), channel_id=1, source_target_pairs={{0,2},{1,0},{2,3},{3,1},{4,6},{5,4},{6,7},{7,5},{8,10},{9,8},{10,1... | collective-permute-start | bytes 1572872 | tf_op jit(solution)/shard_map/ppermute | solution.py:472
  13.9 0.7 dynamic-slice_bitcast_fusion.down_t_ref
  14.7 3.5 %fusion.refs_2_ = bf16[1024,2048]{1,0:T(8,128)(2,1)S(1)} fusion(bf16[1024,2048]{1,0:T(8,128)(2,1)} %param.11, bf16[16,2048]{1,0:T(8,128)(2,1)S(1)} %constant_dynamic-slice_fusion.refs_3_, bf16[1024,16]{0,1:T(8,128)(2,1)} %param.12), kind=kOutput, calls=%fused_computation.1 | convolution fusion | flops 75497472 | bytes 8486912 | tf_op jit(solution)/shard_map/dot_general | solution.py:26
  18.2 7.7 %collective-permute-done.1.refs_1_ = bf16[128,2048]{1,0:T(8,128)(2,1)S(1)} collective-permute-done((bf16[128,2048]{1,0:T(8,128)(2,1)}, bf16[128,2048]{1,0:T(8,128)(2,1)S(1)}, u32[]{:S(2)}, u32[]{:S(2)}) %collective-permute-start.1) | collective-permute-done | bytes 524320 | tf_op jit(solution)/shard_map/ppermute | solution.py:472
  25.9 2.1 %shard_map.111 = (f32[1040,128]{1,0:T(8,128)S(1)}, bf16[1040,128]{1,0:T(8,128)(2,1)S(1)}) custom-call(s32[4]{0:T(128)S(1)} %pad_add_fusion.plan_ref, bf16[128,2048]{1,0:T(8,128)(2,1)S(1)} %collective-permute-done.refs_0_, bf16[128,2048]{1,0:T(8,128)(2,1)S(1)} %collective-permute-done.1.refs_1_, bf16[1024,2048]{1,0:T(8,128)(2,1)S(1)} %fusion.refs_2_, ...), custom_call_target="tpu_custom_call" | custom-call | bytes 1024 | tf_op jit(solution)/shard_map/pallas_call | solution.py:235
  28.2 0.8 collective-permute-start.2
  29.1 1.2 %shard_map.112 = (f32[128,1024]{1,0:T(8,128)S(1)}, f32[8,1024]{1,0:T(8,128)S(1)}) custom-call(s32[1]{0:T(128)} %bitcast.1.scalar_ref, bf16[8,384,128]{2,1,0:T(8,128)(2,1)S(1)} %maximum_select_fusion.own_ref), custom_call_target="tpu_custom_call" | custom-call | flops 335544320 | bytes 1343492 | tf_op jit(solution)/shard_map/pallas_call | solution.py:235
  30.6 1.4 %shard_map.113 = (bf16[128,1024]{1,0:T(8,128)(2,1)S(1)}, f32[16,1024]{1,0:T(8,128)S(1)}, f32[8,1024]{1,0:T(8,128)S(1)}) custom-call(s32[1]{0:T(128)} %bitcast.1.scalar_ref, bf16[8,384,128]{2,1,0:T(8,128)(2,1)S(1)} %maximum_select_fusion.own_ref, bf16[8,256,128]{2,1,0:T(8,128)(2,1)S(1)} %collective-permute-done.2.other_ref, ...), custom_call_target="tpu_custom_call" | custom-call | flops 335544320 | bytes 2232324 | tf_op jit(solution)/shard_map/pallas_call | solution.py:235
  32.2 14.4 %all_to_all.15 = bf16[8,160,128]{2,1,0:T(8,128)(2,1)S(1)} all-to-all(bf16[8,160,128]{2,1,0:T(8,128)(2,1)S(1)} %shard_map.114), channel_id=1, replica_groups={{16,20,24,28,0,4,8,12},{18,22,26,30,2,6,10,14},{17,21,25,29,1,5,9,13},{..., dimensions={0} | all-to-all | bytes 655360 | tf_op jit(solution)/shard_map/all_to_all | solution.py:448
  46.6 1.5 %collective-permute-start.4 = (f32[16,128]{1,0:T(8,128)S(1)}, f32[16,128]{1,0:T(8,128)S(1)}, u32[]{:S(2)}, u32[]{:S(2)}) collective-permute-start(f32[16,128]{1,0:T(8,128)S(1)} %convert_reduce_fusion), channel_id=1, source_target_pairs={{0,2},{2,0},{1,3},{3,1},{4,6},{6,4},{5,7},{7,5},{8,10},{10,8},{9,1... | collective-permute-start | bytes 24584 | tf_op jit(solution)/shard_map/ppermute | solution.py:549
  48.2 4.0 %shard_map.115 = (bf16[8,128,128]{2,1,0:T(8,128)(2,1)S(1)}, f32[8,128,128]{2,1,0:T(8,128)S(1)}, f32[8,128,128]{2,1,0:T(8,128)S(1)}, bf16[8,256,128]{2,1,0:T(8,128)(2,1)S(1)}, f32[16,128]{1,0:T(8,128)S(1)}) custom-call(s32[1]{0:T(128)} %bitcast.1.scalar_ref, bf16[8,384,128]{2,1,0:T(8,128)(2,1)S(1)} %maximum_select_fusion.own_ref, ...), custom_call_target="tpu_custom_call" | custom-call | flops 1677721600 | bytes 3743748 | tf_op jit(solution)/shard_map/pallas_call | solution.py:235
  52.4 0.9 %collective-permute-start.7 = (bf16[16,2048]{1,0:T(8,128)(2,1)S(1)}, bf16[16,2048]{1,0:T(8,128)(2,1)S(1)}, u32[]{:S(2)}, u32[]{:S(2)}) collective-permute-start(bf16[16,2048]{1,0:T(8,128)(2,1)S(1)} %fusion.1), channel_id=1, source_target_pairs={{0,4},{4,0},{8,12},{12,8},{16,20},{20,16},{24,28},{28,24},{1,5},{5... | collective-permute-start | bytes 196616 | tf_op jit(solution)/shard_map/ppermute | solution.py:258
  53.5 1.0 %collective-permute-done.6.taken_ref = f32[16,128]{1,0:T(8,128)S(1)} collective-permute-done((f32[16,128]{1,0:T(8,128)S(1)}, f32[16,128]{1,0:T(8,128)S(1)}, u32[]{:S(2)}, u32[]{:S(2)}) %collective-permute-start.6) | collective-permute-done | bytes 8224 | tf_op jit(solution)/shard_map/ppermute | solution.py:455
  54.5 1.0 %shard_map.116 = bf16[8,400,128]{2,1,0:T(8,128)(2,1)} custom-call(s32[1]{0:T(128)} %bitcast.turn_ref, bf16[8,128,128]{2,1,0:T(8,128)(2,1)S(1)} %get-tuple-element.40.dq_ref, f32[8,128,128]{2,1,0:T(8,128)S(1)} %get-tuple-element.41.dk_ref, f32[8,128,128]{2,1,0:T(8,128)S(1)} %get-tuple-element.42.dv_ref, ...), custom_call_target="tpu_custom_call" | custom-call | bytes 1638400 | tf_op jit(solution)/shard_map/pallas_call | solution.py:332
  55.5 4.8 %all-to-all-start.2 = ((bf16[8,400,128]{2,1,0:T(8,128)(2,1)}), bf16[8,400,128]{2,1,0:T(8,128)(2,1)S(1)}, u32[]{:S(2)}, u32[]{:S(2)}) async-start(bf16[8,400,128]{2,1,0:T(8,128)(2,1)} %shard_map.116), calls=%async_computation.2 | async-start | bytes 1638400 | tf_op jit(solution)/shard_map/all_to_all | solution.py:448
  60.3 0.6 collective-permute-start.8
  61.0 14.5 %collective-permute-done.8 = bf16[16,2048]{1,0:T(8,128)(2,1)S(1)} collective-permute-done((bf16[16,2048]{1,0:T(8,128)(2,1)S(1)}, bf16[16,2048]{1,0:T(8,128)(2,1)S(1)}, u32[]{:S(2)}, u32[]{:S(2)}) %collective-permute-start.8) | collective-permute-done | bytes 65568 | tf_op jit(solution)/shard_map/ppermute | solution.py:258
  75.5 2.9 %collective-permute-start.9 = (bf16[16,2048]{1,0:T(8,128)(2,1)S(1)}, bf16[16,2048]{1,0:T(8,128)(2,1)S(1)}, u32[]{:S(2)}, u32[]{:S(2)}) collective-permute-start(bf16[16,2048]{1,0:T(8,128)(2,1)S(1)} %add_convert_fusion), channel_id=1, source_target_pairs={{0,16},{4,20},{8,24},{12,28},{16,0},{20,4},{24,8},{28,12},{1,17},{... | collective-permute-start | bytes 196616 | tf_op jit(solution)/shard_map/ppermute | solution.py:258
  78.4 3.0 %collective-permute-done.9 = bf16[16,2048]{1,0:T(8,128)(2,1)S(1)} collective-permute-done((bf16[16,2048]{1,0:T(8,128)(2,1)S(1)}, bf16[16,2048]{1,0:T(8,128)(2,1)S(1)}, u32[]{:S(2)}, u32[]{:S(2)}) %collective-permute-start.9) | collective-permute-done | bytes 65568 | tf_op jit(solution)/shard_map/ppermute | solution.py:258
  81.5 1.1 %shard_map.117 = (bf16[128,1024]{1,0:T(8,128)(2,1)}, bf16[128,1024]{1,0:T(8,128)(2,1)}, bf16[128,1024]{1,0:T(8,128)(2,1)}, f32[16,1024]{1,0:T(8,128)}) custom-call(bf16[8,400,128]{2,1,0:T(8,128)(2,1)S(1)} %all-to-all-done.2.back_ref), custom_call_target="tpu_custom_call" | custom-call | bytes 1671168 | tf_op jit(solution)/shard_map/pallas_call | solution.py:361
  82.7 0.7 convert_add_fusion
  (34 shorter events, 1.6 us)
Async XLA Ops:
  0.6 14.0 %copy-start = (bf16[16,4096]{1,0:T(8,128)(2,1)S(1)}, bf16[16,4096]{1,0:T(8,128)(2,1)}, u32[]{:S(2)}) copy-start(bf16[16,4096]{1,0:T(8,128)(2,1)} %param.13) | copy-start | bytes 393220
  2.6 25.4 %all-to-all-start = ((bf16[8,384,128]{2,1,0:T(8,128)(2,1)}), bf16[8,384,128]{2,1,0:T(8,128)(2,1)S(1)}, u32[]{:S(2)}, u32[]{:S(2)}) async-start(bf16[8,384,128]{2,1,0:T(8,128)(2,1)} %shard_map.110), calls=%async_computation | async-start | bytes 1572864 | tf_op jit(solution)/shard_map/all_to_all | solution.py:448
  10.5 7.7 %collective-permute-start = (bf16[128,2048]{1,0:T(8,128)(2,1)}, bf16[128,2048]{1,0:T(8,128)(2,1)S(1)}, u32[]{:S(2)}, u32[]{:S(2)}) collective-permute-start(bf16[128,2048]{1,0:T(8,128)(2,1)} %param.10), channel_id=1, source_target_pairs={{0,0},{1,2},{2,1},{3,3},{4,4},{5,6},{6,5},{7,7},{8,8},{9,10},{10,9... | collective-permute-start | bytes 1572872 | tf_op jit(solution)/shard_map/ppermute | solution.py:472
  12.2 13.7 %collective-permute-start.1 = (bf16[128,2048]{1,0:T(8,128)(2,1)}, bf16[128,2048]{1,0:T(8,128)(2,1)S(1)}, u32[]{:S(2)}, u32[]{:S(2)}) collective-permute-start(bf16[128,2048]{1,0:T(8,128)(2,1)} %param.10), channel_id=1, source_target_pairs={{0,2},{1,0},{2,3},{3,1},{4,6},{5,4},{6,7},{7,5},{8,10},{9,8},{10,1... | collective-permute-start | bytes 1572872 | tf_op jit(solution)/shard_map/ppermute | solution.py:472
  28.2 2.4 %collective-permute-start.2 = (bf16[8,256,128]{2,1,0:T(8,128)(2,1)S(1)}, bf16[8,256,128]{2,1,0:T(8,128)(2,1)S(1)}, u32[]{:S(2)}, u32[]{:S(2)}) collective-permute-start(bf16[8,256,128]{2,1,0:T(8,128)(2,1)S(1)} %slice.38), channel_id=1, source_target_pairs={{0,1},{1,0},{2,3},{3,2},{4,5},{5,4},{6,7},{7,6},{8,9},{9,8},{10,11... | collective-permute-start | bytes 1572872 | tf_op jit(solution)/shard_map/ppermute | solution.py:455
  29.1 3.0 %collective-permute-start.3 = (bf16[1040,128]{1,0:T(8,128)(2,1)S(1)}, bf16[1040,128]{1,0:T(8,128)(2,1)S(1)}, u32[]{:S(2)}, u32[]{:S(2)}) collective-permute-start(bf16[1040,128]{1,0:T(8,128)(2,1)S(1)} %get-tuple-element.31), channel_id=1, source_target_pairs={{0,1},{1,0},{2,3},{3,2},{4,5},{5,4},{6,7},{7,6},{8,9},{9,8},{10,11... | collective-permute-start | bytes 798728 | tf_op jit(solution)/shard_map/ppermute | solution.py:455
  32.1 20.1 %copy-start.1 = (bf16[128,2048]{1,0:T(8,128)(2,1)S(1)}, bf16[128,2048]{1,0:T(8,128)(2,1)}, u32[]{:S(2)}) copy-start(bf16[128,2048]{1,0:T(8,128)(2,1)} %param.10) | copy-start | bytes 1572868
  46.6 5.5 %collective-permute-start.4 = (f32[16,128]{1,0:T(8,128)S(1)}, f32[16,128]{1,0:T(8,128)S(1)}, u32[]{:S(2)}, u32[]{:S(2)}) collective-permute-start(f32[16,128]{1,0:T(8,128)S(1)} %convert_reduce_fusion), channel_id=1, source_target_pairs={{0,2},{2,0},{1,3},{3,1},{4,6},{6,4},{5,7},{7,5},{8,10},{10,8},{9,1... | collective-permute-start | bytes 24584 | tf_op jit(solution)/shard_map/ppermute | solution.py:549
  52.1 2.3 %collective-permute-start.5 = (bf16[8,256,128]{2,1,0:T(8,128)(2,1)S(1)}, bf16[8,256,128]{2,1,0:T(8,128)(2,1)S(1)}, u32[]{:S(2)}, u32[]{:S(2)}) collective-permute-start(bf16[8,256,128]{2,1,0:T(8,128)(2,1)S(1)} %get-tuple-element.44), channel_id=1, source_target_pairs={{0,1},{1,0},{2,3},{3,2},{4,5},{5,4},{6,7},{7,6},{8,9},{9,8},{10,11... | collective-permute-start | bytes 1572872 | tf_op jit(solution)/shard_map/ppermute | solution.py:455
  52.4 7.9 %collective-permute-start.7 = (bf16[16,2048]{1,0:T(8,128)(2,1)S(1)}, bf16[16,2048]{1,0:T(8,128)(2,1)S(1)}, u32[]{:S(2)}, u32[]{:S(2)}) collective-permute-start(bf16[16,2048]{1,0:T(8,128)(2,1)S(1)} %fusion.1), channel_id=1, source_target_pairs={{0,4},{4,0},{8,12},{12,8},{16,20},{20,16},{24,28},{28,24},{1,5},{5... | collective-permute-start | bytes 196616 | tf_op jit(solution)/shard_map/ppermute | solution.py:258
  53.3 1.2 %collective-permute-start.6 = (f32[16,128]{1,0:T(8,128)S(1)}, f32[16,128]{1,0:T(8,128)S(1)}, u32[]{:S(2)}, u32[]{:S(2)}) collective-permute-start(f32[16,128]{1,0:T(8,128)S(1)} %get-tuple-element.45.down_ref), channel_id=1, source_target_pairs={{0,1},{1,0},{2,3},{3,2},{4,5},{5,4},{6,7},{7,6},{8,9},{9,8},{10,11... | collective-permute-start | bytes 24584 | tf_op jit(solution)/shard_map/ppermute | solution.py:455
  55.5 25.9 %all-to-all-start.2 = ((bf16[8,400,128]{2,1,0:T(8,128)(2,1)}), bf16[8,400,128]{2,1,0:T(8,128)(2,1)S(1)}, u32[]{:S(2)}, u32[]{:S(2)}) async-start(bf16[8,400,128]{2,1,0:T(8,128)(2,1)} %shard_map.116), calls=%async_computation.2 | async-start | bytes 1638400 | tf_op jit(solution)/shard_map/all_to_all | solution.py:448
  60.3 15.1 %collective-permute-start.8 = (bf16[16,2048]{1,0:T(8,128)(2,1)S(1)}, bf16[16,2048]{1,0:T(8,128)(2,1)S(1)}, u32[]{:S(2)}, u32[]{:S(2)}) collective-permute-start(bf16[16,2048]{1,0:T(8,128)(2,1)S(1)} %add_convert_fusion.1), channel_id=1, source_target_pairs={{0,8},{4,12},{8,0},{12,4},{16,24},{20,28},{24,16},{28,20},{1,9},{5... | collective-permute-start | bytes 196616 | tf_op jit(solution)/shard_map/ppermute | solution.py:258
  75.5 5.9 %collective-permute-start.9 = (bf16[16,2048]{1,0:T(8,128)(2,1)S(1)}, bf16[16,2048]{1,0:T(8,128)(2,1)S(1)}, u32[]{:S(2)}, u32[]{:S(2)}) collective-permute-start(bf16[16,2048]{1,0:T(8,128)(2,1)S(1)} %add_convert_fusion), channel_id=1, source_target_pairs={{0,16},{4,20},{8,24},{12,28},{16,0},{20,4},{24,8},{28,12},{1,17},{... | collective-permute-start | bytes 196616 | tf_op jit(solution)/shard_map/ppermute | solution.py:258
  81.4 1.3 %collective-permute-start.10 = (bf16[16,2048]{1,0:T(8,128)(2,1)S(1)}, bf16[16,2048]{1,0:T(8,128)(2,1)S(1)}, u32[]{:S(2)}, u32[]{:S(2)}) collective-permute-start(bf16[16,2048]{1,0:T(8,128)(2,1)S(1)} %convert_add_fusion.1), channel_id=1, source_target_pairs={{0,1},{1,0},{2,3},{3,2},{4,5},{5,4},{6,7},{7,6},{8,9},{9,8},{10,11... | collective-permute-start | bytes 196616 | tf_op jit(solution)/shard_map/ppermute | solution.py:258

commit v7 on v6

--- a/solution.py
+++ b/solution.py
@@ -68,7 +68,7 @@
     finish(tiles[-1], worked)
 
 
-def forward_own_kernel(tok, scalar_ref, own_ref, total_ref, stat_ref):
+def forward_own_kernel(tok, scalar_ref, own_ref, total_ref, stat_ref, keys_t_ref):
     blocks = own_ref.shape[0]
     step = TILE // tok
     values_t = rows_of(own_ref, blocks, 2 * tok, tok).T
@@ -91,7 +91,8 @@
             values_t[:, : (tile + 1) * TILE], powers
         )
 
-    in_stages(prepare, work, finish, range(blocks // step))
+    in_stages(prepare, work, finish, reversed(range(blocks // step)))
+    keys_t_ref[...] = rows_of(own_ref, blocks, tok, tok).T
 
 
 def forward_kernel(
@@ -137,7 +138,7 @@
         attn = (attn + total_ref[:, here] * share) * inverse
         attn_ref[:, here] = attn.astype(jnp.bfloat16)
 
-    in_stages(prepare, work, finish, range(blocks // step))
+    in_stages(prepare, work, finish, reversed(range(blocks // step)))
     mid_ref[...] = dot_nn(down_t_ref[...], attn_ref[...])
 
 
@@ -149,6 +150,7 @@
     dout_ref,
     attn_ref,
     stat_ref,
+    keys_t_ref,
     dq_ref,
     dk_own_ref,
     dv_own_ref,
@@ -163,7 +165,7 @@
     step = TILE // tok
     sub = scalar_ref[0]
     low_rank = down_grad_ref.shape[0]
-    keys_own_t = rows_of(own_ref, blocks, tok, tok).T
+    keys_own_t = keys_t_ref[...]
     keys_other_t = rows_of(other_ref, blocks, 0, tok).T
     tiles = blocks // step
     lora = jnp.concatenate(
@@ -501,9 +503,13 @@
 
     rows = ranks * tok
     pair_count = rows * (rows + TILE)
-    own_total, own_stats = call_kernel(
+    own_total, own_stats, own_keys_t = call_kernel(
         functools.partial(forward_own_kernel, tok),
-        [shape_of((HD, rows), jnp.float32), shape_of((8, rows), jnp.float32)],
+        [
+            shape_of((HD, rows), jnp.float32),
+            shape_of((8, rows), jnp.float32),
+            shape_of((HD, rows), jnp.bfloat16),
+        ],
         [],
         2 * pair_count * HD,
         pair_count // 2,
@@ -568,6 +574,7 @@
         in_order(arrived[:, : HD + low_rank]),
         attn_t,
         stats,
+        own_keys_t,
         limit=28,
     )
     pair_other, _ = lax.optimization_barrier((pair_other, middle))

time: 83.8 us -> 83.7 us (level)
  no operation moved by 1% of the time
where the time goes in v7:
time: 83.7 us; the launch traced here: 83.3 us
  waiting for transfers between devices  26.6 us (32%)
  starting transfers between devices  23.3 us (28%)
  blocking collectives  14.4 us (17%)
  Pallas kernels  12.6 us (15%)
  matrix products  3.69 us (4%)
  other arithmetic  1 us (1%)
  between operations  0.84 us (1%)
    ppermute x4, waiting for transfers between devices, butterfly_sum(): taken = lax.ppermute(value, axis, pairs)  17.6 us
    all_to_all x1, blocking collectives, exchange(): lax.all_to_all(parts, ('seq', 'head'), 0, 0, axis_index_groups=groups, ti...  14.4 us
    all_to_all x2, starting transfers between devices, exchange(): lax.all_to_all(parts, ('seq', 'head'), 0, 0, axis_index_groups=groups, ti...  12.7 us
    pallas_call x4, Pallas kernels, call_kernel(): pl.pallas_call(body, out_shape=outs, in_specs=specs, out_specs=[pl.BlockS...  8.48 us
    ppermute x2, waiting for transfers between devices, on_device(): pieces.append(lax.ppermute(output_gradient, ('head', 'sub'), pairs))  7.71 us
    ppermute x4, starting transfers between devices, butterfly_sum(): taken = lax.ppermute(value, axis, pairs)  4.52 us
    dot_general x2, matrix products, dot_nn(): return jnp.dot(left, right, preferred_element_type=jnp.float32)  3.69 us
    ppermute x2, starting transfers between devices, on_device(): pieces.append(lax.ppermute(output_gradient, ('head', 'sub'), pairs))  3.42 us
  transfers between devices with their start and end apart: 13, of which 6 were waited for; matrix products, arithmetic and copies ran while one was open for 6% of the time, Pallas kernels for 13%

profile of v7, /device:TPU:0, one launch (start us, length us, event | category | flops | bytes accessed | tf_op | source)
XLA Modules:
  0.0 83.3 jit_solution(7460730680856893763)
XLA Ops:
  0.6 2.0 %shard_map.110 = bf16[8,384,128]{2,1,0:T(8,128)(2,1)} custom-call(bf16[128,1024]{1,0:T(8,128)(2,1)} %refs_0_.1, bf16[128,1024]{1,0:T(8,128)(2,1)} %refs_1_.1, bf16[128,1024]{1,0:T(8,128)(2,1)} %refs_2_.1), custom_call_target="tpu_custom_call" | custom-call | bytes 1572864 | tf_op jit(solution)/shard_map/pallas_call | solution.py:298
  2.6 7.9 %all-to-all-start = ((bf16[8,384,128]{2,1,0:T(8,128)(2,1)}), bf16[8,384,128]{2,1,0:T(8,128)(2,1)S(1)}, u32[]{:S(2)}, u32[]{:S(2)}) async-start(bf16[8,384,128]{2,1,0:T(8,128)(2,1)} %shard_map.110), calls=%async_computation | async-start | bytes 1572864 | tf_op jit(solution)/shard_map/all_to_all | solution.py:450
  10.5 1.7 %collective-permute-start = (bf16[128,2048]{1,0:T(8,128)(2,1)}, bf16[128,2048]{1,0:T(8,128)(2,1)S(1)}, u32[]{:S(2)}, u32[]{:S(2)}) collective-permute-start(bf16[128,2048]{1,0:T(8,128)(2,1)} %param.10), channel_id=1, source_target_pairs={{0,0},{1,2},{2,1},{3,3},{4,4},{5,6},{6,5},{7,7},{8,8},{9,10},{10,9... | collective-permute-start | bytes 1572872 | tf_op jit(solution)/shard_map/ppermute | solution.py:474
  12.2 1.7 %collective-permute-start.1 = (bf16[128,2048]{1,0:T(8,128)(2,1)}, bf16[128,2048]{1,0:T(8,128)(2,1)S(1)}, u32[]{:S(2)}, u32[]{:S(2)}) collective-permute-start(bf16[128,2048]{1,0:T(8,128)(2,1)} %param.10), channel_id=1, source_target_pairs={{0,2},{1,0},{2,3},{3,1},{4,6},{5,4},{6,7},{7,5},{8,10},{9,8},{10,1... | collective-permute-start | bytes 1572872 | tf_op jit(solution)/shard_map/ppermute | solution.py:474
  13.9 0.7 dynamic-slice_bitcast_fusion.down_t_ref
  14.7 3.5 %fusion.refs_2_ = bf16[1024,2048]{1,0:T(8,128)(2,1)S(1)} fusion(bf16[1024,2048]{1,0:T(8,128)(2,1)} %param.11, bf16[16,2048]{1,0:T(8,128)(2,1)S(1)} %constant_dynamic-slice_fusion.refs_3_, bf16[1024,16]{0,1:T(8,128)(2,1)} %param.12), kind=kOutput, calls=%fused_computation.1 | convolution fusion | flops 75497472 | bytes 8486912 | tf_op jit(solution)/shard_map/dot_general | solution.py:26
  18.2 7.7 %collective-permute-done.1.refs_1_ = bf16[128,2048]{1,0:T(8,128)(2,1)S(1)} collective-permute-done((bf16[128,2048]{1,0:T(8,128)(2,1)}, bf16[128,2048]{1,0:T(8,128)(2,1)S(1)}, u32[]{:S(2)}, u32[]{:S(2)}) %collective-permute-start.1) | collective-permute-done | bytes 524320 | tf_op jit(solution)/shard_map/ppermute | solution.py:474
  25.9 2.1 %shard_map.111 = (f32[1040,128]{1,0:T(8,128)S(1)}, bf16[1040,128]{1,0:T(8,128)(2,1)S(1)}) custom-call(s32[4]{0:T(128)S(1)} %pad_add_fusion.plan_ref, bf16[128,2048]{1,0:T(8,128)(2,1)S(1)} %collective-permute-done.refs_0_, bf16[128,2048]{1,0:T(8,128)(2,1)S(1)} %collective-permute-done.1.refs_1_, bf16[1024,2048]{1,0:T(8,128)(2,1)S(1)} %fusion.refs_2_, ...), custom_call_target="tpu_custom_call" | custom-call | bytes 1024 | tf_op jit(solution)/shard_map/pallas_call | solution.py:237
  28.2 0.8 collective-permute-start.2
  29.1 1.1 %shard_map.112 = (f32[128,1024]{1,0:T(8,128)S(1)}, f32[8,1024]{1,0:T(8,128)S(1)}, bf16[128,1024]{1,0:T(8,128)(2,1)S(1)}) custom-call(s32[1]{0:T(128)} %bitcast.1.scalar_ref, bf16[8,384,128]{2,1,0:T(8,128)(2,1)S(1)} %maximum_select_fusion.own_ref), custom_call_target="tpu_custom_call" | custom-call | flops 335544320 | bytes 1605636 | tf_op jit(solution)/shard_map/pallas_call | solution.py:237
  30.6 1.3 %shard_map.113 = (bf16[128,1024]{1,0:T(8,128)(2,1)S(1)}, f32[16,1024]{1,0:T(8,128)S(1)}, f32[8,1024]{1,0:T(8,128)S(1)}) custom-call(s32[1]{0:T(128)} %bitcast.1.scalar_ref, bf16[8,384,128]{2,1,0:T(8,128)(2,1)S(1)} %maximum_select_fusion.own_ref, bf16[8,256,128]{2,1,0:T(8,128)(2,1)S(1)} %collective-permute-done.2.other_ref, ...), custom_call_target="tpu_custom_call" | custom-call | flops 335544320 | bytes 2232324 | tf_op jit(solution)/shard_map/pallas_call | solution.py:237
  32.1 14.4 %all_to_all.15 = bf16[8,160,128]{2,1,0:T(8,128)(2,1)S(1)} all-to-all(bf16[8,160,128]{2,1,0:T(8,128)(2,1)S(1)} %shard_map.114), channel_id=1, replica_groups={{16,20,24,28,0,4,8,12},{18,22,26,30,2,6,10,14},{17,21,25,29,1,5,9,13},{..., dimensions={0} | all-to-all | bytes 655360 | tf_op jit(solution)/shard_map/all_to_all | solution.py:450
  46.5 1.5 %collective-permute-start.4 = (f32[16,128]{1,0:T(8,128)S(1)}, f32[16,128]{1,0:T(8,128)S(1)}, u32[]{:S(2)}, u32[]{:S(2)}) collective-permute-start(f32[16,128]{1,0:T(8,128)S(1)} %convert_reduce_fusion), channel_id=1, source_target_pairs={{0,2},{2,0},{1,3},{3,1},{4,6},{6,4},{5,7},{7,5},{8,10},{10,8},{9,1... | collective-permute-start | bytes 24584 | tf_op jit(solution)/shard_map/ppermute | solution.py:555
  48.1 4.0 %shard_map.115 = (bf16[8,128,128]{2,1,0:T(8,128)(2,1)S(1)}, f32[8,128,128]{2,1,0:T(8,128)S(1)}, f32[8,128,128]{2,1,0:T(8,128)S(1)}, bf16[8,256,128]{2,1,0:T(8,128)(2,1)S(1)}, f32[16,128]{1,0:T(8,128)S(1)}) custom-call(s32[1]{0:T(128)} %bitcast.1.scalar_ref, bf16[8,384,128]{2,1,0:T(8,128)(2,1)S(1)} %maximum_select_fusion.own_ref, ...), custom_call_target="tpu_custom_call" | custom-call | flops 1677721600 | bytes 4005892 | tf_op jit(solution)/shard_map/pallas_call | solution.py:237
  52.3 0.9 %collective-permute-start.7 = (bf16[16,2048]{1,0:T(8,128)(2,1)S(1)}, bf16[16,2048]{1,0:T(8,128)(2,1)S(1)}, u32[]{:S(2)}, u32[]{:S(2)}) collective-permute-start(bf16[16,2048]{1,0:T(8,128)(2,1)S(1)} %fusion.1), channel_id=1, source_target_pairs={{0,4},{4,0},{8,12},{12,8},{16,20},{20,16},{24,28},{28,24},{1,5},{5... | collective-permute-start | bytes 196616 | tf_op jit(solution)/shard_map/ppermute | solution.py:260
  53.4 1.0 %collective-permute-done.6.taken_ref = f32[16,128]{1,0:T(8,128)S(1)} collective-permute-done((f32[16,128]{1,0:T(8,128)S(1)}, f32[16,128]{1,0:T(8,128)S(1)}, u32[]{:S(2)}, u32[]{:S(2)}) %collective-permute-start.6) | collective-permute-done | bytes 8224 | tf_op jit(solution)/shard_map/ppermute | solution.py:457
  54.4 1.0 %shard_map.116 = bf16[8,400,128]{2,1,0:T(8,128)(2,1)} custom-call(s32[1]{0:T(128)} %bitcast.turn_ref, bf16[8,128,128]{2,1,0:T(8,128)(2,1)S(1)} %get-tuple-element.42.dq_ref, f32[8,128,128]{2,1,0:T(8,128)S(1)} %get-tuple-element.43.dk_ref, f32[8,128,128]{2,1,0:T(8,128)S(1)} %get-tuple-element.44.dv_ref, ...), custom_call_target="tpu_custom_call" | custom-call | bytes 1638400 | tf_op jit(solution)/shard_map/pallas_call | solution.py:334
  55.4 4.8 %all-to-all-start.2 = ((bf16[8,400,128]{2,1,0:T(8,128)(2,1)}), bf16[8,400,128]{2,1,0:T(8,128)(2,1)S(1)}, u32[]{:S(2)}, u32[]{:S(2)}) async-start(bf16[8,400,128]{2,1,0:T(8,128)(2,1)} %shard_map.116), calls=%async_computation.2 | async-start | bytes 1638400 | tf_op jit(solution)/shard_map/all_to_all | solution.py:450
  60.2 0.6 collective-permute-start.8
  60.9 14.5 %collective-permute-done.8 = bf16[16,2048]{1,0:T(8,128)(2,1)S(1)} collective-permute-done((bf16[16,2048]{1,0:T(8,128)(2,1)S(1)}, bf16[16,2048]{1,0:T(8,128)(2,1)S(1)}, u32[]{:S(2)}, u32[]{:S(2)}) %collective-permute-start.8) | collective-permute-done | bytes 65568 | tf_op jit(solution)/shard_map/ppermute | solution.py:260
  75.4 2.9 %collective-permute-start.9 = (bf16[16,2048]{1,0:T(8,128)(2,1)S(1)}, bf16[16,2048]{1,0:T(8,128)(2,1)S(1)}, u32[]{:S(2)}, u32[]{:S(2)}) collective-permute-start(bf16[16,2048]{1,0:T(8,128)(2,1)S(1)} %add_convert_fusion), channel_id=1, source_target_pairs={{0,16},{4,20},{8,24},{12,28},{16,0},{20,4},{24,8},{28,12},{1,17},{... | collective-permute-start | bytes 196616 | tf_op jit(solution)/shard_map/ppermute | solution.py:260
  78.3 3.0 %collective-permute-done.9 = bf16[16,2048]{1,0:T(8,128)(2,1)S(1)} collective-permute-done((bf16[16,2048]{1,0:T(8,128)(2,1)S(1)}, bf16[16,2048]{1,0:T(8,128)(2,1)S(1)}, u32[]{:S(2)}, u32[]{:S(2)}) %collective-permute-start.9) | collective-permute-done | bytes 65568 | tf_op jit(solution)/shard_map/ppermute | solution.py:260
  81.4 1.1 %shard_map.117 = (bf16[128,1024]{1,0:T(8,128)(2,1)}, bf16[128,1024]{1,0:T(8,128)(2,1)}, bf16[128,1024]{1,0:T(8,128)(2,1)}, f32[16,1024]{1,0:T(8,128)}) custom-call(bf16[8,400,128]{2,1,0:T(8,128)(2,1)S(1)} %all-to-all-done.2.back_ref), custom_call_target="tpu_custom_call" | custom-call | bytes 1671168 | tf_op jit(solution)/shard_map/pallas_call | solution.py:363
  82.6 0.7 convert_add_fusion
  (34 shorter events, 1.6 us)
Async XLA Ops:
  0.6 14.0 %copy-start = (bf16[16,4096]{1,0:T(8,128)(2,1)S(1)}, bf16[16,4096]{1,0:T(8,128)(2,1)}, u32[]{:S(2)}) copy-start(bf16[16,4096]{1,0:T(8,128)(2,1)} %param.13) | copy-start | bytes 393220
  2.6 25.4 %all-to-all-start = ((bf16[8,384,128]{2,1,0:T(8,128)(2,1)}), bf16[8,384,128]{2,1,0:T(8,128)(2,1)S(1)}, u32[]{:S(2)}, u32[]{:S(2)}) async-start(bf16[8,384,128]{2,1,0:T(8,128)(2,1)} %shard_map.110), calls=%async_computation | async-start | bytes 1572864 | tf_op jit(solution)/shard_map/all_to_all | solution.py:450
  10.5 7.7 %collective-permute-start = (bf16[128,2048]{1,0:T(8,128)(2,1)}, bf16[128,2048]{1,0:T(8,128)(2,1)S(1)}, u32[]{:S(2)}, u32[]{:S(2)}) collective-permute-start(bf16[128,2048]{1,0:T(8,128)(2,1)} %param.10), channel_id=1, source_target_pairs={{0,0},{1,2},{2,1},{3,3},{4,4},{5,6},{6,5},{7,7},{8,8},{9,10},{10,9... | collective-permute-start | bytes 1572872 | tf_op jit(solution)/shard_map/ppermute | solution.py:474
  12.2 13.7 %collective-permute-start.1 = (bf16[128,2048]{1,0:T(8,128)(2,1)}, bf16[128,2048]{1,0:T(8,128)(2,1)S(1)}, u32[]{:S(2)}, u32[]{:S(2)}) collective-permute-start(bf16[128,2048]{1,0:T(8,128)(2,1)} %param.10), channel_id=1, source_target_pairs={{0,2},{1,0},{2,3},{3,1},{4,6},{5,4},{6,7},{7,5},{8,10},{9,8},{10,1... | collective-permute-start | bytes 1572872 | tf_op jit(solution)/shard_map/ppermute | solution.py:474
  28.2 2.4 %collective-permute-start.2 = (bf16[8,256,128]{2,1,0:T(8,128)(2,1)S(1)}, bf16[8,256,128]{2,1,0:T(8,128)(2,1)S(1)}, u32[]{:S(2)}, u32[]{:S(2)}) collective-permute-start(bf16[8,256,128]{2,1,0:T(8,128)(2,1)S(1)} %slice.38), channel_id=1, source_target_pairs={{0,1},{1,0},{2,3},{3,2},{4,5},{5,4},{6,7},{7,6},{8,9},{9,8},{10,11... | collective-permute-start | bytes 1572872 | tf_op jit(solution)/shard_map/ppermute | solution.py:457
  29.1 2.9 %collective-permute-start.3 = (bf16[1040,128]{1,0:T(8,128)(2,1)S(1)}, bf16[1040,128]{1,0:T(8,128)(2,1)S(1)}, u32[]{:S(2)}, u32[]{:S(2)}) collective-permute-start(bf16[1040,128]{1,0:T(8,128)(2,1)S(1)} %get-tuple-element.32), channel_id=1, source_target_pairs={{0,1},{1,0},{2,3},{3,2},{4,5},{5,4},{6,7},{7,6},{8,9},{9,8},{10,11... | collective-permute-start | bytes 798728 | tf_op jit(solution)/shard_map/ppermute | solution.py:457
  32.0 20.1 %copy-start.1 = (bf16[128,2048]{1,0:T(8,128)(2,1)S(1)}, bf16[128,2048]{1,0:T(8,128)(2,1)}, u32[]{:S(2)}) copy-start(bf16[128,2048]{1,0:T(8,128)(2,1)} %param.10) | copy-start | bytes 1572868
  46.5 5.6 %collective-permute-start.4 = (f32[16,128]{1,0:T(8,128)S(1)}, f32[16,128]{1,0:T(8,128)S(1)}, u32[]{:S(2)}, u32[]{:S(2)}) collective-permute-start(f32[16,128]{1,0:T(8,128)S(1)} %convert_reduce_fusion), channel_id=1, source_target_pairs={{0,2},{2,0},{1,3},{3,1},{4,6},{6,4},{5,7},{7,5},{8,10},{10,8},{9,1... | collective-permute-start | bytes 24584 | tf_op jit(solution)/shard_map/ppermute | solution.py:555
  52.0 2.3 %collective-permute-start.5 = (bf16[8,256,128]{2,1,0:T(8,128)(2,1)S(1)}, bf16[8,256,128]{2,1,0:T(8,128)(2,1)S(1)}, u32[]{:S(2)}, u32[]{:S(2)}) collective-permute-start(bf16[8,256,128]{2,1,0:T(8,128)(2,1)S(1)} %get-tuple-element.46), channel_id=1, source_target_pairs={{0,1},{1,0},{2,3},{3,2},{4,5},{5,4},{6,7},{7,6},{8,9},{9,8},{10,11... | collective-permute-start | bytes 1572872 | tf_op jit(solution)/shard_map/ppermute | solution.py:457
  52.3 7.9 %collective-permute-start.7 = (bf16[16,2048]{1,0:T(8,128)(2,1)S(1)}, bf16[16,2048]{1,0:T(8,128)(2,1)S(1)}, u32[]{:S(2)}, u32[]{:S(2)}) collective-permute-start(bf16[16,2048]{1,0:T(8,128)(2,1)S(1)} %fusion.1), channel_id=1, source_target_pairs={{0,4},{4,0},{8,12},{12,8},{16,20},{20,16},{24,28},{28,24},{1,5},{5... | collective-permute-start | bytes 196616 | tf_op jit(solution)/shard_map/ppermute | solution.py:260
  53.2 1.2 %collective-permute-start.6 = (f32[16,128]{1,0:T(8,128)S(1)}, f32[16,128]{1,0:T(8,128)S(1)}, u32[]{:S(2)}, u32[]{:S(2)}) collective-permute-start(f32[16,128]{1,0:T(8,128)S(1)} %get-tuple-element.47.down_ref), channel_id=1, source_target_pairs={{0,1},{1,0},{2,3},{3,2},{4,5},{5,4},{6,7},{7,6},{8,9},{9,8},{10,11... | collective-permute-start | bytes 24584 | tf_op jit(solution)/shard_map/ppermute | solution.py:457
  55.4 25.9 %all-to-all-start.2 = ((bf16[8,400,128]{2,1,0:T(8,128)(2,1)}), bf16[8,400,128]{2,1,0:T(8,128)(2,1)S(1)}, u32[]{:S(2)}, u32[]{:S(2)}) async-start(bf16[8,400,128]{2,1,0:T(8,128)(2,1)} %shard_map.116), calls=%async_computation.2 | async-start | bytes 1638400 | tf_op jit(solution)/shard_map/all_to_all | solution.py:450
  60.2 15.1 %collective-permute-start.8 = (bf16[16,2048]{1,0:T(8,128)(2,1)S(1)}, bf16[16,2048]{1,0:T(8,128)(2,1)S(1)}, u32[]{:S(2)}, u32[]{:S(2)}) collective-permute-start(bf16[16,2048]{1,0:T(8,128)(2,1)S(1)} %add_convert_fusion.1), channel_id=1, source_target_pairs={{0,8},{4,12},{8,0},{12,4},{16,24},{20,28},{24,16},{28,20},{1,9},{5... | collective-permute-start | bytes 196616 | tf_op jit(solution)/shard_map/ppermute | solution.py:260
  75.4 5.9 %collective-permute-start.9 = (bf16[16,2048]{1,0:T(8,128)(2,1)S(1)}, bf16[16,2048]{1,0:T(8,128)(2,1)S(1)}, u32[]{:S(2)}, u32[]{:S(2)}) collective-permute-start(bf16[16,2048]{1,0:T(8,128)(2,1)S(1)} %add_convert_fusion), channel_id=1, source_target_pairs={{0,16},{4,20},{8,24},{12,28},{16,0},{20,4},{24,8},{28,12},{1,17},{... | collective-permute-start | bytes 196616 | tf_op jit(solution)/shard_map/ppermute | solution.py:260
  81.3 1.3 %collective-permute-start.10 = (bf16[16,2048]{1,0:T(8,128)(2,1)S(1)}, bf16[16,2048]{1,0:T(8,128)(2,1)S(1)}, u32[]{:S(2)}, u32[]{:S(2)}) collective-permute-start(bf16[16,2048]{1,0:T(8,128)(2,1)S(1)} %convert_add_fusion.1), channel_id=1, source_target_pairs={{0,1},{1,0},{2,3},{3,2},{4,5},{5,4},{6,7},{7,6},{8,9},{9,8},{10,11... | collective-permute-start | bytes 196616 | tf_op jit(solution)/shard_map/ppermute | solution.py:260

commit v8 on v7

--- a/solution.py
+++ b/solution.py
@@ -594,7 +594,8 @@
         outs.append(down_terms.transpose(1, 0, 2).reshape(low_rank, feats))
     query_gradient, key_gradient, value_gradient, down_gradient = outs
 
-    up_sum = butterfly_sum(up_part, "seq", powers_below(seqs), seqs)
+    bits = powers_below(seqs)
+    up_sum = butterfly_sum(up_part, "seq", bits[1:2] + bits[:1] + bits[2:], seqs)
     _, up_sum = lax.optimization_barrier((back, up_sum))
     up_gradient = butterfly_sum(up_sum, "sub", powers_below(subs), subs)
     return (query_gradient, key_gradient, value_gradient, down_gradient.T, up_gradient)

time: 83.7 us -> 85.1 us (1.017)
  waiting for transfers between devices: 26.6 us -> 29.2 us
  starting transfers between devices: 23.3 us -> 22.1 us
    ppermute x4, waiting for transfers between devices: 17.6 us -> 20.1 us  [butterfly_sum(): taken = lax.ppermute(value, axis, pairs)]
    ppermute x4, starting transfers between devices: 4.52 us -> 2.47 us  [butterfly_sum(): taken = lax.ppermute(value, axis, pairs)]
  transfers between devices with their start and end apart: 13 -> 13, of which waited for: 6 -> 6; matrix products, arithmetic and copies ran while one was open for 6% -> 5% of each run, Pallas kernels for 13% -> 12%
where the time goes in v8:
time: 85.1 us; the launch traced here: 84.6 us
  waiting for transfers between devices  29.2 us (34%)
  starting transfers between devices  22.1 us (26%)
  blocking collectives  14.4 us (17%)
  Pallas kernels  12.6 us (15%)
  matrix products  3.69 us (4%)
  other arithmetic  1 us (1%)
    ppermute x4, waiting for transfers between devices, butterfly_sum(): taken = lax.ppermute(value, axis, pairs)  20.1 us
    all_to_all x1, blocking collectives, exchange(): lax.all_to_all(parts, ('seq', 'head'), 0, 0, axis_index_groups=groups, ti...  14.4 us
    all_to_all x2, starting transfers between devices, exchange(): lax.all_to_all(parts, ('seq', 'head'), 0, 0, axis_index_groups=groups, ti...  13.5 us
    pallas_call x4, Pallas kernels, call_kernel(): pl.pallas_call(body, out_shape=outs, in_specs=specs, out_specs=[pl.BlockS...  8.48 us
    ppermute x2, waiting for transfers between devices, on_device(): pieces.append(lax.ppermute(output_gradient, ('head', 'sub'), pairs))  7.71 us
    dot_general x2, matrix products, dot_nn(): return jnp.dot(left, right, preferred_element_type=jnp.float32)  3.69 us
    ppermute x2, starting transfers between devices, on_device(): pieces.append(lax.ppermute(output_gradient, ('head', 'sub'), pairs))  3.42 us
    ppermute x4, starting transfers between devices, butterfly_sum(): taken = lax.ppermute(value, axis, pairs)  2.47 us
  transfers between devices with their start and end apart: 13, of which 6 were waited for; matrix products, arithmetic and copies ran while one was open for 5% of the time, Pallas kernels for 12%

profile of v8, /device:TPU:0, one launch (start us, length us, event | category | flops | bytes accessed | tf_op | source)
XLA Modules:
  0.0 84.6 jit_solution(12430924234283121419)
XLA Ops:
  0.6 2.0 %shard_map.110 = bf16[8,384,128]{2,1,0:T(8,128)(2,1)} custom-call(bf16[128,1024]{1,0:T(8,128)(2,1)} %refs_0_.1, bf16[128,1024]{1,0:T(8,128)(2,1)} %refs_1_.1, bf16[128,1024]{1,0:T(8,128)(2,1)} %refs_2_.1), custom_call_target="tpu_custom_call" | custom-call | bytes 1572864 | tf_op jit(solution)/shard_map/pallas_call | solution.py:298
  2.6 7.9 %all-to-all-start = ((bf16[8,384,128]{2,1,0:T(8,128)(2,1)}), bf16[8,384,128]{2,1,0:T(8,128)(2,1)S(1)}, u32[]{:S(2)}, u32[]{:S(2)}) async-start(bf16[8,384,128]{2,1,0:T(8,128)(2,1)} %shard_map.110), calls=%async_computation | async-start | bytes 1572864 | tf_op jit(solution)/shard_map/all_to_all | solution.py:450
  10.5 1.7 %collective-permute-start = (bf16[128,2048]{1,0:T(8,128)(2,1)}, bf16[128,2048]{1,0:T(8,128)(2,1)S(1)}, u32[]{:S(2)}, u32[]{:S(2)}) collective-permute-start(bf16[128,2048]{1,0:T(8,128)(2,1)} %param.10), channel_id=1, source_target_pairs={{0,0},{1,2},{2,1},{3,3},{4,4},{5,6},{6,5},{7,7},{8,8},{9,10},{10,9... | collective-permute-start | bytes 1572872 | tf_op jit(solution)/shard_map/ppermute | solution.py:474
  12.2 1.7 %collective-permute-start.1 = (bf16[128,2048]{1,0:T(8,128)(2,1)}, bf16[128,2048]{1,0:T(8,128)(2,1)S(1)}, u32[]{:S(2)}, u32[]{:S(2)}) collective-permute-start(bf16[128,2048]{1,0:T(8,128)(2,1)} %param.10), channel_id=1, source_target_pairs={{0,2},{1,0},{2,3},{3,1},{4,6},{5,4},{6,7},{7,5},{8,10},{9,8},{10,1... | collective-permute-start | bytes 1572872 | tf_op jit(solution)/shard_map/ppermute | solution.py:474
  13.9 0.7 dynamic-slice_bitcast_fusion.down_t_ref
  14.7 3.5 %fusion.refs_2_ = bf16[1024,2048]{1,0:T(8,128)(2,1)S(1)} fusion(bf16[1024,2048]{1,0:T(8,128)(2,1)} %param.11, bf16[16,2048]{1,0:T(8,128)(2,1)S(1)} %constant_dynamic-slice_fusion.refs_3_, bf16[1024,16]{0,1:T(8,128)(2,1)} %param.12), kind=kOutput, calls=%fused_computation.1 | convolution fusion | flops 75497472 | bytes 8486912 | tf_op jit(solution)/shard_map/dot_general | solution.py:26
  18.2 7.7 %collective-permute-done.1.refs_1_ = bf16[128,2048]{1,0:T(8,128)(2,1)S(1)} collective-permute-done((bf16[128,2048]{1,0:T(8,128)(2,1)}, bf16[128,2048]{1,0:T(8,128)(2,1)S(1)}, u32[]{:S(2)}, u32[]{:S(2)}) %collective-permute-start.1) | collective-permute-done | bytes 524320 | tf_op jit(solution)/shard_map/ppermute | solution.py:474
  25.9 2.1 %shard_map.111 = (f32[1040,128]{1,0:T(8,128)S(1)}, bf16[1040,128]{1,0:T(8,128)(2,1)S(1)}) custom-call(s32[4]{0:T(128)S(1)} %pad_add_fusion.plan_ref, bf16[128,2048]{1,0:T(8,128)(2,1)S(1)} %collective-permute-done.refs_0_, bf16[128,2048]{1,0:T(8,128)(2,1)S(1)} %collective-permute-done.1.refs_1_, bf16[1024,2048]{1,0:T(8,128)(2,1)S(1)} %fusion.refs_2_, ...), custom_call_target="tpu_custom_call" | custom-call | bytes 1024 | tf_op jit(solution)/shard_map/pallas_call | solution.py:237
  28.2 0.8 collective-permute-start.2
  29.1 1.1 %shard_map.112 = (f32[128,1024]{1,0:T(8,128)S(1)}, f32[8,1024]{1,0:T(8,128)S(1)}, bf16[128,1024]{1,0:T(8,128)(2,1)S(1)}) custom-call(s32[1]{0:T(128)} %bitcast.1.scalar_ref, bf16[8,384,128]{2,1,0:T(8,128)(2,1)S(1)} %maximum_select_fusion.own_ref), custom_call_target="tpu_custom_call" | custom-call | flops 335544320 | bytes 1605636 | tf_op jit(solution)/shard_map/pallas_call | solution.py:237
  30.3 0.3 collective-permute-done.2.other_ref
  30.6 1.3 %shard_map.113 = (bf16[128,1024]{1,0:T(8,128)(2,1)S(1)}, f32[16,1024]{1,0:T(8,128)S(1)}, f32[8,1024]{1,0:T(8,128)S(1)}) custom-call(s32[1]{0:T(128)} %bitcast.1.scalar_ref, bf16[8,384,128]{2,1,0:T(8,128)(2,1)S(1)} %maximum_select_fusion.own_ref, bf16[8,256,128]{2,1,0:T(8,128)(2,1)S(1)} %collective-permute-done.2.other_ref, ...), custom_call_target="tpu_custom_call" | custom-call | flops 335544320 | bytes 2232324 | tf_op jit(solution)/shard_map/pallas_call | solution.py:237
  32.1 14.4 %all_to_all.15 = bf16[8,160,128]{2,1,0:T(8,128)(2,1)S(1)} all-to-all(bf16[8,160,128]{2,1,0:T(8,128)(2,1)S(1)} %shard_map.114), channel_id=1, replica_groups={{16,20,24,28,0,4,8,12},{18,22,26,30,2,6,10,14},{17,21,25,29,1,5,9,13},{..., dimensions={0} | all-to-all | bytes 655360 | tf_op jit(solution)/shard_map/all_to_all | solution.py:450
  46.5 1.5 %collective-permute-start.4 = (f32[16,128]{1,0:T(8,128)S(1)}, f32[16,128]{1,0:T(8,128)S(1)}, u32[]{:S(2)}, u32[]{:S(2)}) collective-permute-start(f32[16,128]{1,0:T(8,128)S(1)} %convert_reduce_fusion), channel_id=1, source_target_pairs={{0,2},{2,0},{1,3},{3,1},{4,6},{6,4},{5,7},{7,5},{8,10},{10,8},{9,1... | collective-permute-start | bytes 24584 | tf_op jit(solution)/shard_map/ppermute | solution.py:555
  48.1 4.0 %shard_map.115 = (bf16[8,128,128]{2,1,0:T(8,128)(2,1)S(1)}, f32[8,128,128]{2,1,0:T(8,128)S(1)}, f32[8,128,128]{2,1,0:T(8,128)S(1)}, bf16[8,256,128]{2,1,0:T(8,128)(2,1)S(1)}, f32[16,128]{1,0:T(8,128)S(1)}) custom-call(s32[1]{0:T(128)} %bitcast.1.scalar_ref, bf16[8,384,128]{2,1,0:T(8,128)(2,1)S(1)} %maximum_select_fusion.own_ref, ...), custom_call_target="tpu_custom_call" | custom-call | flops 1677721600 | bytes 4005892 | tf_op jit(solution)/shard_map/pallas_call | solution.py:237
  52.3 0.8 collective-permute-start.7
  53.3 1.0 %collective-permute-done.6.taken_ref = f32[16,128]{1,0:T(8,128)S(1)} collective-permute-done((f32[16,128]{1,0:T(8,128)S(1)}, f32[16,128]{1,0:T(8,128)S(1)}, u32[]{:S(2)}, u32[]{:S(2)}) %collective-permute-start.6) | collective-permute-done | bytes 8224 | tf_op jit(solution)/shard_map/ppermute | solution.py:457
  54.3 1.0 %shard_map.116 = bf16[8,400,128]{2,1,0:T(8,128)(2,1)} custom-call(s32[1]{0:T(128)} %bitcast.turn_ref, bf16[8,128,128]{2,1,0:T(8,128)(2,1)S(1)} %get-tuple-element.42.dq_ref, f32[8,128,128]{2,1,0:T(8,128)S(1)} %get-tuple-element.43.dk_ref, f32[8,128,128]{2,1,0:T(8,128)S(1)} %get-tuple-element.44.dv_ref, ...), custom_call_target="tpu_custom_call" | custom-call | bytes 1638400 | tf_op jit(solution)/shard_map/pallas_call | solution.py:334
  55.3 5.7 %all-to-all-start.2 = ((bf16[8,400,128]{2,1,0:T(8,128)(2,1)}), bf16[8,400,128]{2,1,0:T(8,128)(2,1)S(1)}, u32[]{:S(2)}, u32[]{:S(2)}) async-start(bf16[8,400,128]{2,1,0:T(8,128)(2,1)} %shard_map.116), calls=%async_computation.2 | async-start | bytes 1638400 | tf_op jit(solution)/shard_map/all_to_all | solution.py:450
  61.0 1.5 %collective-permute-start.8 = (bf16[16,2048]{1,0:T(8,128)(2,1)S(1)}, bf16[16,2048]{1,0:T(8,128)(2,1)S(1)}, u32[]{:S(2)}, u32[]{:S(2)}) collective-permute-start(bf16[16,2048]{1,0:T(8,128)(2,1)S(1)} %add_convert_fusion.1), channel_id=1, source_target_pairs={{0,4},{4,0},{8,12},{12,8},{16,20},{20,16},{24,28},{28,24},{1,5},{5... | collective-permute-start | bytes 196616 | tf_op jit(solution)/shard_map/ppermute | solution.py:260
  62.5 8.7 %collective-permute-done.8 = bf16[16,2048]{1,0:T(8,128)(2,1)S(1)} collective-permute-done((bf16[16,2048]{1,0:T(8,128)(2,1)S(1)}, bf16[16,2048]{1,0:T(8,128)(2,1)S(1)}, u32[]{:S(2)}, u32[]{:S(2)}) %collective-permute-start.8) | collective-permute-done | bytes 65568 | tf_op jit(solution)/shard_map/ppermute | solution.py:260
  71.4 11.3 %collective-permute-done.9 = bf16[16,2048]{1,0:T(8,128)(2,1)S(1)} collective-permute-done((bf16[16,2048]{1,0:T(8,128)(2,1)S(1)}, bf16[16,2048]{1,0:T(8,128)(2,1)S(1)}, u32[]{:S(2)}, u32[]{:S(2)}) %collective-permute-start.9) | collective-permute-done | bytes 65568 | tf_op jit(solution)/shard_map/ppermute | solution.py:260
  82.7 1.1 %shard_map.117 = (bf16[128,1024]{1,0:T(8,128)(2,1)}, bf16[128,1024]{1,0:T(8,128)(2,1)}, bf16[128,1024]{1,0:T(8,128)(2,1)}, f32[16,1024]{1,0:T(8,128)}) custom-call(bf16[8,400,128]{2,1,0:T(8,128)(2,1)S(1)} %all-to-all-done.2.back_ref), custom_call_target="tpu_custom_call" | custom-call | bytes 1671168 | tf_op jit(solution)/shard_map/pallas_call | solution.py:363
  84.0 0.7 convert_add_fusion
  (34 shorter events, 1.4 us)
Async XLA Ops:
  0.6 14.0 %copy-start = (bf16[16,4096]{1,0:T(8,128)(2,1)S(1)}, bf16[16,4096]{1,0:T(8,128)(2,1)}, u32[]{:S(2)}) copy-start(bf16[16,4096]{1,0:T(8,128)(2,1)} %param.13) | copy-start | bytes 393220
  2.6 25.4 %all-to-all-start = ((bf16[8,384,128]{2,1,0:T(8,128)(2,1)}), bf16[8,384,128]{2,1,0:T(8,128)(2,1)S(1)}, u32[]{:S(2)}, u32[]{:S(2)}) async-start(bf16[8,384,128]{2,1,0:T(8,128)(2,1)} %shard_map.110), calls=%async_computation | async-start | bytes 1572864 | tf_op jit(solution)/shard_map/all_to_all | solution.py:450
  10.5 7.7 %collective-permute-start = (bf16[128,2048]{1,0:T(8,128)(2,1)}, bf16[128,2048]{1,0:T(8,128)(2,1)S(1)}, u32[]{:S(2)}, u32[]{:S(2)}) collective-permute-start(bf16[128,2048]{1,0:T(8,128)(2,1)} %param.10), channel_id=1, source_target_pairs={{0,0},{1,2},{2,1},{3,3},{4,4},{5,6},{6,5},{7,7},{8,8},{9,10},{10,9... | collective-permute-start | bytes 1572872 | tf_op jit(solution)/shard_map/ppermute | solution.py:474
  12.2 13.7 %collective-permute-start.1 = (bf16[128,2048]{1,0:T(8,128)(2,1)}, bf16[128,2048]{1,0:T(8,128)(2,1)S(1)}, u32[]{:S(2)}, u32[]{:S(2)}) collective-permute-start(bf16[128,2048]{1,0:T(8,128)(2,1)} %param.10), channel_id=1, source_target_pairs={{0,2},{1,0},{2,3},{3,1},{4,6},{5,4},{6,7},{7,5},{8,10},{9,8},{10,1... | collective-permute-start | bytes 1572872 | tf_op jit(solution)/shard_map/ppermute | solution.py:474
  28.2 2.4 %collective-permute-start.2 = (bf16[8,256,128]{2,1,0:T(8,128)(2,1)S(1)}, bf16[8,256,128]{2,1,0:T(8,128)(2,1)S(1)}, u32[]{:S(2)}, u32[]{:S(2)}) collective-permute-start(bf16[8,256,128]{2,1,0:T(8,128)(2,1)S(1)} %slice.38), channel_id=1, source_target_pairs={{0,1},{1,0},{2,3},{3,2},{4,5},{5,4},{6,7},{7,6},{8,9},{9,8},{10,11... | collective-permute-start | bytes 1572872 | tf_op jit(solution)/shard_map/ppermute | solution.py:457
  29.1 2.9 %collective-permute-start.3 = (bf16[1040,128]{1,0:T(8,128)(2,1)S(1)}, bf16[1040,128]{1,0:T(8,128)(2,1)S(1)}, u32[]{:S(2)}, u32[]{:S(2)}) collective-permute-start(bf16[1040,128]{1,0:T(8,128)(2,1)S(1)} %get-tuple-element.32), channel_id=1, source_target_pairs={{0,1},{1,0},{2,3},{3,2},{4,5},{5,4},{6,7},{7,6},{8,9},{9,8},{10,11... | collective-permute-start | bytes 798728 | tf_op jit(solution)/shard_map/ppermute | solution.py:457
  32.0 20.1 %copy-start.1 = (bf16[128,2048]{1,0:T(8,128)(2,1)S(1)}, bf16[128,2048]{1,0:T(8,128)(2,1)}, u32[]{:S(2)}) copy-start(bf16[128,2048]{1,0:T(8,128)(2,1)} %param.10) | copy-start | bytes 1572868
  46.5 5.6 %collective-permute-start.4 = (f32[16,128]{1,0:T(8,128)S(1)}, f32[16,128]{1,0:T(8,128)S(1)}, u32[]{:S(2)}, u32[]{:S(2)}) collective-permute-start(f32[16,128]{1,0:T(8,128)S(1)} %convert_reduce_fusion), channel_id=1, source_target_pairs={{0,2},{2,0},{1,3},{3,1},{4,6},{6,4},{5,7},{7,5},{8,10},{10,8},{9,1... | collective-permute-start | bytes 24584 | tf_op jit(solution)/shard_map/ppermute | solution.py:555
  52.0 2.2 %collective-permute-start.5 = (bf16[8,256,128]{2,1,0:T(8,128)(2,1)S(1)}, bf16[8,256,128]{2,1,0:T(8,128)(2,1)S(1)}, u32[]{:S(2)}, u32[]{:S(2)}) collective-permute-start(bf16[8,256,128]{2,1,0:T(8,128)(2,1)S(1)} %get-tuple-element.46), channel_id=1, source_target_pairs={{0,1},{1,0},{2,3},{3,2},{4,5},{5,4},{6,7},{7,6},{8,9},{9,8},{10,11... | collective-permute-start | bytes 1572872 | tf_op jit(solution)/shard_map/ppermute | solution.py:457
  52.3 8.6 %collective-permute-start.7 = (bf16[16,2048]{1,0:T(8,128)(2,1)S(1)}, bf16[16,2048]{1,0:T(8,128)(2,1)S(1)}, u32[]{:S(2)}, u32[]{:S(2)}) collective-permute-start(bf16[16,2048]{1,0:T(8,128)(2,1)S(1)} %fusion.1), channel_id=1, source_target_pairs={{0,8},{4,12},{8,0},{12,4},{16,24},{20,28},{24,16},{28,20},{1,9},{5... | collective-permute-start | bytes 196616 | tf_op jit(solution)/shard_map/ppermute | solution.py:260
  53.1 1.2 %collective-permute-start.6 = (f32[16,128]{1,0:T(8,128)S(1)}, f32[16,128]{1,0:T(8,128)S(1)}, u32[]{:S(2)}, u32[]{:S(2)}) collective-permute-start(f32[16,128]{1,0:T(8,128)S(1)} %get-tuple-element.47.down_ref), channel_id=1, source_target_pairs={{0,1},{1,0},{2,3},{3,2},{4,5},{5,4},{6,7},{7,6},{8,9},{9,8},{10,11... | collective-permute-start | bytes 24584 | tf_op jit(solution)/shard_map/ppermute | solution.py:457
  55.3 27.4 %all-to-all-start.2 = ((bf16[8,400,128]{2,1,0:T(8,128)(2,1)}), bf16[8,400,128]{2,1,0:T(8,128)(2,1)S(1)}, u32[]{:S(2)}, u32[]{:S(2)}) async-start(bf16[8,400,128]{2,1,0:T(8,128)(2,1)} %shard_map.116), calls=%async_computation.2 | async-start | bytes 1638400 | tf_op jit(solution)/shard_map/all_to_all | solution.py:450
  61.0 10.3 %collective-permute-start.8 = (bf16[16,2048]{1,0:T(8,128)(2,1)S(1)}, bf16[16,2048]{1,0:T(8,128)(2,1)S(1)}, u32[]{:S(2)}, u32[]{:S(2)}) collective-permute-start(bf16[16,2048]{1,0:T(8,128)(2,1)S(1)} %add_convert_fusion.1), channel_id=1, source_target_pairs={{0,4},{4,0},{8,12},{12,8},{16,20},{20,16},{24,28},{28,24},{1,5},{5... | collective-permute-start | bytes 196616 | tf_op jit(solution)/shard_map/ppermute | solution.py:260
  71.3 11.3 %collective-permute-start.9 = (bf16[16,2048]{1,0:T(8,128)(2,1)S(1)}, bf16[16,2048]{1,0:T(8,128)(2,1)S(1)}, u32[]{:S(2)}, u32[]{:S(2)}) collective-permute-start(bf16[16,2048]{1,0:T(8,128)(2,1)S(1)} %add_convert_fusion), channel_id=1, source_target_pairs={{0,16},{4,20},{8,24},{12,28},{16,0},{20,4},{24,8},{28,12},{1,17},{... | collective-permute-start | bytes 196616 | tf_op jit(solution)/shard_map/ppermute | solution.py:260
  82.6 1.3 %collective-permute-start.10 = (bf16[16,2048]{1,0:T(8,128)(2,1)S(1)}, bf16[16,2048]{1,0:T(8,128)(2,1)S(1)}, u32[]{:S(2)}, u32[]{:S(2)}) collective-permute-start(bf16[16,2048]{1,0:T(8,128)(2,1)S(1)} %convert_add_fusion.1), channel_id=1, source_target_pairs={{0,1},{1,0},{2,3},{3,2},{4,5},{5,4},{6,7},{7,6},{8,9},{9,8},{10,11... | collective-permute-start | bytes 196616 | tf_op jit(solution)/shard_map/ppermute | solution.py:260
